TPU v7x, 32 devices: a whole 2x2x4 slice. The times are simulated.
32 devices in a mesh: dp: 2 (over core), ctx: 4 (over z), head: 4 (over y, x).
Axes of the slice: x: 2, y: 2, z: 4, core: 2. Of those that a mesh axis runs over, the one named last changes fastest.
Arguments:
- queries: bfloat16 [2, 1024, 2048], P('dp', 'ctx', 'head'), may hold values from -6 to 6
- keys: bfloat16 [2, 1024, 2048], P('dp', 'ctx', 'head'), may hold values from -6 to 6
- values: bfloat16 [2, 1024, 2048], P('dp', 'ctx', 'head'), may hold values from -32 to 32
- spikes: int32 [2, 1024, 2048], P('dp', 'ctx', 'head'), may hold values 0 or 1
- gain: float32 [2048], P('head'), may hold values from 0.25 to 1.75
- upstream: bfloat16 [2, 1024, 2048], P('dp', 'ctx', 'head'), may hold values from -16 to 16
Outputs:
- grad_queries: bfloat16 [2, 1024, 2048], P('dp', 'ctx', 'head')
- grad_keys: bfloat16 [2, 1024, 2048], P('dp', 'ctx', 'head')
- grad_values: bfloat16 [2, 1024, 2048], P('dp', 'ctx', 'head')
- grad_gain: float32 [2048], P('head')
All inputs are finite; a program needn't handle non-finite values. No bound on the sum of `spikes` on one device may be relied on, other than what follows from the above.
Results may differ from a plain program's by a relative error of at most 0.0058.
Values sent between devices are 32-bit elements; how exact they have to be, the bound alone decides.
No kernel may reach another device: no remote copies, remote signals or barrier semaphores. Data moves between devices by JAX's collectives and lax.ppermute only.
A program may use at most 64 MiB of HBM per device.

v0:
```python
import math

import jax
import jax.numpy as jnp
from jax import lax
from jax.sharding import PartitionSpec as P

DH = 128
HEADS = 16


EPS = 1e-06


def carried_in(array, axis, combine, identity, reverse):
    devices, position = (lax.axis_size(axis), lax.axis_index(axis))
    everything = lax.all_gather(array, axis)
    start = jnp.broadcast_to(jnp.asarray(identity, array.dtype), array.shape)

    def hop(k, before):
        at = devices - 1 - k if reverse else k
        reached = at > position if reverse else at < position
        new = combine(before, everything[at])
        return jnp.where(reached, new, before)

    return lax.fori_loop(0, devices, hop, start)


def add_states(earlier, later):
    return earlier + later


def head_major(array, tok_rows, head_count):
    return jnp.transpose(array[0].reshape(tok_rows, head_count, DH), (1, 0, 2))


def token_major(array, tok_rows, width_dev):
    return jnp.transpose(array.astype(jnp.bfloat16), (1, 0, 2)).reshape(1, tok_rows, width_dev)


def per_device(queries, keys, values, spikes, gain, upstream):
    tok_rows = queries.shape[1]
    width_dev = queries.shape[2]
    head_count = width_dev // DH
    width = HEADS * DH
    spike_mask = head_major(spikes, tok_rows, head_count).astype(jnp.bfloat16)
    query_heads = head_major(queries, tok_rows, head_count)
    spiked = head_major(keys, tok_rows, head_count) * spike_mask
    value_heads = head_major(values, tok_rows, head_count)
    upper_heads = head_major(upstream, tok_rows, head_count).astype(jnp.float32)
    gain_heads = gain.reshape(head_count, 1, DH)
    causal = lax.broadcasted_iota(jnp.int32, (tok_rows, tok_rows), 0) >= lax.broadcasted_iota(
        jnp.int32, (tok_rows, tok_rows), 1
    )
    local_state = jnp.einsum(
        "hsd,hse->hde", spiked, value_heads, preferred_element_type=jnp.float32
    )
    zero_state = jnp.zeros_like(local_state)
    prior_state = carried_in(local_state, "ctx", add_states, zero_state, False).astype(jnp.bfloat16)
    scores = jnp.einsum("htd,hsd->hts", query_heads, spiked, preferred_element_type=jnp.float32)
    scores = jnp.where(causal, scores, 0.0).astype(jnp.bfloat16)
    attended = jnp.einsum(
        "htd,hde->hte", query_heads, prior_state, preferred_element_type=jnp.float32
    )
    attended = attended + jnp.einsum(
        "hts,hse->hte", scores, value_heads, preferred_element_type=jnp.float32
    )
    scaled = upper_heads * gain_heads
    squares = lax.psum(jnp.sum(attended * attended, axis=(0, 2)), "head")
    inv_rms = lax.rsqrt(squares / width + EPS)[None, :, None]
    normed = attended * inv_rms
    cross_sum = lax.psum(jnp.sum(scaled * normed, axis=(0, 2)), "head")
    grad_attended = inv_rms * (scaled - normed * (cross_sum[None, :, None] / width))
    grad_attended = grad_attended.astype(jnp.bfloat16)
    gain_part = jnp.sum(upper_heads * normed, axis=1).reshape(width_dev)
    total_tokens = tok_rows * lax.axis_size("ctx") * lax.axis_size("dp")
    grad_gain = lax.psum(gain_part, ("dp", "ctx")) / math.sqrt(total_tokens)
    local_grad = jnp.einsum(
        "htd,hte->hde", query_heads, grad_attended, preferred_element_type=jnp.float32
    )
    later_state = carried_in(local_grad, "ctx", add_states, zero_state, True)
    later_state = later_state.astype(jnp.bfloat16)
    pair_scores = jnp.einsum(
        "hte,hse->hts", grad_attended, value_heads, preferred_element_type=jnp.float32
    )
    pair_scores = jnp.where(causal, pair_scores, 0.0).astype(jnp.bfloat16)
    grad_query = jnp.einsum(
        "hte,hde->htd", grad_attended, prior_state, preferred_element_type=jnp.float32
    )
    grad_query = grad_query + jnp.einsum(
        "hts,hsd->htd", pair_scores, spiked, preferred_element_type=jnp.float32
    )
    grad_key = jnp.einsum(
        "hts,htd->hsd", pair_scores, query_heads, preferred_element_type=jnp.float32
    )
    grad_key = (
        grad_key
        + jnp.einsum("hse,hde->hsd", value_heads, later_state, preferred_element_type=jnp.float32)
    ) * spike_mask
    grad_value = jnp.einsum(
        "hts,hte->hse", scores, grad_attended, preferred_element_type=jnp.float32
    )
    grad_value = grad_value + jnp.einsum(
        "hsd,hde->hse", spiked, later_state, preferred_element_type=jnp.float32
    )
    return (
        token_major(grad_query, tok_rows, width_dev),
        token_major(grad_key, tok_rows, width_dev),
        token_major(grad_value, tok_rows, width_dev),
        grad_gain,
    )


def solution(mesh):
    return jax.shard_map(
        per_device,
        mesh=mesh,
        in_specs=(
            P("dp", "ctx", "head"),
            P("dp", "ctx", "head"),
            P("dp", "ctx", "head"),
            P("dp", "ctx", "head"),
            P("head"),
            P("dp", "ctx", "head"),
        ),
        out_specs=(
            P("dp", "ctx", "head"),
            P("dp", "ctx", "head"),
            P("dp", "ctx", "head"),
            P("head"),
        ),
        check_vma=False,
    )
```

profile of v0, /device:TPU:0, one launch (start us, length us, event | category | flops | bytes accessed | tf_op | source)
XLA Modules:
  0.0 107.1 jit_solution(8246321347177595412)
XLA Ops:
  7.2 1.1 reshape_squeeze.4
  8.3 1.0 convert_multiply_fusion
  9.4 1.0 fusion.17
  10.4 0.9 copy-done.6
  11.4 0.9 copy-done.5
  12.7 1.1 %fusion.13 = f32[4,256,128]{1,2,0:T(8,128)} fusion(bf16[4,256,256]{1,2,0:T(8,128)(2,1)S(1)} %fusion.2, bf16[256,4,128]{2,1,0:T(4,128)(2,1)S(1)} %reshape_squeeze.4), kind=kOutput, calls=%fused_computation.27 | convolution fusion | flops 67108864 | bytes 1310720 | tf_op jit(solution)/shard_map/hts,hse->hte/dot_general | solution.py:65
  13.8 27.3 %all-gather.5.cloned.1.call-done = f32[16,128,128]{2,1,0:T(8,128)} async-done(((f32[4,128,128]{2,1,0:T(8,128)}), f32[16,128,128]{2,1,0:T(8,128)}) %all-gather.5.cloned.1.call-update) | async-done | bytes 1048592 | tf_op jit(solution)/shard_map/all_gather | solution.py:17
  41.2 4.2 %while.30 = (s32[]{:T(128)}, f32[4,128,128]{2,1,0:T(8,128)S(1)}, s32[]{:T(128)}, f32[4,4,128,128]{3,2,1,0:T(8,128)}, s32[]{:T(128)}, /*index=5*/s32[]{:T(128)}) while((s32[]{:T(128)}, f32[4,128,128]{2,1,0:T(8,128)S(1)}, s32[]{:T(128)}, f32[4,4,128,128]{3,2,1,0:T(8,128)}, s32[]{:T(128)}, /*index=5*/s32[]{:T(128)}) %tuple.87), condition=%wide.region_1.2_spmd.clone, body=%wide.region_0.1_spmd.clone.sunk | while | flops 196612 | bytes 786533 | solution.py:26
  41.2 1.0 add_select_fusion.4
  42.2 1.0 add_select_fusion.4
  43.3 1.0 add_select_fusion.4
  44.3 1.0 add_select_fusion.4
  45.4 1.3 %multiply_reduce_fusion.2 = (f32[256]{0:T(256)S(1)}, f32[4,256,128]{1,2,0:T(8,128)S(1)}) fusion(f32[4,256,128]{1,2,0:T(8,128)} %fusion.13, bf16[256,4,128]{2,1,0:T(4,128)(2,1)S(1)} %reshape_squeeze.10, f32[4,128,128]{2,1,0:T(8,128)S(1)} %get-tuple-element.193), kind=kOutput, calls=%fused_computation.22 | convolution fusion | flops 34012928 | bytes 1573888 | tf_op jit(solution)/shard_map/htd,hde->hte/dot_general | solution.py:62
  46.8 9.9 %psum.21 = f32[256]{0:T(256)S(1)} all-reduce(f32[256]{0:T(256)S(1)} %get-tuple-element.255), channel_id=1, replica_groups=mesh['dp'=2,'ctx'=4,'head'=4] {'head'}, use_global_device_ids=true, to_apply=%region_3.4 | all-reduce | flops 256 | bytes 2048 | tf_op jit(solution)/shard_map/psum | solution.py:69
  56.6 0.7 copy-done.7
  57.6 7.9 %psum.22 = f32[256]{0:T(256)S(1)} all-reduce(f32[256]{0:T(256)S(1)} %get-tuple-element.238), channel_id=1, replica_groups=mesh['dp'=2,'ctx'=4,'head'=4] {'head'}, use_global_device_ids=true, to_apply=%region_5.6 | all-reduce | flops 256 | bytes 2048 | tf_op jit(solution)/shard_map/psum | solution.py:72
  65.9 0.8 copy.47
  67.6 0.5 copy-done.3
  68.3 0.8 copy.51
  69.2 15.7 %psum.23 = f32[512]{0:T(512)S(1)} all-reduce(f32[512]{0:T(512)S(1)} %bitcast.100), channel_id=1, replica_groups=mesh['dp'=2,'ctx'=4,'head'=4] {'dp','ctx'}, use_global_device_ids=true, to_apply=%region_9.10 | all-reduce | flops 512 | bytes 4096 | tf_op jit(solution)/shard_map/psum | solution.py:77
  84.9 0.6 broadcast_multiply_fusion
  85.4 0.3 fusion.40
  85.8 0.7 copy-done.4
  86.5 0.3 convolution_bitcast_fusion.2
  86.8 7.0 %all-gather.7.cloned.1.call-done = f32[16,128,128]{2,1,0:T(8,128)} async-done(((f32[4,128,128]{2,1,0:T(8,128)}), f32[16,128,128]{2,1,0:T(8,128)}) %all-gather.7.cloned.1.call-update) | async-done | bytes 1048592 | tf_op jit(solution)/shard_map/all_gather | solution.py:17
  93.8 4.2 %while.31 = (s32[]{:T(128)}, f32[4,128,128]{2,1,0:T(8,128)S(1)}, s32[]{:T(128)}, f32[4,4,128,128]{3,2,1,0:T(8,128)}, s32[]{:T(128)}, /*index=5*/s32[]{:T(128)}, s32[]{:T(128)}, s32[]{:T(128)}) while((s32[]{:T(128)}, f32[4,128,128]{2,1,0:T(8,128)S(1)}, s32[]{:T(128)}, f32[4,4,128,128]{3,2,1,0:T(8,128)}, s32[]{:T(128)}, ...), condition=%wide.region_7.8_spmd.clone, body=%wide.region_6.7_spmd.clone.sunk | while | flops 196616 | bytes 786595 | solution.py:26
  93.8 1.0 add_select_fusion.5
  94.9 1.0 add_select_fusion.5
  95.9 1.0 add_select_fusion.5
  97.0 1.0 add_select_fusion.5
  98.3 0.8 copy.53
  99.4 0.8 copy.52
  (34 shorter events, 2.8 us)
Async XLA Ops:
  7.2 1.1 %copy-start = (s32[1,256,512]{2,1,0:T(8,128)S(1)}, s32[1,256,512]{2,1,0:T(8,128)}, u32[]{:S(2)}) copy-start(s32[1,256,512]{2,1,0:T(8,128)} %param.13) | copy-start | bytes 1572868
  7.2 34.0 %all-gather.5.cloned.1.call-start = ((), (), s32[]{:S(2)}) async-start(), calls=%async_computation | async-start | bytes 1310720 | tf_op jit(solution)/shard_map/all_gather | solution.py:17
  10.3 0.9 copy-start.6
  10.4 83.4 %all-gather.7.cloned.1.call-start = ((), (), s32[]{:S(2)}) async-start(), calls=%async_computation.1 | async-start | bytes 1310720 | tf_op jit(solution)/shard_map/all_gather | solution.py:17
  11.3 0.9 copy-start.5
  12.7 1.1 %copy-start.1 = (bf16[4,256,256]{1,2,0:T(8,128)(2,1)}, bf16[4,256,256]{1,2,0:T(8,128)(2,1)S(1)}, u32[]{:S(2)}) copy-start(bf16[4,256,256]{1,2,0:T(8,128)(2,1)S(1)} %fusion.2) | copy-start | bytes 1572868
  56.6 0.7 copy-start.7
  67.3 0.8 copy-start.3
  68.3 17.1 %copy-start.2 = (bf16[4,256,256]{1,2,0:T(8,128)(2,1)S(1)}, bf16[4,256,256]{1,2,0:T(8,128)(2,1)}, u32[]{:S(2)}) copy-start(bf16[4,256,256]{1,2,0:T(8,128)(2,1)} %copy-done.1) | copy-start | bytes 1572868
  85.4 1.0 copy-start.4
Sparse Core Ops, SparseCore 0:
  10.5 30.6 all-gather.4
  66.9 26.8 all-gather.6
where the time goes:
time: 108 us; the launch traced here: 107 us
  waiting for transfers between devices  34.4 us (32%)
  blocking collectives  33.5 us (31%)
  between operations  14.2 us (13%)
  other arithmetic  10.4 us (10%)
  local copies, waits for them, and re-layouts  8.59 us (8%)
  matrix products  5.79 us (5%)
    all_gather x2, waiting for transfers between devices, carried_in(): everything = lax.all_gather(array, axis)  34.3 us
    psum x1, blocking collectives, per_device(): grad_gain = lax.psum(gain_part, ('dp', 'ctx')) / math.sqrt(total_tokens)  15.7 us
    psum x1, blocking collectives, per_device(): squares = lax.psum(jnp.sum(attended * attended, axis=(0, 2)), 'head')  9.88 us
    select_n x8, other arithmetic, hop(): return jnp.where(reached, new, before)  8.32 us
    psum x1, blocking collectives, per_device(): cross_sum = lax.psum(jnp.sum(scaled * normed, axis=(0, 2)), 'head')  7.94 us
    unnamed x19, local copies, waits for them, and re-layouts  6.23 us
  transfers between devices with their start and end apart: 2, of which 2 were waited for; matrix products, arithmetic and copies ran while one was open for 4% of the time, Pallas kernels for 0%

commit v1 on v0

v1 whole, which is shorter than its diff:
```python
import functools
import math

import jax
import jax.numpy as jnp
from jax import lax
from jax.experimental import pallas as pl
from jax.experimental.pallas import tpu as pltpu
from jax.sharding import PartitionSpec as P

DH = 128
HEADS = 16
EPS = 1e-06

F32 = jnp.float32
BF16 = jnp.bfloat16
VMEM = pl.BlockSpec(memory_space=pltpu.VMEM)


def dot(a, b, ca, cb):
    return lax.dot_general(a, b, (((ca,), (cb,)), ((), ())), preferred_element_type=F32)


def cols(h):
    return slice(h * DH, (h + 1) * DH)


def call(body, outs, *args, flops=0, moved=0):
    return pl.pallas_call(
        body,
        out_shape=outs,
        in_specs=[VMEM] * len(args),
        out_specs=[VMEM] * len(outs),
        cost_estimate=pl.CostEstimate(flops=flops, bytes_accessed=moved, transcendentals=0),
        compiler_params=pltpu.CompilerParams(vmem_limit_bytes=32 * 2**20),
    )(*args)


def causal_mask(tok):
    rows = lax.broadcasted_iota(jnp.int32, (tok, tok), 0)
    return rows >= lax.broadcasted_iota(jnp.int32, (tok, tok), 1)


def state_kernel(keys, spikes, values, spiked, *states):
    per = states[0].shape[0]
    for h in range(per * len(states)):
        block = keys[0, :, cols(h)] * spikes[0, :, cols(h)].astype(F32).astype(BF16)
        spiked[:, cols(h)] = block
        states[h // per][h % per] = dot(block, values[0, :, cols(h)], 0, 0)


def scores_kernel(queries, spiked, values, scores, intra):
    heads, tok, _ = scores.shape
    causal = causal_mask(tok)
    for h in range(heads):
        raw = dot(queries[0, :, cols(h)], spiked[:, cols(h)], 1, 1)
        block = jnp.where(causal, raw, 0.0).astype(BF16)
        scores[h] = block
        intra[:, cols(h)] = dot(block, values[0, :, cols(h)], 1, 0)


def attend_kernel(queries, intra, upstream, gain, sum_a, sum_b, attended, prior, sums):
    heads = prior.shape[0]
    per = heads // 2
    tok = intra.shape[0]
    square = jnp.zeros((tok, DH), F32)
    cross = jnp.zeros((tok, DH), F32)
    for h in range(heads):
        state = (sum_a if h < per else sum_b)[h % per].astype(BF16)
        prior[h] = state
        block = dot(queries[0, :, cols(h)], state, 1, 0) + intra[:, cols(h)]
        attended[:, cols(h)] = block
        scaled = upstream[0, :, cols(h)].astype(F32) * gain[:, cols(h)]
        square += block * block
        cross += scaled * block
    sums[0:1, :] = jnp.sum(square.T, axis=0, keepdims=True)
    sums[1:2, :] = jnp.sum(cross.T, axis=0, keepdims=True)


def grad_kernel(width, queries, attended, upstream, gain, sums, grad, gain_part, *locals_):
    tok = attended.shape[0]
    per = locals_[0].shape[0]
    inv = lax.rsqrt(sums[0:1, :] / width + EPS)
    factor = inv * inv * inv * (sums[1:2, :] / width)
    inv = jnp.broadcast_to(inv, (DH, tok)).T
    factor = jnp.broadcast_to(factor, (DH, tok)).T
    for h in range(per * len(locals_)):
        block = attended[:, cols(h)]
        upper = upstream[0, :, cols(h)].astype(F32)
        scaled = upper * gain[:, cols(h)]
        result = (inv * scaled - block * factor).astype(BF16)
        grad[:, cols(h)] = result
        gain_part[:, cols(h)] = jnp.sum(upper * block * inv, axis=0, keepdims=True)
        locals_[h // per][h % per] = dot(queries[0, :, cols(h)], result, 0, 0)


def pairs_kernel(queries, spiked, values, grad, prior, scores, grad_query, key_part, value_part):
    heads, tok, _ = scores.shape
    causal = causal_mask(tok)
    for h in range(heads):
        result = grad[:, cols(h)]
        raw = dot(result, values[0, :, cols(h)], 1, 1)
        pairs = jnp.where(causal, raw, 0.0).astype(BF16)
        query_part = dot(result, prior[h], 1, 1) + dot(pairs, spiked[:, cols(h)], 1, 0)
        grad_query[0, :, cols(h)] = query_part.astype(BF16)
        key_part[:, cols(h)] = dot(pairs, queries[0, :, cols(h)], 0, 0)
        value_part[:, cols(h)] = dot(scores[h], result, 0, 0)


def final_kernel(values, spiked, spikes, key_part, value_part, sum_a, sum_b, grad_key, grad_value):
    per = sum_a.shape[0]
    for h in range(2 * per):
        later = (sum_a if h < per else sum_b)[h % per].astype(BF16)
        inner = key_part[:, cols(h)] + dot(values[0, :, cols(h)], later, 1, 1)
        mask = spikes[0, :, cols(h)].astype(F32)
        grad_key[0, :, cols(h)] = (inner * mask).astype(BF16)
        block = value_part[:, cols(h)] + dot(spiked[:, cols(h)], later, 1, 0)
        grad_value[0, :, cols(h)] = block.astype(BF16)


def swap(array, axis, stride):
    size = lax.axis_size(axis)
    return lax.ppermute(array, axis, [(i, i ^ stride) for i in range(size)])


def strides(axis):
    size = lax.axis_size(axis)
    assert size & (size - 1) == 0
    return [1 << k for k in range(size.bit_length() - 1)]


def scan_pair(up, down, axis, reverse):
    at = lax.axis_index(axis)
    order = strides(axis)
    total = up
    up_sum = jnp.zeros_like(up)
    down_sum = jnp.zeros_like(down)
    for small, large in zip(order, order[::-1]):
        from_before = ((at & small) == 0) if reverse else ((at & small) != 0)
        serves_after = ((at & large) != 0) if reverse else ((at & large) == 0)
        if large == order[-1]:
            sent = down
        else:
            sent = down_sum + jnp.where(serves_after, down, 0.0)
        got_down = swap(sent, axis, large)
        got_up = swap(total, axis, small)
        if large == order[-1]:
            got_down = jnp.where(serves_after, 0.0, got_down)
        down_sum = down_sum + got_down
        up_sum = up_sum + jnp.where(from_before, got_up, 0.0)
        total = total + got_up
    return up_sum, down_sum


def per_device(queries, keys, values, spikes, gain, upstream):
    tok = queries.shape[1]
    width_dev = queries.shape[2]
    heads = width_dev // DH
    half = heads // 2
    width = HEADS * DH
    gain_row = gain.reshape(1, width_dev)
    shape = jax.ShapeDtypeStruct
    flat = (tok, width_dev)
    piece = shape((half, DH, DH), F32)
    whole = shape((1, tok, width_dev), BF16)
    small = 2 * heads * tok * DH * DH
    big = 2 * heads * tok * tok * DH

    spiked, state_a, state_b = call(
        state_kernel, [shape(flat, BF16), piece, piece], keys, spikes, values, flops=small, moved=2**20
    )
    scores, intra = call(
        scores_kernel,
        [shape((heads, tok, tok), BF16), shape(flat, F32)],
        queries, spiked, values,
        flops=2 * big, moved=2**21,
    )
    prior_a, prior_b = scan_pair(state_a, state_b, "ctx", False)
    attended, prior, sums = call(
        attend_kernel,
        [shape(flat, F32), shape((heads, DH, DH), BF16), shape((2, tok), F32)],
        queries, intra, upstream, gain_row, prior_a, prior_b,
        flops=small, moved=2**21,
    )
    for stride in strides("head"):
        sums = sums + swap(sums, "head", stride)
    grad, gain_part, local_a, local_b = call(
        functools.partial(grad_kernel, width),
        [shape(flat, BF16), shape((1, width_dev), F32), piece, piece],
        queries, attended, upstream, gain_row, sums,
        flops=small, moved=2**21,
    )
    grad_query, key_part, value_part = call(
        pairs_kernel,
        [whole, shape(flat, F32), shape(flat, F32)],
        queries, spiked, values, grad, prior, scores,
        flops=4 * big + small, moved=2**22,
    )
    later_a, later_b = scan_pair(local_a, local_b, "ctx", True)
    for axis in ("dp", "ctx"):
        for stride in strides(axis):
            gain_part = gain_part + swap(gain_part, axis, stride)
    grad_key, grad_value = call(
        final_kernel,
        [whole, whole],
        values, spiked, spikes, key_part, value_part, later_a, later_b,
        flops=2 * small, moved=2**22,
    )
    total_tokens = tok * lax.axis_size("ctx") * lax.axis_size("dp")
    grad_gain = gain_part.reshape(width_dev) / math.sqrt(total_tokens)
    return grad_query, grad_key, grad_value, grad_gain


def solution(mesh):
    spec = P("dp", "ctx", "head")
    return jax.shard_map(
        per_device,
        mesh=mesh,
        in_specs=(spec, spec, spec, spec, P("head"), spec),
        out_specs=(spec, spec, spec, P("head")),
        check_vma=False,
    )
```

time: 108 us -> 55.7 us (0.52)
  blocking collectives: 33.5 us -> 0 us
  starting transfers between devices: 0.08 us -> 20.5 us
  between operations: 14.2 us -> 0.78 us
  other arithmetic: 10.4 us -> 0.73 us
  waiting for transfers between devices: 34.4 us -> 25 us
  matrix products: 5.79 us -> 0 us
  local copies, waits for them, and re-layouts: 8.59 us -> 3.62 us
  Pallas kernels: 0 us -> 4.74 us
    all_gather x2 -> x0, waiting for transfers between devices: 34.3 us -> none  [carried_in(): everything = lax.all_gather(array, axis)]
    psum x3 -> x0, blocking collectives: 33.5 us -> none  [the longest x1 15.7 us: per_device(): grad_gain = lax.psum(gain_part, ('dp', 'ctx')) / math.sqrt(total_tokens)]
    ppermute x0 -> x13, waiting for transfers between devices: none -> 25 us  [swap(): return lax.ppermute(array, axis, [(i, i ^ stride) for i in range(size)])]
    ppermute x0 -> x13, starting transfers between devices: none -> 20.5 us  [swap(): return lax.ppermute(array, axis, [(i, i ^ stride) for i in range(size)])]
    select_n x8 -> x0, other arithmetic: 8.32 us -> none  [hop(): return jnp.where(reached, new, before)]
    dot_general x12 -> x0, matrix products: 5.79 us -> none  [the longest x1 1.35 us: per_device(): jnp.einsum('htd,hde->hte', query_heads, prior_state, preferred_element_ty...]
    pallas_call x0 -> x6, Pallas kernels: none -> 4.74 us  [call(): pl.pallas_call(body, out_shape=outs, in_specs=[VMEM] * len(args), out_spe...]
    unnamed x19 -> x16, local copies, waits for them, and re-layouts: 6.23 us -> 3.62 us
  transfers between devices with their start and end apart: 2 -> 13, of which waited for: 2 -> 10; matrix products, arithmetic and copies ran while one was open for 4% -> 1% of each run, Pallas kernels for 0% -> 5%
where the time goes in v1:
time: 55.7 us; the launch traced here: 55.4 us
  waiting for transfers between devices  25 us (45%)
  starting transfers between devices  20.5 us (37%)
  Pallas kernels  4.74 us (9%)
  local copies, waits for them, and re-layouts  3.62 us (6%)
  between operations  0.78 us (1%)
  other arithmetic  0.73 us (1%)
    ppermute x13, waiting for transfers between devices, swap(): return lax.ppermute(array, axis, [(i, i ^ stride) for i in range(size)])  25 us
    ppermute x13, starting transfers between devices, swap(): return lax.ppermute(array, axis, [(i, i ^ stride) for i in range(size)])  20.5 us
    pallas_call x6, Pallas kernels, call(): pl.pallas_call(body, out_shape=outs, in_specs=[VMEM] * len(args), out_spe...  4.74 us
    unnamed x16, local copies, waits for them, and re-layouts  3.62 us
  transfers between devices with their start and end apart: 13, of which 10 were waited for; matrix products, arithmetic and copies ran while one was open for 1% of the time, Pallas kernels for 5%

profile of v1, /device:TPU:0, one launch (start us, length us, event | category | flops | bytes accessed | tf_op | source)
XLA Modules:
  0.0 55.4 jit_solution(4304524233288123589)
XLA Ops:
  0.6 0.9 %copy-done.1 = bf16[1,256,512]{2,1,0:T(8,128)(2,1)S(1)} copy-done((bf16[1,256,512]{2,1,0:T(8,128)(2,1)S(1)}, bf16[1,256,512]{2,1,0:T(8,128)(2,1)}, u32[]{:S(2)}) %copy-start.1) | copy-done | bytes 262168
  1.6 1.0 %copy-done.3 = s32[1,256,512]{2,1,0:T(8,128)S(1)} copy-done((s32[1,256,512]{2,1,0:T(8,128)S(1)}, s32[1,256,512]{2,1,0:T(8,128)}, u32[]{:S(2)}) %copy-start.3) | copy-done | bytes 524312
  2.6 0.9 %copy-done.6 = bf16[1,256,512]{2,1,0:T(8,128)(2,1)S(1)} copy-done((bf16[1,256,512]{2,1,0:T(8,128)(2,1)S(1)}, bf16[1,256,512]{2,1,0:T(8,128)(2,1)}, u32[]{:S(2)}) %copy-start.6) | copy-done | bytes 262168
  3.6 0.3 shard_map.93
  3.9 4.1 %collective-permute-start.2 = (f32[2,128,128]{2,1,0:T(8,128)S(1)}, f32[2,128,128]{2,1,0:T(8,128)S(1)}, u32[]{:S(2)}, u32[]{:S(2)}) collective-permute-start(f32[2,128,128]{2,1,0:T(8,128)S(1)} %get-tuple-element.24), channel_id=1, source_target_pairs={{0,8},{4,12},{8,0},{12,4},{1,9},{5,13},{9,1},{13,5},{2,10},{6,14},... | collective-permute-start | bytes 393224 | tf_op jit(solution)/shard_map/ppermute | solution.py:123
  8.0 1.6 %collective-permute-start = (f32[2,128,128]{2,1,0:T(8,128)S(1)}, f32[2,128,128]{2,1,0:T(8,128)S(1)}, u32[]{:S(2)}, u32[]{:S(2)}) collective-permute-start(f32[2,128,128]{2,1,0:T(8,128)S(1)} %get-tuple-element.23), channel_id=1, source_target_pairs={{0,4},{4,0},{8,12},{12,8},{1,5},{5,1},{9,13},{13,9},{2,6},{6,2},{1... | collective-permute-start | bytes 393224 | tf_op jit(solution)/shard_map/ppermute | solution.py:123
  9.6 4.8 %collective-permute-done.2 = f32[2,128,128]{2,1,0:T(8,128)S(1)} collective-permute-done((f32[2,128,128]{2,1,0:T(8,128)S(1)}, f32[2,128,128]{2,1,0:T(8,128)S(1)}, u32[]{:S(2)}, u32[]{:S(2)}) %collective-permute-start.2) | collective-permute-done | bytes 131104 | tf_op jit(solution)/shard_map/ppermute | solution.py:123
  14.4 0.7 %collective-permute-start.3 = (f32[2,128,128]{2,1,0:T(8,128)S(1)}, f32[2,128,128]{2,1,0:T(8,128)S(1)}, u32[]{:S(2)}, u32[]{:S(2)}) collective-permute-start(f32[2,128,128]{2,1,0:T(8,128)S(1)} %select_add_fusion.2), channel_id=1, source_target_pairs={{0,4},{4,0},{8,12},{12,8},{1,5},{5,1},{9,13},{13,9},{2,6},{6,2},{1... | collective-permute-start | bytes 393224 | tf_op jit(solution)/shard_map/ppermute | solution.py:123
  15.1 0.7 %shard_map.94 = (bf16[4,256,256]{2,1,0:T(8,128)(2,1)S(1)}, f32[256,512]{1,0:T(8,128)S(1)}) custom-call(bf16[1,256,512]{2,1,0:T(8,128)(2,1)S(1)} %copy-done, bf16[256,512]{1,0:T(8,128)(2,1)S(1)} %get-tuple-element.21.spiked, bf16[1,256,512]{2,1,0:T(8,128)(2,1)S(1)} %copy-done.2), custom_call_target="tpu_custom_call" | custom-call | flops 134217728 | bytes 2097152 | tf_op jit(solution)/shard_map/pallas_call | solution.py:29
  15.8 3.4 %collective-permute-start.1 = (f32[2,128,128]{2,1,0:T(8,128)S(1)}, f32[2,128,128]{2,1,0:T(8,128)S(1)}, u32[]{:S(2)}, u32[]{:S(2)}) collective-permute-start(f32[2,128,128]{2,1,0:T(8,128)S(1)} %add.39), channel_id=1, source_target_pairs={{0,8},{4,12},{8,0},{12,4},{1,9},{5,13},{9,1},{13,5},{2,10},{6,14},... | collective-permute-start | bytes 393224 | tf_op jit(solution)/shard_map/ppermute | solution.py:123
  19.2 0.2 collective-permute-done.3
  19.5 6.0 %collective-permute-done.1 = f32[2,128,128]{2,1,0:T(8,128)S(1)} collective-permute-done((f32[2,128,128]{2,1,0:T(8,128)S(1)}, f32[2,128,128]{2,1,0:T(8,128)S(1)}, u32[]{:S(2)}, u32[]{:S(2)}) %collective-permute-start.1) | collective-permute-done | bytes 131104 | tf_op jit(solution)/shard_map/ppermute | solution.py:123
  25.5 0.7 %copy-done.7 = f32[512]{0:T(512)S(1)} copy-done((f32[512]{0:T(512)S(1)}, f32[512]{0:T(512)}, u32[]{:S(2)}) %copy-start.7) | copy-done | bytes 2072
  26.1 0.4 shard_map.95
  26.5 1.6 %collective-permute-start.4 = (f32[2,256]{1,0:T(2,128)S(1)}, f32[2,256]{1,0:T(2,128)S(1)}, u32[]{:S(2)}, u32[]{:S(2)}) collective-permute-start(f32[2,256]{1,0:T(2,128)S(1)} %get-tuple-element.26), channel_id=1, source_target_pairs={{0,1},{1,0},{2,3},{3,2},{4,5},{5,4},{6,7},{7,6},{8,9},{9,8},{10,11... | collective-permute-start | bytes 6152 | tf_op jit(solution)/shard_map/ppermute | solution.py:123
  28.1 2.1 %collective-permute-done.4 = f32[2,256]{1,0:T(2,128)S(1)} collective-permute-done((f32[2,256]{1,0:T(2,128)S(1)}, f32[2,256]{1,0:T(2,128)S(1)}, u32[]{:S(2)}, u32[]{:S(2)}) %collective-permute-start.4) | collective-permute-done | bytes 2080 | tf_op jit(solution)/shard_map/ppermute | solution.py:123
  30.2 1.5 %collective-permute-start.5 = (f32[2,256]{1,0:T(2,128)S(1)}, f32[2,256]{1,0:T(2,128)S(1)}, u32[]{:S(2)}, u32[]{:S(2)}) collective-permute-start(f32[2,256]{1,0:T(2,128)S(1)} %add.43), channel_id=1, source_target_pairs={{0,2},{1,3},{2,0},{3,1},{4,6},{5,7},{6,4},{7,5},{8,10},{9,11},{10,... | collective-permute-start | bytes 6152 | tf_op jit(solution)/shard_map/ppermute | solution.py:123
  31.7 2.1 %collective-permute-done.5 = f32[2,256]{1,0:T(2,128)S(1)} collective-permute-done((f32[2,256]{1,0:T(2,128)S(1)}, f32[2,256]{1,0:T(2,128)S(1)}, u32[]{:S(2)}, u32[]{:S(2)}) %collective-permute-start.5) | collective-permute-done | bytes 2080 | tf_op jit(solution)/shard_map/ppermute | solution.py:123
  33.7 0.4 shard_map.96
  34.2 0.1 collective-permute-start.10
  34.3 1.1 %collective-permute-done.10 = f32[1,512]{1,0:T(1,128)S(1)} collective-permute-done((f32[1,512]{1,0:T(1,128)S(1)}, f32[1,512]{1,0:T(1,128)S(1)}, u32[]{:S(2)}, u32[]{:S(2)}) %collective-permute-start.10) | collective-permute-done | bytes 2080 | tf_op jit(solution)/shard_map/ppermute | solution.py:123
  35.4 2.0 %collective-permute-start.6 = (f32[2,128,128]{2,1,0:T(8,128)S(1)}, f32[2,128,128]{2,1,0:T(8,128)S(1)}, u32[]{:S(2)}, u32[]{:S(2)}) collective-permute-start(f32[2,128,128]{2,1,0:T(8,128)S(1)} %get-tuple-element.33), channel_id=1, source_target_pairs={{0,4},{4,0},{8,12},{12,8},{1,5},{5,1},{9,13},{13,9},{2,6},{6,2},{1... | collective-permute-start | bytes 393224 | tf_op jit(solution)/shard_map/ppermute | solution.py:123
  37.4 1.0 %collective-permute-start.8 = (f32[2,128,128]{2,1,0:T(8,128)S(1)}, f32[2,128,128]{2,1,0:T(8,128)S(1)}, u32[]{:S(2)}, u32[]{:S(2)}) collective-permute-start(f32[2,128,128]{2,1,0:T(8,128)S(1)} %get-tuple-element.34), channel_id=1, source_target_pairs={{0,8},{4,12},{8,0},{12,4},{1,9},{5,13},{9,1},{13,5},{2,10},{6,14},... | collective-permute-start | bytes 393224 | tf_op jit(solution)/shard_map/ppermute | solution.py:123
  38.5 0.5 collective-permute-done.11
  39.0 1.4 %collective-permute-start.12 = (f32[1,512]{1,0:T(1,128)S(1)}, f32[1,512]{1,0:T(1,128)S(1)}, u32[]{:S(2)}, u32[]{:S(2)}) collective-permute-start(f32[1,512]{1,0:T(1,128)S(1)} %add.50), channel_id=1, source_target_pairs={{0,8},{4,12},{8,0},{12,4},{1,9},{5,13},{9,1},{13,5},{2,10},{6,14},... | collective-permute-start | bytes 6152 | tf_op jit(solution)/shard_map/ppermute | solution.py:123
  40.4 1.9 %shard_map.97 = (bf16[1,256,512]{2,1,0:T(8,128)(2,1)}, f32[256,512]{1,0:T(8,128)S(1)}, f32[256,512]{1,0:T(8,128)S(1)}) custom-call(bf16[1,256,512]{2,1,0:T(8,128)(2,1)S(1)} %copy-done, bf16[256,512]{1,0:T(8,128)(2,1)S(1)} %get-tuple-element.21.spiked, bf16[1,256,512]{2,1,0:T(8,128)(2,1)S(1)} %copy-done.2, bf16[256,512]{1,0:T(8,128)(2,1)S(1)} %get-tuple-element.27.grad, ...), custom_call_target="tpu_custom_call" | custom-call | flops 301989888 | bytes 4194304 | tf_op jit(solution)/shard_map/pallas_call | solution.py:29
  42.4 3.9 %collective-permute-done.12 = f32[1,512]{1,0:T(1,128)S(1)} collective-permute-done((f32[1,512]{1,0:T(1,128)S(1)}, f32[1,512]{1,0:T(1,128)S(1)}, u32[]{:S(2)}, u32[]{:S(2)}) %collective-permute-start.12) | collective-permute-done | bytes 2080 | tf_op jit(solution)/shard_map/ppermute | solution.py:123
  46.3 0.6 %add_multiply_fusion = f32[1,512]{1,0:T(1,128)} fusion(f32[1,512]{1,0:T(1,128)S(1)} %add.50, f32[1,512]{1,0:T(1,128)S(1)} %collective-permute-done.12), kind=kLoop, calls=%fused_computation.6 | loop fusion | flops 1024 | bytes 6144 | tf_op jit(solution)/shard_map/div | solution.py:210
  46.9 0.4 collective-permute-start.7
  47.3 2.7 %collective-permute-start.9 = (f32[2,128,128]{2,1,0:T(8,128)S(1)}, f32[2,128,128]{2,1,0:T(8,128)S(1)}, u32[]{:S(2)}, u32[]{:S(2)}) collective-permute-start(f32[2,128,128]{2,1,0:T(8,128)S(1)} %select_add_fusion), channel_id=1, source_target_pairs={{0,4},{4,0},{8,12},{12,8},{1,5},{5,1},{9,13},{13,9},{2,6},{6,2},{1... | collective-permute-start | bytes 393224 | tf_op jit(solution)/shard_map/ppermute | solution.py:123
  50.0 4.2 %collective-permute-done.7 = f32[2,128,128]{2,1,0:T(8,128)S(1)} collective-permute-done((f32[2,128,128]{2,1,0:T(8,128)S(1)}, f32[2,128,128]{2,1,0:T(8,128)S(1)}, u32[]{:S(2)}, u32[]{:S(2)}) %collective-permute-start.7) | collective-permute-done | bytes 131104 | tf_op jit(solution)/shard_map/ppermute | solution.py:123
  54.3 1.1 %shard_map.98 = (bf16[1,256,512]{2,1,0:T(8,128)(2,1)}, bf16[1,256,512]{2,1,0:T(8,128)(2,1)}) custom-call(bf16[1,256,512]{2,1,0:T(8,128)(2,1)S(1)} %copy-done.2, bf16[256,512]{1,0:T(8,128)(2,1)S(1)} %get-tuple-element.21.spiked, s32[1,256,512]{2,1,0:T(8,128)S(1)} %copy-done.4, f32[256,512]{1,0:T(8,128)S(1)} %get-tuple-element.31.key_part, ...), custom_call_target="tpu_custom_call" | custom-call | flops 67108864 | bytes 4194304 | tf_op jit(solution)/shard_map/pallas_call | solution.py:29
  (29 shorter events, 0.2 us)
Async XLA Ops:
  0.6 1.0 %copy-start.1 = (bf16[1,256,512]{2,1,0:T(8,128)(2,1)S(1)}, bf16[1,256,512]{2,1,0:T(8,128)(2,1)}, u32[]{:S(2)}) copy-start(bf16[1,256,512]{2,1,0:T(8,128)(2,1)} %values.7) | copy-start | bytes 786436
  1.6 1.0 %copy-start.3 = (s32[1,256,512]{2,1,0:T(8,128)S(1)}, s32[1,256,512]{2,1,0:T(8,128)}, u32[]{:S(2)}) copy-start(s32[1,256,512]{2,1,0:T(8,128)} %spikes.3) | copy-start | bytes 1572868
  2.6 0.9 %copy-start.6 = (bf16[1,256,512]{2,1,0:T(8,128)(2,1)S(1)}, bf16[1,256,512]{2,1,0:T(8,128)(2,1)}, u32[]{:S(2)}) copy-start(bf16[1,256,512]{2,1,0:T(8,128)(2,1)} %keys.1) | copy-start | bytes 786436
  3.6 11.5 %copy-start.2 = (bf16[1,256,512]{2,1,0:T(8,128)(2,1)S(1)}, bf16[1,256,512]{2,1,0:T(8,128)(2,1)}, u32[]{:S(2)}) copy-start(bf16[1,256,512]{2,1,0:T(8,128)(2,1)} %values.7) | copy-start | bytes 786436
  3.9 11.2 %copy-start = (bf16[1,256,512]{2,1,0:T(8,128)(2,1)S(1)}, bf16[1,256,512]{2,1,0:T(8,128)(2,1)}, u32[]{:S(2)}) copy-start(bf16[1,256,512]{2,1,0:T(8,128)(2,1)} %queries.7) | copy-start | bytes 786436
  3.9 10.5 %collective-permute-start.2 = (f32[2,128,128]{2,1,0:T(8,128)S(1)}, f32[2,128,128]{2,1,0:T(8,128)S(1)}, u32[]{:S(2)}, u32[]{:S(2)}) collective-permute-start(f32[2,128,128]{2,1,0:T(8,128)S(1)} %get-tuple-element.24), channel_id=1, source_target_pairs={{0,8},{4,12},{8,0},{12,4},{1,9},{5,13},{9,1},{13,5},{2,10},{6,14},... | collective-permute-start | bytes 393224 | tf_op jit(solution)/shard_map/ppermute | solution.py:123
  8.0 7.8 %collective-permute-start = (f32[2,128,128]{2,1,0:T(8,128)S(1)}, f32[2,128,128]{2,1,0:T(8,128)S(1)}, u32[]{:S(2)}, u32[]{:S(2)}) collective-permute-start(f32[2,128,128]{2,1,0:T(8,128)S(1)} %get-tuple-element.23), channel_id=1, source_target_pairs={{0,4},{4,0},{8,12},{12,8},{1,5},{5,1},{9,13},{13,9},{2,6},{6,2},{1... | collective-permute-start | bytes 393224 | tf_op jit(solution)/shard_map/ppermute | solution.py:123
  14.4 5.0 %collective-permute-start.3 = (f32[2,128,128]{2,1,0:T(8,128)S(1)}, f32[2,128,128]{2,1,0:T(8,128)S(1)}, u32[]{:S(2)}, u32[]{:S(2)}) collective-permute-start(f32[2,128,128]{2,1,0:T(8,128)S(1)} %select_add_fusion.2), channel_id=1, source_target_pairs={{0,4},{4,0},{8,12},{12,8},{1,5},{5,1},{9,13},{13,9},{2,6},{6,2},{1... | collective-permute-start | bytes 393224 | tf_op jit(solution)/shard_map/ppermute | solution.py:123
  15.8 9.7 %collective-permute-start.1 = (f32[2,128,128]{2,1,0:T(8,128)S(1)}, f32[2,128,128]{2,1,0:T(8,128)S(1)}, u32[]{:S(2)}, u32[]{:S(2)}) collective-permute-start(f32[2,128,128]{2,1,0:T(8,128)S(1)} %add.39), channel_id=1, source_target_pairs={{0,8},{4,12},{8,0},{12,4},{1,9},{5,13},{9,1},{13,5},{2,10},{6,14},... | collective-permute-start | bytes 393224 | tf_op jit(solution)/shard_map/ppermute | solution.py:123
  19.5 6.0 %copy-start.5 = (bf16[1,256,512]{2,1,0:T(8,128)(2,1)S(1)}, bf16[1,256,512]{2,1,0:T(8,128)(2,1)}, u32[]{:S(2)}) copy-start(bf16[1,256,512]{2,1,0:T(8,128)(2,1)} %upstream.3) | copy-start | bytes 786436
  25.5 0.7 %copy-start.7 = (f32[512]{0:T(512)S(1)}, f32[512]{0:T(512)}, u32[]{:S(2)}) copy-start(f32[512]{0:T(512)} %param.10) | copy-start | bytes 6148
  26.5 3.6 %collective-permute-start.4 = (f32[2,256]{1,0:T(2,128)S(1)}, f32[2,256]{1,0:T(2,128)S(1)}, u32[]{:S(2)}, u32[]{:S(2)}) collective-permute-start(f32[2,256]{1,0:T(2,128)S(1)} %get-tuple-element.26), channel_id=1, source_target_pairs={{0,1},{1,0},{2,3},{3,2},{4,5},{5,4},{6,7},{7,6},{8,9},{9,8},{10,11... | collective-permute-start | bytes 6152 | tf_op jit(solution)/shard_map/ppermute | solution.py:123
  30.2 3.6 %collective-permute-start.5 = (f32[2,256]{1,0:T(2,128)S(1)}, f32[2,256]{1,0:T(2,128)S(1)}, u32[]{:S(2)}, u32[]{:S(2)}) collective-permute-start(f32[2,256]{1,0:T(2,128)S(1)} %add.43), channel_id=1, source_target_pairs={{0,2},{1,3},{2,0},{3,1},{4,6},{5,7},{6,4},{7,5},{8,10},{9,11},{10,... | collective-permute-start | bytes 6152 | tf_op jit(solution)/shard_map/ppermute | solution.py:123
  34.2 1.2 %collective-permute-start.10 = (f32[1,512]{1,0:T(1,128)S(1)}, f32[1,512]{1,0:T(1,128)S(1)}, u32[]{:S(2)}, u32[]{:S(2)}) collective-permute-start(f32[1,512]{1,0:T(1,128)S(1)} %get-tuple-element.37), channel_id=1, source_target_pairs={{0,16},{16,0},{1,17},{17,1},{2,18},{18,2},{3,19},{19,3},{4,20},{20... | collective-permute-start | bytes 6152 | tf_op jit(solution)/shard_map/ppermute | solution.py:123
  35.4 3.6 %collective-permute-start.11 = (f32[1,512]{1,0:T(1,128)S(1)}, f32[1,512]{1,0:T(1,128)S(1)}, u32[]{:S(2)}, u32[]{:S(2)}) collective-permute-start(f32[1,512]{1,0:T(1,128)S(1)} %add.49), channel_id=1, source_target_pairs={{0,4},{4,0},{8,12},{12,8},{1,5},{5,1},{9,13},{13,9},{2,6},{6,2},{1... | collective-permute-start | bytes 6152 | tf_op jit(solution)/shard_map/ppermute | solution.py:123
  35.4 11.5 %collective-permute-start.6 = (f32[2,128,128]{2,1,0:T(8,128)S(1)}, f32[2,128,128]{2,1,0:T(8,128)S(1)}, u32[]{:S(2)}, u32[]{:S(2)}) collective-permute-start(f32[2,128,128]{2,1,0:T(8,128)S(1)} %get-tuple-element.33), channel_id=1, source_target_pairs={{0,4},{4,0},{8,12},{12,8},{1,5},{5,1},{9,13},{13,9},{2,6},{6,2},{1... | collective-permute-start | bytes 393224 | tf_op jit(solution)/shard_map/ppermute | solution.py:123
  37.4 9.8 %collective-permute-start.8 = (f32[2,128,128]{2,1,0:T(8,128)S(1)}, f32[2,128,128]{2,1,0:T(8,128)S(1)}, u32[]{:S(2)}, u32[]{:S(2)}) collective-permute-start(f32[2,128,128]{2,1,0:T(8,128)S(1)} %get-tuple-element.34), channel_id=1, source_target_pairs={{0,8},{4,12},{8,0},{12,4},{1,9},{5,13},{9,1},{13,5},{2,10},{6,14},... | collective-permute-start | bytes 393224 | tf_op jit(solution)/shard_map/ppermute | solution.py:123
  39.0 7.3 %collective-permute-start.12 = (f32[1,512]{1,0:T(1,128)S(1)}, f32[1,512]{1,0:T(1,128)S(1)}, u32[]{:S(2)}, u32[]{:S(2)}) collective-permute-start(f32[1,512]{1,0:T(1,128)S(1)} %add.50), channel_id=1, source_target_pairs={{0,8},{4,12},{8,0},{12,4},{1,9},{5,13},{9,1},{13,5},{2,10},{6,14},... | collective-permute-start | bytes 6152 | tf_op jit(solution)/shard_map/ppermute | solution.py:123
  46.9 7.4 %copy-start.4 = (s32[1,256,512]{2,1,0:T(8,128)S(1)}, s32[1,256,512]{2,1,0:T(8,128)}, u32[]{:S(2)}) copy-start(s32[1,256,512]{2,1,0:T(8,128)} %spikes.3) | copy-start | bytes 1572868
  46.9 7.3 %collective-permute-start.7 = (f32[2,128,128]{2,1,0:T(8,128)S(1)}, f32[2,128,128]{2,1,0:T(8,128)S(1)}, u32[]{:S(2)}, u32[]{:S(2)}) collective-permute-start(f32[2,128,128]{2,1,0:T(8,128)S(1)} %add.45), channel_id=1, source_target_pairs={{0,8},{4,12},{8,0},{12,4},{1,9},{5,13},{9,1},{13,5},{2,10},{6,14},... | collective-permute-start | bytes 393224 | tf_op jit(solution)/shard_map/ppermute | solution.py:123
  47.3 7.0 %collective-permute-start.9 = (f32[2,128,128]{2,1,0:T(8,128)S(1)}, f32[2,128,128]{2,1,0:T(8,128)S(1)}, u32[]{:S(2)}, u32[]{:S(2)}) collective-permute-start(f32[2,128,128]{2,1,0:T(8,128)S(1)} %select_add_fusion), channel_id=1, source_target_pairs={{0,4},{4,0},{8,12},{12,8},{1,5},{5,1},{9,13},{13,9},{2,6},{6,2},{1... | collective-permute-start | bytes 393224 | tf_op jit(solution)/shard_map/ppermute | solution.py:123

commit v2 on v1

v2 whole, which is shorter than its diff:
```python
import functools
import math

import jax
import jax.numpy as jnp
from jax import lax
from jax.experimental import pallas as pl
from jax.experimental.pallas import tpu as pltpu
from jax.sharding import PartitionSpec as P

DH = 128
HEADS = 16
EPS = 1e-06

F32 = jnp.float32
BF16 = jnp.bfloat16
VMEM = pl.BlockSpec(memory_space=pltpu.VMEM)
HBM = pl.BlockSpec(memory_space=pltpu.HBM)
GAIN_ROWS = 8


def dot(a, b, ca, cb):
    return lax.dot_general(a, b, (((ca,), (cb,)), ((), ())), preferred_element_type=F32)


def cols(h):
    return slice(h * DH, (h + 1) * DH)


def block_of(pieces, h):
    per = pieces[-1].shape[0] // DH
    return pieces[h // per], cols(h % per)


def call(body, outs, *args, hbm=(), hbm_outs=(), aliases={}, scratch=(), flops=0, moved=0):
    args = [
        pltpu.with_memory_space_constraint(arg, pltpu.HBM) if k in hbm else arg
        for k, arg in enumerate(args)
    ]
    return pl.pallas_call(
        body,
        out_shape=outs,
        in_specs=[HBM if k in hbm else VMEM for k in range(len(args))],
        out_specs=[HBM if k in hbm_outs else VMEM for k in range(len(outs))],
        input_output_aliases=aliases,
        scratch_shapes=scratch,
        cost_estimate=pl.CostEstimate(flops=flops, bytes_accessed=moved, transcendentals=0),
        compiler_params=pltpu.CompilerParams(vmem_limit_bytes=32 * 2**20),
    )(*args)


def causal_mask(tok):
    rows = lax.broadcasted_iota(jnp.int32, (tok, tok), 0)
    return rows >= lax.broadcasted_iota(jnp.int32, (tok, tok), 1)


def score_heads(queries, spiked, values, scores, intra):
    heads, tok, _ = scores.shape
    causal = causal_mask(tok)
    for h in range(heads):
        raw = dot(queries[0, :, cols(h)], spiked[:, cols(h)], 1, 1)
        block = jnp.where(causal, raw, 0.0).astype(BF16)
        scores[h] = block
        intra[:, cols(h)] = dot(block, values[0, :, cols(h)], 1, 0)


def scores_first():
    return lax.axis_index("dp") % 2 == 1


def state_kernel(
    queries, keys, spikes, values, held_queries, spiked, held_values, scores, intra, *rest
):
    *states, key_buf, spike_buf, sems = rest
    heads = spiked.shape[1] // DH
    pairs = (
        (keys, key_buf), (spikes, spike_buf), (values, held_values), (queries, held_queries)
    )
    copies = [pltpu.make_async_copy(src, dst, sems.at[k]) for k, (src, dst) in enumerate(pairs)]
    for copy in copies:
        copy.start()
    for copy in copies[:3]:
        copy.wait()
    for h in range(heads):
        block = key_buf[0, :, cols(h)] * spike_buf[0, :, cols(h)].astype(F32).astype(BF16)
        spiked[:, cols(h)] = block
        ref, rows = block_of(states, h)
        ref[rows, :] = dot(block, held_values[0, :, cols(h)], 0, 0)
    copies[3].wait()

    @pl.when(scores_first())
    def _():
        score_heads(held_queries, spiked, held_values, scores, intra)


def scores_kernel(
    queries, spiked, values, upstream, gain, after, scores_in, intra_in,
    scores, intra, scaled, upper, gain_buf, sems,
):
    del after, scores_in, intra_in
    copies = [
        pltpu.make_async_copy(upstream, upper, sems.at[0]),
        pltpu.make_async_copy(gain, gain_buf, sems.at[1]),
    ]
    for copy in copies:
        copy.start()

    @pl.when(jnp.logical_not(scores_first()))
    def _():
        score_heads(queries, spiked, values, scores, intra)

    for copy in copies:
        copy.wait()
    scaled[...] = upper[0].astype(F32) * gain_buf[...]


def attend_kernel(queries, intra, scaled, sum_a, sum_b, attended, prior, sums):
    heads = prior.shape[0]
    tok = intra.shape[0]
    square = jnp.zeros((tok, DH), F32)
    cross = jnp.zeros((tok, DH), F32)
    for h in range(heads):
        ref, rows = block_of((sum_a, sum_b), h)
        state = ref[rows, :].astype(BF16)
        prior[h] = state
        block = dot(queries[0, :, cols(h)], state, 1, 0) + intra[:, cols(h)]
        attended[:, cols(h)] = block
        square += block * block
        cross += scaled[:, cols(h)] * block
    sums[0:1, :] = jnp.sum(square.T, axis=0, keepdims=True)
    sums[1:2, :] = jnp.sum(cross.T, axis=0, keepdims=True)


def grad_kernel(width, queries, attended, scaled, upper, sums, grad, *locals_):
    tok = attended.shape[0]
    heads = attended.shape[1] // DH
    inv = lax.rsqrt(sums[0:1, :] / width + EPS)
    factor = inv * inv * inv * (sums[1:2, :] / width)
    inv = jnp.broadcast_to(inv, (DH, tok)).T
    factor = jnp.broadcast_to(factor, (DH, tok)).T
    gain_at = locals_[0].shape[0] - GAIN_ROWS
    locals_[0][gain_at:, :] = jnp.zeros((GAIN_ROWS, DH), F32)
    for h in range(heads):
        block = attended[:, cols(h)]
        result = (inv * scaled[:, cols(h)] - block * factor).astype(BF16)
        grad[:, cols(h)] = result
        ref, rows = block_of(locals_, h)
        ref[rows, :] = dot(queries[0, :, cols(h)], result, 0, 0)
        terms = upper[0, :, cols(h)].astype(F32) * block * inv
        locals_[0][gain_at + h : gain_at + h + 1, :] = jnp.sum(terms, axis=0, keepdims=True)


def pairs_kernel(
    queries, spiked, values, grad, prior, scores, after, grad_query, key_part, value_part
):
    del after
    heads, tok, _ = scores.shape
    causal = causal_mask(tok)
    for h in range(heads):
        result = grad[:, cols(h)]
        raw = dot(result, values[0, :, cols(h)], 1, 1)
        pairs = jnp.where(causal, raw, 0.0).astype(BF16)
        query_part = dot(result, prior[h], 1, 1) + dot(pairs, spiked[:, cols(h)], 1, 0)
        grad_query[0, :, cols(h)] = query_part.astype(BF16)
        key_part[:, cols(h)] = dot(pairs, queries[0, :, cols(h)], 0, 0)
        value_part[:, cols(h)] = dot(scores[h], result, 0, 0)


def final_half(first, values, spiked, spikes, key_part, value_part, sums, outs, bufs, sems):
    copies = []
    for h in range(sums.shape[0] // DH):
        at = cols(first + h)
        later = sums[cols(h), :].astype(BF16)
        inner = key_part[:, at] + dot(values[0, :, at], later, 1, 1)
        bufs[0][0, :, cols(h)] = (inner * spikes[0, :, at].astype(F32)).astype(BF16)
        block = value_part[:, at] + dot(spiked[:, at], later, 1, 0)
        bufs[1][0, :, cols(h)] = block.astype(BF16)
        for k in range(2):
            copies.append(
                pltpu.make_async_copy(
                    bufs[k].at[:, :, cols(h)], outs[k].at[:, :, at], sems.at[h, k]
                )
            )
            copies[-1].start()
    return copies


def final_first_kernel(
    values, spiked, spikes, key_part, value_part, sums, grad_key, grad_value, *scratch
):
    *bufs, sems = scratch
    outs = (grad_key, grad_value)
    for copy in final_half(
        0, values, spiked, spikes, key_part, value_part, sums, outs, bufs, sems
    ):
        copy.wait()


def final_last_kernel(
    scale, values, spiked, spikes, key_part, value_part, sums, gain_here, gain_there,
    key_in, value_in, grad_key, grad_value, grad_gain, *scratch,
):
    del key_in, value_in
    *bufs, sems = scratch
    outs = (grad_key, grad_value)
    heads = spiked.shape[1] // DH
    copies = final_half(
        heads // 2, values, spiked, spikes, key_part, value_part, sums, outs, bufs, sems
    )
    for h in range(heads):
        grad_gain[:, cols(h)] = (gain_here[h : h + 1, :] + gain_there[h : h + 1, :]) * scale
    for copy in copies:
        copy.wait()


def swap(array, axis, stride):
    size = lax.axis_size(axis)
    return lax.ppermute(array, axis, [(i, i ^ stride) for i in range(size)])


def strides(axis):
    size = lax.axis_size(axis)
    assert size & (size - 1) == 0
    return [1 << k for k in range(size.bit_length() - 1)]


def scan_pair(up, down, axis, reverse, between, finish=None):
    at = lax.axis_index(axis)
    order = strides(axis)
    total = up
    up_sum = jnp.zeros_like(up)
    down_sum = jnp.zeros_like(down)
    result = None
    for small, large in zip(order, order[::-1]):
        first = large == order[-1]
        from_before = ((at & small) == 0) if reverse else ((at & small) != 0)
        serves_after = ((at & large) != 0) if reverse else ((at & large) == 0)
        sent = down if first else down_sum + jnp.where(serves_after, down, 0.0)
        got_up = swap(total, axis, small)
        got_down = swap(sent, axis, large)
        total = total + got_up
        up_sum = up_sum + jnp.where(from_before, got_up, 0.0)
        if first:
            token, result = between(total)
            got_down, _ = lax.optimization_barrier((got_down, token))
            got_down = jnp.where(serves_after, 0.0, got_down)
        elif small != order[-1] or finish is None:
            got_down, up_sum = lax.optimization_barrier((got_down, up_sum))
        else:
            token, result = finish(up_sum, total, result)
            got_down, _ = lax.optimization_barrier((got_down, token))
        down_sum = down_sum + got_down
    return up_sum, down_sum, result


def per_device(queries, keys, values, spikes, gain, upstream):
    tok = queries.shape[1]
    width_dev = queries.shape[2]
    heads = width_dev // DH
    half = heads // 2
    width = HEADS * DH
    gain_row = gain.reshape(1, width_dev)
    shape = jax.ShapeDtypeStruct
    flat = (tok, width_dev)
    piece = shape((half * DH, DH), F32)
    longer = shape((half * DH + GAIN_ROWS, DH), F32)
    whole = shape((1, tok, width_dev), BF16)
    small = 2 * heads * tok * DH * DH
    big = 2 * heads * tok * tok * DH

    held_queries, spiked, held_values, scores, intra, state_a, state_b = call(
        state_kernel,
        [
            whole, shape(flat, BF16), whole,
            shape((heads, tok, tok), BF16), shape(flat, F32), piece, piece,
        ],
        queries, keys, spikes, values,
        hbm=(0, 1, 2, 3),
        scratch=[
            pltpu.VMEM((1, *flat), BF16),
            pltpu.VMEM((1, *flat), jnp.int32),
            pltpu.SemaphoreType.DMA((4,)),
        ],
        flops=small, moved=2**20,
    )

    def score(total):
        outs = call(
            scores_kernel,
            [shape((heads, tok, tok), BF16), shape(flat, F32), shape(flat, F32), whole],
            held_queries, spiked, held_values, upstream, gain_row, total, scores, intra,
            hbm=(3, 4),
            aliases={6: 0, 7: 1},
            scratch=[pltpu.VMEM((1, width_dev), F32), pltpu.SemaphoreType.DMA((2,))],
            flops=2 * big, moved=2**21,
        )
        return outs[1], outs

    prior_a, prior_b, (scores, intra, scaled, upper) = scan_pair(
        state_a, state_b, "ctx", False, score
    )
    attended, prior, sums = call(
        attend_kernel,
        [shape(flat, F32), shape((heads, DH, DH), BF16), shape((2, tok), F32)],
        held_queries, intra, scaled, prior_a, prior_b,
        flops=small, moved=2**21,
    )
    for stride in strides("head"):
        sums = sums + swap(sums, "head", stride)
    grad, local_a, local_b = call(
        functools.partial(grad_kernel, width),
        [shape(flat, BF16), longer, piece],
        held_queries, attended, scaled, upper, sums,
        flops=small, moved=2**21,
    )

    def pair(total):
        outs = call(
            pairs_kernel,
            [whole, shape(flat, F32), shape(flat, F32)],
            held_queries, spiked, held_values, grad, prior, scores, total,
            flops=4 * big + small, moved=2**22,
        )
        return outs[1], outs

    final_scratch = [pltpu.VMEM((1, tok, half * DH), BF16)] * 2
    final_scratch.append(pltpu.SemaphoreType.DMA((half, 2)))

    def finish(later_a, total, paired):
        grad_query, key_part, value_part = paired
        gain_here = total[half * DH :]
        gain_there = swap(gain_here, "dp", 1)
        first = call(
            final_first_kernel,
            [whole, whole],
            held_values, spiked, spikes, key_part, value_part, later_a,
            hbm_outs=(0, 1),
            scratch=final_scratch,
            flops=small, moved=2**21,
        )
        return first[0], (*paired, gain_here, gain_there, *first)

    _, later_b, (grad_query, key_part, value_part, gain_here, gain_there, *first) = scan_pair(
        local_a, local_b, "ctx", True, pair, finish
    )
    total_tokens = tok * lax.axis_size("ctx") * lax.axis_size("dp")
    grad_key, grad_value, grad_gain = call(
        functools.partial(final_last_kernel, 1.0 / math.sqrt(total_tokens)),
        [whole, whole, shape((1, width_dev), F32)],
        held_values, spiked, spikes, key_part, value_part, later_b, gain_here, gain_there, *first,
        hbm=(8, 9),
        hbm_outs=(0, 1),
        aliases={8: 0, 9: 1},
        scratch=final_scratch,
        flops=small, moved=2**21,
    )
    return grad_query, grad_key, grad_value, grad_gain.reshape(width_dev)


def solution(mesh):
    spec = P("dp", "ctx", "head")
    return jax.shard_map(
        per_device,
        mesh=mesh,
        in_specs=(spec, spec, spec, spec, P("head"), spec),
        out_specs=(spec, spec, spec, P("head")),
        check_vma=False,
    )
```

time: 55.7 us -> 46.8 us (0.84)
  starting transfers between devices: 20.5 us -> 15.4 us
  local copies, waits for them, and re-layouts: 3.62 us -> 0.01 us
  Pallas kernels: 4.74 us -> 7.65 us
  waiting for transfers between devices: 25 us -> 22.7 us
  other arithmetic: 0.73 us -> 0.15 us
    ppermute x13 -> x11, starting transfers between devices: 20.5 us -> 15.4 us  [swap(): return lax.ppermute(array, axis, [(i, i ^ stride) for i in range(size)])]
    unnamed x16 -> x2, local copies, waits for them, and re-layouts: 3.62 us -> 0.01 us
    pallas_call x6 -> x7, Pallas kernels: 4.74 us -> 7.65 us  [call(): pl.pallas_call(body, out_shape=outs, in_specs=[HBM if k in hbm else VMEM...]
    ppermute x13 -> x11, waiting for transfers between devices: 25 us -> 22.7 us  [swap(): return lax.ppermute(array, axis, [(i, i ^ stride) for i in range(size)])]
    div x1 -> x0, other arithmetic: 0.58 us -> none  [per_device(): grad_gain = gain_part.reshape(width_dev) / math.sqrt(total_tokens)]
  transfers between devices with their start and end apart: 13 -> 11, of which waited for: 10 -> 10; matrix products, arithmetic and copies ran while one was open for 1% -> 0% of each run, Pallas kernels for 5% -> 8%
where the time goes in v2:
time: 46.8 us; the launch traced here: 46.7 us
  waiting for transfers between devices  22.7 us (49%)
  starting transfers between devices  15.4 us (33%)
  Pallas kernels  7.65 us (16%)
  between operations  0.73 us (2%)
    ppermute x11, waiting for transfers between devices, swap(): return lax.ppermute(array, axis, [(i, i ^ stride) for i in range(size)])  22.7 us
    ppermute x11, starting transfers between devices, swap(): return lax.ppermute(array, axis, [(i, i ^ stride) for i in range(size)])  15.4 us
    pallas_call x7, Pallas kernels, call(): pl.pallas_call(body, out_shape=outs, in_specs=[HBM if k in hbm else VMEM...  7.65 us
  transfers between devices with their start and end apart: 11, of which 10 were waited for; matrix products, arithmetic and copies ran while one was open for 0% of the time, Pallas kernels for 8%

profile of v2, /device:TPU:0, one launch (start us, length us, event | category | flops | bytes accessed | tf_op | source)
XLA Modules:
  0.0 46.7 jit_solution(7520353468952367020)
XLA Ops:
  0.6 1.5 %shard_map.93 = (bf16[1,256,512]{2,1,0:T(8,128)(2,1)S(1)}, bf16[256,512]{1,0:T(8,128)(2,1)S(1)}, bf16[1,256,512]{2,1,0:T(8,128)(2,1)S(1)}, bf16[4,256,256]{2,1,0...) custom-call(bf16[1,256,512]{2,1,0:T(8,128)(2,1)} %queries.1, ...), custom_call_target="tpu_custom_call" | custom-call | flops 33554432 | bytes 1048576 | tf_op jit(solution)/shard_map/pallas_call | solution.py:40
  2.2 3.1 %collective-permute-start = (f32[256,128]{1,0:T(8,128)S(1)}, f32[256,128]{1,0:T(8,128)S(1)}, u32[]{:S(2)}, u32[]{:S(2)}) collective-permute-start(f32[256,128]{1,0:T(8,128)S(1)} %get-tuple-element.37), channel_id=1, source_target_pairs={{0,4},{4,0},{8,12},{12,8},{1,5},{5,1},{9,13},{13,9},{2,6},{6,2},{1... | collective-permute-start | bytes 393224 | tf_op jit(solution)/shard_map/ppermute | solution.py:218
  5.2 2.6 %collective-permute-start.1 = (f32[256,128]{1,0:T(8,128)S(1)}, f32[256,128]{1,0:T(8,128)S(1)}, u32[]{:S(2)}, u32[]{:S(2)}) collective-permute-start(f32[256,128]{1,0:T(8,128)S(1)} %get-tuple-element.42), channel_id=1, source_target_pairs={{0,8},{4,12},{8,0},{12,4},{1,9},{5,13},{9,1},{13,5},{2,10},{6,14},... | collective-permute-start | bytes 393224 | tf_op jit(solution)/shard_map/ppermute | solution.py:218
  7.8 4.1 %collective-permute-done = f32[256,128]{1,0:T(8,128)S(1)} collective-permute-done((f32[256,128]{1,0:T(8,128)S(1)}, f32[256,128]{1,0:T(8,128)S(1)}, u32[]{:S(2)}, u32[]{:S(2)}) %collective-permute-start) | collective-permute-done | bytes 131104 | tf_op jit(solution)/shard_map/ppermute | solution.py:218
  12.0 0.9 %collective-permute-start.3 = (f32[256,128]{1,0:T(8,128)S(1)}, f32[256,128]{1,0:T(8,128)S(1)}, u32[]{:S(2)}, u32[]{:S(2)}) collective-permute-start(f32[256,128]{1,0:T(8,128)S(1)} %add.33.after), channel_id=1, source_target_pairs={{0,8},{4,12},{8,0},{12,4},{1,9},{5,13},{9,1},{13,5},{2,10},{6,14},... | collective-permute-start | bytes 393224 | tf_op jit(solution)/shard_map/ppermute | solution.py:218
  12.9 1.0 %shard_map.94 = (bf16[4,256,256]{2,1,0:T(8,128)(2,1)S(1)}, f32[256,512]{1,0:T(8,128)S(1)}, f32[256,512]{1,0:T(8,128)S(1)}, bf16[1,256,512]{2,1,0:T(8,128)(2,1)S(1)}) custom-call(bf16[1,256,512]{2,1,0:T(8,128)(2,1)S(1)} %get-tuple-element.34.queries, bf16[256,512]{1,0:T(8,128)(2,1)S(1)} %get-tuple-element.35.spiked, ...), custom_call_target="tpu_custom_call", output_to_operand_aliasing={{0}: (6, {}), {1}: (7, {})} | custom-call | flops 134217728 | bytes 2097152 | tf_op jit(solution)/shard_map/pallas_call | solution.py:40
  13.9 0.7 %collective-permute-done.1 = f32[256,128]{1,0:T(8,128)S(1)} collective-permute-done((f32[256,128]{1,0:T(8,128)S(1)}, f32[256,128]{1,0:T(8,128)S(1)}, u32[]{:S(2)}, u32[]{:S(2)}) %collective-permute-start.1) | collective-permute-done | bytes 131104 | tf_op jit(solution)/shard_map/ppermute | solution.py:218
  14.6 1.9 %collective-permute-start.2 = (f32[256,128]{1,0:T(8,128)S(1)}, f32[256,128]{1,0:T(8,128)S(1)}, u32[]{:S(2)}, u32[]{:S(2)}) collective-permute-start(f32[256,128]{1,0:T(8,128)S(1)} %select_add_fusion.3), channel_id=1, source_target_pairs={{0,4},{4,0},{8,12},{12,8},{1,5},{5,1},{9,13},{13,9},{2,6},{6,2},{1... | collective-permute-start | bytes 393224 | tf_op jit(solution)/shard_map/ppermute | solution.py:218
  16.5 4.5 %collective-permute-done.3 = f32[256,128]{1,0:T(8,128)S(1)} collective-permute-done((f32[256,128]{1,0:T(8,128)S(1)}, f32[256,128]{1,0:T(8,128)S(1)}, u32[]{:S(2)}, u32[]{:S(2)}) %collective-permute-start.3) | collective-permute-done | bytes 131104 | tf_op jit(solution)/shard_map/ppermute | solution.py:218
  21.0 1.2 %collective-permute-done.2 = f32[256,128]{1,0:T(8,128)S(1)} collective-permute-done((f32[256,128]{1,0:T(8,128)S(1)}, f32[256,128]{1,0:T(8,128)S(1)}, u32[]{:S(2)}, u32[]{:S(2)}) %collective-permute-start.2) | collective-permute-done | bytes 131104 | tf_op jit(solution)/shard_map/ppermute | solution.py:218
  22.2 0.4 shard_map.95
  22.6 1.5 %collective-permute-start.4 = (f32[2,256]{1,0:T(2,128)S(1)}, f32[2,256]{1,0:T(2,128)S(1)}, u32[]{:S(2)}, u32[]{:S(2)}) collective-permute-start(f32[2,256]{1,0:T(2,128)S(1)} %get-tuple-element.48), channel_id=1, source_target_pairs={{0,1},{1,0},{2,3},{3,2},{4,5},{5,4},{6,7},{7,6},{8,9},{9,8},{10,11... | collective-permute-start | bytes 6152 | tf_op jit(solution)/shard_map/ppermute | solution.py:218
  24.1 2.2 %collective-permute-done.4 = f32[2,256]{1,0:T(2,128)S(1)} collective-permute-done((f32[2,256]{1,0:T(2,128)S(1)}, f32[2,256]{1,0:T(2,128)S(1)}, u32[]{:S(2)}, u32[]{:S(2)}) %collective-permute-start.4) | collective-permute-done | bytes 2080 | tf_op jit(solution)/shard_map/ppermute | solution.py:218
  26.2 1.4 %collective-permute-start.5 = (f32[2,256]{1,0:T(2,128)S(1)}, f32[2,256]{1,0:T(2,128)S(1)}, u32[]{:S(2)}, u32[]{:S(2)}) collective-permute-start(f32[2,256]{1,0:T(2,128)S(1)} %add.37), channel_id=1, source_target_pairs={{0,2},{1,3},{2,0},{3,1},{4,6},{5,7},{6,4},{7,5},{8,10},{9,11},{10,... | collective-permute-start | bytes 6152 | tf_op jit(solution)/shard_map/ppermute | solution.py:218
  27.7 2.1 %collective-permute-done.5 = f32[2,256]{1,0:T(2,128)S(1)} collective-permute-done((f32[2,256]{1,0:T(2,128)S(1)}, f32[2,256]{1,0:T(2,128)S(1)}, u32[]{:S(2)}, u32[]{:S(2)}) %collective-permute-start.5) | collective-permute-done | bytes 2080 | tf_op jit(solution)/shard_map/ppermute | solution.py:218
  29.8 0.4 shard_map.96
  30.2 0.1 collective-permute-start.6
  30.3 3.1 %collective-permute-start.7 = (f32[256,128]{1,0:T(8,128)S(1)}, f32[256,128]{1,0:T(8,128)S(1)}, u32[]{:S(2)}, u32[]{:S(2)}) collective-permute-start(f32[256,128]{1,0:T(8,128)S(1)} %get-tuple-element.56), channel_id=1, source_target_pairs={{0,8},{4,12},{8,0},{12,4},{1,9},{5,13},{9,1},{13,5},{2,10},{6,14},... | collective-permute-start | bytes 393224 | tf_op jit(solution)/shard_map/ppermute | solution.py:218
  33.4 3.5 %collective-permute-done.6 = f32[264,128]{1,0:T(8,128)S(1)} collective-permute-done((f32[264,128]{1,0:T(8,128)S(1)}, f32[264,128]{1,0:T(8,128)S(1)}, u32[]{:S(2)}, u32[]{:S(2)}) %collective-permute-start.6) | collective-permute-done | bytes 135200 | tf_op jit(solution)/shard_map/ppermute | solution.py:218
  37.0 0.1 collective-permute-start.9
  37.0 1.9 %shard_map.97 = (bf16[1,256,512]{2,1,0:T(8,128)(2,1)}, f32[256,512]{1,0:T(8,128)S(1)}, f32[256,512]{1,0:T(8,128)S(1)}) custom-call(bf16[1,256,512]{2,1,0:T(8,128)(2,1)S(1)} %get-tuple-element.34.queries, bf16[256,512]{1,0:T(8,128)(2,1)S(1)} %get-tuple-element.35.spiked, bf16[1,256,512]{2,1,0:T(8,128)(2,1)S(1)} %get-tuple-element.36.values, ...), custom_call_target="tpu_custom_call" | custom-call | flops 301989888 | bytes 4194304 | tf_op jit(solution)/shard_map/pallas_call | solution.py:40
  39.0 0.0 copy-start
  39.0 1.1 %collective-permute-done.7 = f32[256,128]{1,0:T(8,128)S(1)} collective-permute-done((f32[256,128]{1,0:T(8,128)S(1)}, f32[256,128]{1,0:T(8,128)S(1)}, u32[]{:S(2)}, u32[]{:S(2)}) %collective-permute-start.7) | collective-permute-done | bytes 131104 | tf_op jit(solution)/shard_map/ppermute | solution.py:218
  40.1 0.8 %collective-permute-start.8 = (f32[256,128]{1,0:T(8,128)S(1)}, f32[256,128]{1,0:T(8,128)S(1)}, u32[]{:S(2)}, u32[]{:S(2)}) collective-permute-start(f32[256,128]{1,0:T(8,128)S(1)} %select_add_fusion.1), channel_id=1, source_target_pairs={{0,4},{4,0},{8,12},{12,8},{1,5},{5,1},{9,13},{13,9},{2,6},{6,2},{1... | collective-permute-start | bytes 393224 | tf_op jit(solution)/shard_map/ppermute | solution.py:218
  40.9 2.5 %collective-permute-done.9 = f32[264,128]{1,0:T(8,128)S(1)} collective-permute-done((f32[264,128]{1,0:T(8,128)S(1)}, f32[264,128]{1,0:T(8,128)S(1)}, u32[]{:S(2)}, u32[]{:S(2)}) %collective-permute-start.9) | collective-permute-done | bytes 135200 | tf_op jit(solution)/shard_map/ppermute | solution.py:218
  43.4 0.0 collective-permute-start.10
  43.4 0.0 copy-done
  43.4 0.9 %shard_map.98 = (bf16[1,256,512]{2,1,0:T(8,128)(2,1)}, bf16[1,256,512]{2,1,0:T(8,128)(2,1)}) custom-call(bf16[1,256,512]{2,1,0:T(8,128)(2,1)S(1)} %get-tuple-element.36.values, bf16[256,512]{1,0:T(8,128)(2,1)S(1)} %get-tuple-element.35.spiked, s32[1,256,512]{2,1,0:T(8,128)S(1)} %copy-done, f32[256,512]{1,0:T(8,128)S(1)} %get-tuple-element.54.key_part, ...), custom_call_target="tpu_custom_call" | custom-call | flops 33554432 | bytes 2097152 | tf_op jit(solution)/shard_map/pallas_call | solution.py:40
  44.3 0.8 %collective-permute-done.8 = f32[256,128]{1,0:T(8,128)S(1)} collective-permute-done((f32[256,128]{1,0:T(8,128)S(1)}, f32[256,128]{1,0:T(8,128)S(1)}, u32[]{:S(2)}, u32[]{:S(2)}) %collective-permute-start.8) | collective-permute-done | bytes 131104 | tf_op jit(solution)/shard_map/ppermute | solution.py:218
  45.2 0.0 collective-permute-done.10.gain_there
  45.2 1.5 %shard_map.99 = (bf16[1,256,512]{2,1,0:T(8,128)(2,1)}, bf16[1,256,512]{2,1,0:T(8,128)(2,1)}, f32[1,512]{1,0:T(1,128)}) custom-call(bf16[1,256,512]{2,1,0:T(8,128)(2,1)S(1)} %get-tuple-element.36.values, bf16[256,512]{1,0:T(8,128)(2,1)S(1)} %get-tuple-element.35.spiked, s32[1,256,512]{2,1,0:T(8,128)S(1)} %copy-done, ...), custom_call_target="tpu_custom_call", output_to_operand_aliasing={{0}: (8, {}), {1}: (9, {})} | custom-call | flops 33554432 | bytes 2097152 | tf_op jit(solution)/shard_map/pallas_call | solution.py:40
  (11 shorter events, 0.2 us)
Async XLA Ops:
  2.2 9.8 %collective-permute-start = (f32[256,128]{1,0:T(8,128)S(1)}, f32[256,128]{1,0:T(8,128)S(1)}, u32[]{:S(2)}, u32[]{:S(2)}) collective-permute-start(f32[256,128]{1,0:T(8,128)S(1)} %get-tuple-element.37), channel_id=1, source_target_pairs={{0,4},{4,0},{8,12},{12,8},{1,5},{5,1},{9,13},{13,9},{2,6},{6,2},{1... | collective-permute-start | bytes 393224 | tf_op jit(solution)/shard_map/ppermute | solution.py:218
  5.2 9.4 %collective-permute-start.1 = (f32[256,128]{1,0:T(8,128)S(1)}, f32[256,128]{1,0:T(8,128)S(1)}, u32[]{:S(2)}, u32[]{:S(2)}) collective-permute-start(f32[256,128]{1,0:T(8,128)S(1)} %get-tuple-element.42), channel_id=1, source_target_pairs={{0,8},{4,12},{8,0},{12,4},{1,9},{5,13},{9,1},{13,5},{2,10},{6,14},... | collective-permute-start | bytes 393224 | tf_op jit(solution)/shard_map/ppermute | solution.py:218
  12.0 9.0 %collective-permute-start.3 = (f32[256,128]{1,0:T(8,128)S(1)}, f32[256,128]{1,0:T(8,128)S(1)}, u32[]{:S(2)}, u32[]{:S(2)}) collective-permute-start(f32[256,128]{1,0:T(8,128)S(1)} %add.33.after), channel_id=1, source_target_pairs={{0,8},{4,12},{8,0},{12,4},{1,9},{5,13},{9,1},{13,5},{2,10},{6,14},... | collective-permute-start | bytes 393224 | tf_op jit(solution)/shard_map/ppermute | solution.py:218
  14.6 7.5 %collective-permute-start.2 = (f32[256,128]{1,0:T(8,128)S(1)}, f32[256,128]{1,0:T(8,128)S(1)}, u32[]{:S(2)}, u32[]{:S(2)}) collective-permute-start(f32[256,128]{1,0:T(8,128)S(1)} %select_add_fusion.3), channel_id=1, source_target_pairs={{0,4},{4,0},{8,12},{12,8},{1,5},{5,1},{9,13},{13,9},{2,6},{6,2},{1... | collective-permute-start | bytes 393224 | tf_op jit(solution)/shard_map/ppermute | solution.py:218
  22.6 3.6 %collective-permute-start.4 = (f32[2,256]{1,0:T(2,128)S(1)}, f32[2,256]{1,0:T(2,128)S(1)}, u32[]{:S(2)}, u32[]{:S(2)}) collective-permute-start(f32[2,256]{1,0:T(2,128)S(1)} %get-tuple-element.48), channel_id=1, source_target_pairs={{0,1},{1,0},{2,3},{3,2},{4,5},{5,4},{6,7},{7,6},{8,9},{9,8},{10,11... | collective-permute-start | bytes 6152 | tf_op jit(solution)/shard_map/ppermute | solution.py:218
  26.2 3.6 %collective-permute-start.5 = (f32[2,256]{1,0:T(2,128)S(1)}, f32[2,256]{1,0:T(2,128)S(1)}, u32[]{:S(2)}, u32[]{:S(2)}) collective-permute-start(f32[2,256]{1,0:T(2,128)S(1)} %add.37), channel_id=1, source_target_pairs={{0,2},{1,3},{2,0},{3,1},{4,6},{5,7},{6,4},{7,5},{8,10},{9,11},{10,... | collective-permute-start | bytes 6152 | tf_op jit(solution)/shard_map/ppermute | solution.py:218
  30.2 6.7 %collective-permute-start.6 = (f32[264,128]{1,0:T(8,128)S(1)}, f32[264,128]{1,0:T(8,128)S(1)}, u32[]{:S(2)}, u32[]{:S(2)}) collective-permute-start(f32[264,128]{1,0:T(8,128)S(1)} %get-tuple-element.52), channel_id=1, source_target_pairs={{0,4},{4,0},{8,12},{12,8},{1,5},{5,1},{9,13},{13,9},{2,6},{6,2},{1... | collective-permute-start | bytes 405512 | tf_op jit(solution)/shard_map/ppermute | solution.py:218
  30.3 9.8 %collective-permute-start.7 = (f32[256,128]{1,0:T(8,128)S(1)}, f32[256,128]{1,0:T(8,128)S(1)}, u32[]{:S(2)}, u32[]{:S(2)}) collective-permute-start(f32[256,128]{1,0:T(8,128)S(1)} %get-tuple-element.56), channel_id=1, source_target_pairs={{0,8},{4,12},{8,0},{12,4},{1,9},{5,13},{9,1},{13,5},{2,10},{6,14},... | collective-permute-start | bytes 393224 | tf_op jit(solution)/shard_map/ppermute | solution.py:218
  37.0 6.4 %collective-permute-start.9 = (f32[264,128]{1,0:T(8,128)S(1)}, f32[264,128]{1,0:T(8,128)S(1)}, u32[]{:S(2)}, u32[]{:S(2)}) collective-permute-start(f32[264,128]{1,0:T(8,128)S(1)} %add.39.after), channel_id=1, source_target_pairs={{0,8},{4,12},{8,0},{12,4},{1,9},{5,13},{9,1},{13,5},{2,10},{6,14},... | collective-permute-start | bytes 405512 | tf_op jit(solution)/shard_map/ppermute | solution.py:218
  39.0 4.4 %copy-start = (s32[1,256,512]{2,1,0:T(8,128)S(1)}, s32[1,256,512]{2,1,0:T(8,128)}, u32[]{:S(2)}) copy-start(s32[1,256,512]{2,1,0:T(8,128)} %spikes.5) | copy-start | bytes 1572868
  40.1 5.0 %collective-permute-start.8 = (f32[256,128]{1,0:T(8,128)S(1)}, f32[256,128]{1,0:T(8,128)S(1)}, u32[]{:S(2)}, u32[]{:S(2)}) collective-permute-start(f32[256,128]{1,0:T(8,128)S(1)} %select_add_fusion.1), channel_id=1, source_target_pairs={{0,4},{4,0},{8,12},{12,8},{1,5},{5,1},{9,13},{13,9},{2,6},{6,2},{1... | collective-permute-start | bytes 393224 | tf_op jit(solution)/shard_map/ppermute | solution.py:218
  43.4 1.8 %collective-permute-start.10 = (f32[8,128]{1,0:T(8,128)S(1)}, f32[8,128]{1,0:T(8,128)S(1)}, u32[]{:S(2)}, u32[]{:S(2)}) collective-permute-start(f32[8,128]{1,0:T(8,128)S(1)} %slice_add_fusion.gain_here), channel_id=1, source_target_pairs={{0,16},{16,0},{1,17},{17,1},{2,18},{18,2},{3,19},{19,3},{4,20},{20... | collective-permute-start | bytes 12296 | tf_op jit(solution)/shard_map/ppermute | solution.py:218

commit v3 on v2

v3 whole, which is shorter than its diff:
```python
import functools
import math

import jax
import jax.numpy as jnp
from jax import lax
from jax.experimental import pallas as pl
from jax.experimental.pallas import tpu as pltpu
from jax.sharding import PartitionSpec as P

DH = 128
HEADS = 16
EPS = 1e-06

F32 = jnp.float32
BF16 = jnp.bfloat16
VMEM = pl.BlockSpec(memory_space=pltpu.VMEM)
HBM = pl.BlockSpec(memory_space=pltpu.HBM)
GAIN_ROWS = 8


def dot(a, b, ca, cb):
    return lax.dot_general(a, b, (((ca,), (cb,)), ((), ())), preferred_element_type=F32)


def cols(h):
    return slice(h * DH, (h + 1) * DH)


def block_of(pieces, h):
    per = pieces[-1].shape[0] // DH
    return pieces[h // per], cols(h % per)


def call(body, outs, *args, hbm=(), scratch=(), flops=0, moved=0):
    args = [
        pltpu.with_memory_space_constraint(arg, pltpu.HBM) if k in hbm else arg
        for k, arg in enumerate(args)
    ]
    return pl.pallas_call(
        body,
        out_shape=outs,
        in_specs=[HBM if k in hbm else VMEM for k in range(len(args))],
        out_specs=[VMEM] * len(outs),
        scratch_shapes=scratch,
        cost_estimate=pl.CostEstimate(flops=flops, bytes_accessed=moved, transcendentals=0),
        compiler_params=pltpu.CompilerParams(vmem_limit_bytes=32 * 2**20),
    )(*args)


def causal_mask(tok):
    rows = lax.broadcasted_iota(jnp.int32, (tok, tok), 0)
    return rows >= lax.broadcasted_iota(jnp.int32, (tok, tok), 1)


def state_kernel(
    queries, keys, spikes, values, upstream, held_queries, held_values, upper, spiked, *rest
):
    *states, key_buf, spike_buf, sems = rest
    heads = spiked.shape[1] // DH
    pairs = (
        (keys, key_buf), (spikes, spike_buf), (values, held_values),
        (queries, held_queries), (upstream, upper),
    )
    copies = [pltpu.make_async_copy(src, dst, sems.at[k]) for k, (src, dst) in enumerate(pairs)]
    for copy in copies:
        copy.start()
    for copy in copies[:3]:
        copy.wait()
    for h in range(heads):
        block = key_buf[0, :, cols(h)] * spike_buf[0, :, cols(h)].astype(F32).astype(BF16)
        spiked[:, cols(h)] = block
        ref, rows = block_of(states, h)
        ref[rows, :] = dot(block, held_values[0, :, cols(h)], 0, 0)
    for copy in copies[3:]:
        copy.wait()


def scores_kernel(queries, spiked, values, scores, intra):
    heads, tok, _ = scores.shape
    causal = causal_mask(tok)
    for h in range(heads):
        raw = dot(queries[0, :, cols(h)], spiked[:, cols(h)], 1, 1)
        block = jnp.where(causal, raw, 0.0).astype(BF16)
        scores[h] = block
        intra[:, cols(h)] = dot(block, values[0, :, cols(h)], 1, 0)


def scale_kernel(upper, gain, after, scaled):
    del after
    scaled[...] = upper[0].astype(F32) * gain[...]


def attend_kernel(queries, intra, scaled, sum_a, sum_b, attended, prior, sums):
    heads = prior.shape[0]
    tok = intra.shape[0]
    square = jnp.zeros((tok, DH), F32)
    cross = jnp.zeros((tok, DH), F32)
    for h in range(heads):
        ref, rows = block_of((sum_a, sum_b), h)
        state = ref[rows, :].astype(BF16)
        prior[h] = state
        block = dot(queries[0, :, cols(h)], state, 1, 0) + intra[:, cols(h)]
        attended[:, cols(h)] = block
        square += block * block
        cross += scaled[:, cols(h)] * block
    sums[0:1, :] = jnp.sum(square.T, axis=0, keepdims=True)
    sums[1:2, :] = jnp.sum(cross.T, axis=0, keepdims=True)


def grad_kernel(width, queries, attended, scaled, upper, sums, grad, *locals_):
    tok = attended.shape[0]
    heads = attended.shape[1] // DH
    inv = lax.rsqrt(sums[0:1, :] / width + EPS)
    factor = inv * inv * inv * (sums[1:2, :] / width)
    inv = jnp.broadcast_to(inv, (DH, tok)).T
    factor = jnp.broadcast_to(factor, (DH, tok)).T
    gain_at = locals_[0].shape[0] - GAIN_ROWS
    locals_[0][gain_at:, :] = jnp.zeros((GAIN_ROWS, DH), F32)
    for h in range(heads):
        block = attended[:, cols(h)]
        result = (inv * scaled[:, cols(h)] - block * factor).astype(BF16)
        grad[:, cols(h)] = result
        ref, rows = block_of(locals_, h)
        ref[rows, :] = dot(queries[0, :, cols(h)], result, 0, 0)
        terms = upper[0, :, cols(h)].astype(F32) * block * inv
        locals_[0][gain_at + h : gain_at + h + 1, :] = jnp.sum(terms, axis=0, keepdims=True)


def pair_heads(
    first, to, queries, spiked, values, grad, prior, scores, grad_query, key_part, value_part
):
    tok = spiked.shape[0]
    causal = causal_mask(tok)
    for h in range(key_part.shape[1] // DH):
        at = cols(first + h)
        result = grad[:, at]
        raw = dot(result, values[0, :, at], 1, 1)
        pairs = jnp.where(causal, raw, 0.0).astype(BF16)
        query_part = dot(result, prior[first + h], 1, 1) + dot(pairs, spiked[:, at], 1, 0)
        grad_query[0, :, cols(to + h)] = query_part.astype(BF16)
        key_part[:, cols(h)] = dot(pairs, queries[0, :, at], 0, 0)
        value_part[:, cols(h)] = dot(scores[first + h], result, 0, 0)


def pairs_first_kernel(*refs):
    pair_heads(0, 0, *refs)


def pairs_last_kernel(
    queries, spiked, values, grad, prior, scores, query_half, after,
    grad_query, key_part, value_part,
):
    del after
    done = query_half.shape[2]
    grad_query[:, :, :done] = query_half[...]
    pair_heads(
        done // DH, done // DH, queries, spiked, values, grad, prior, scores,
        grad_query, key_part, value_part,
    )


def final_half(first, values, spiked, spikes, key_part, value_part, sums, outs, to):
    for h in range(sums.shape[0] // DH):
        at = cols(first + h)
        later = sums[cols(h), :].astype(BF16)
        inner = key_part[:, cols(h)] + dot(values[0, :, at], later, 1, 1)
        outs[0][0, :, cols(to + h)] = (inner * spikes[0, :, at].astype(F32)).astype(BF16)
        block = value_part[:, cols(h)] + dot(spiked[:, at], later, 1, 0)
        outs[1][0, :, cols(to + h)] = block.astype(BF16)


def final_first_kernel(
    values, spiked, spikes, key_part, value_part, sums, key_half, value_half
):
    outs = (key_half, value_half)
    final_half(0, values, spiked, spikes, key_part, value_part, sums, outs, 0)


def final_last_kernel(
    scale, values, spiked, spikes, key_part, value_part, sums, gain_here, gain_there,
    key_half, value_half, grad_key, grad_value, grad_gain,
):
    outs = (grad_key, grad_value)
    width = spiked.shape[1]
    done = key_half.shape[2]
    for out, half in zip(outs, (key_half, value_half)):
        out[:, :, :done] = half[...]
    final_half(
        done // DH, values, spiked, spikes, key_part, value_part, sums, outs, done // DH
    )
    for h in range(width // DH):
        grad_gain[:, cols(h)] = (gain_here[h : h + 1, :] + gain_there[h : h + 1, :]) * scale


def swap(array, axis, stride):
    size = lax.axis_size(axis)
    return lax.ppermute(array, axis, [(i, i ^ stride) for i in range(size)])


def gathered_sum(array, axis):
    got = [swap(array, axis, stride) for stride in range(lax.axis_size(axis) - 1, 0, -1)]
    total = array
    for k, other in enumerate(got):
        if k:
            other, total = lax.optimization_barrier((other, total))
        total = total + other
    return total


def strides(axis):
    size = lax.axis_size(axis)
    assert size & (size - 1) == 0
    return [1 << k for k in range(size.bit_length() - 1)]


def swap_by_core(array, axis, even, odd):
    size = lax.axis_size(axis)
    pairs = []
    for core in range(lax.axis_size("dp")):
        stride = odd if core % 2 else even
        pairs += [(core * size + i, core * size + (i ^ stride)) for i in range(size)]
    return lax.ppermute(array, ("dp", axis), pairs)


def scan_pair(lead, last, axis, reverse, by_core, between, finish=None):
    at = lax.axis_index(axis)
    lead_up = lax.axis_index("dp") % 2 == 0 if by_core else jnp.bool_(True)
    up_order = strides(axis)
    down_order = up_order[::-1]
    rounds = len(up_order)
    extra = lax.broadcasted_iota(jnp.int32, lead.shape, 0) >= last.shape[0]
    own = [lead, last]
    goes_up = [lead_up, jnp.logical_not(lead_up)]
    sent = [lead, last]
    total = [lead, last]
    sums = [None, None]
    result = None
    for k in range(rounds):
        up, down = up_order[k], down_order[k]
        got = [
            swap_by_core(sent[0], axis, up, down if by_core else up),
            swap_by_core(sent[1], axis, down, up if by_core else down),
        ]
        for p in range(2):
            stride = jnp.where(goes_up[p], up, down)
            after_partner = ((at & stride) == 0) if reverse else ((at & stride) != 0)
            total[p] = total[p] + got[p]
            if k == 0:
                sums[p] = jnp.where(after_partner, got[p], 0.0)
            else:
                keep = jnp.logical_or(after_partner, jnp.logical_not(goes_up[p]))
                sums[p] = sums[p] + jnp.where(keep, got[p], 0.0)
            if k < rounds - 1:
                next_down = down_order[k + 1]
                serves = ((at & next_down) != 0) if reverse else ((at & next_down) == 0)
                partial = sums[p] + jnp.where(serves, own[p], 0.0)
                whole = jnp.logical_or(goes_up[p], extra) if p == 0 else goes_up[p]
                sent[p] = jnp.where(whole, total[p], partial)
            if p == 0:
                token = sums[0]
                if k == 0:
                    token, result = between(sent[0])
                if k == rounds - 1 and finish is not None:
                    token, result = finish(sums[0], total[0], result)
                got[1], _ = lax.optimization_barrier((got[1], token))
    return sums[0], sums[1], result


def per_device(queries, keys, values, spikes, gain, upstream):
    tok = queries.shape[1]
    width_dev = queries.shape[2]
    heads = width_dev // DH
    half = heads // 2
    width = HEADS * DH
    gain_row = gain.reshape(1, width_dev)
    shape = jax.ShapeDtypeStruct
    flat = (tok, width_dev)
    piece = shape((half * DH, DH), F32)
    longer = shape((half * DH + GAIN_ROWS, DH), F32)
    whole = shape((1, tok, width_dev), BF16)
    small = 2 * heads * tok * DH * DH
    big = 2 * heads * tok * tok * DH

    held_queries, held_values, upper, spiked, state_a, state_b = call(
        state_kernel,
        [whole, whole, whole, shape(flat, BF16), piece, piece],
        queries, keys, spikes, values, upstream,
        hbm=(0, 1, 2, 3, 4),
        scratch=[
            pltpu.VMEM((1, *flat), BF16),
            pltpu.VMEM((1, *flat), jnp.int32),
            pltpu.SemaphoreType.DMA((5,)),
        ],
        flops=small, moved=2**20,
    )
    scores, intra = call(
        scores_kernel,
        [shape((heads, tok, tok), BF16), shape(flat, F32)],
        held_queries, spiked, held_values,
        flops=2 * big, moved=2**21,
    )

    def scale(total):
        scaled = call(scale_kernel, [shape(flat, F32)], upper, gain_row, total, moved=2**20)[0]
        return scaled, scaled

    prior_a, prior_b, scaled = scan_pair(state_a, state_b, "ctx", False, True, scale)
    attended, prior, sums = call(
        attend_kernel,
        [shape(flat, F32), shape((heads, DH, DH), BF16), shape((2, tok), F32)],
        held_queries, intra, scaled, prior_a, prior_b,
        flops=small, moved=2**21,
    )
    sums = gathered_sum(sums, "head")
    grad, local_a, local_b = call(
        functools.partial(grad_kernel, width),
        [shape(flat, BF16), longer, piece],
        held_queries, attended, scaled, upper, sums,
        flops=small, moved=2**21,
    )

    half_outs = [shape((1, tok, half * DH), BF16)] + [shape((tok, half * DH), F32)] * 2
    pair_args = (held_queries, spiked, held_values, grad, prior, scores)
    query_half, *first_parts = call(
        pairs_first_kernel, half_outs, *pair_args, flops=2 * big, moved=2**21
    )

    def pair(total):
        outs = call(
            pairs_last_kernel,
            [whole, *half_outs[1:]],
            *pair_args, query_half, total,
            flops=2 * big, moved=2**21,
        )
        return outs[1], outs

    def finish(later_a, total, paired):
        gain_here = total[half * DH :]
        gain_there = swap(gain_here, "dp", 1)
        first = call(
            final_first_kernel,
            [shape((1, tok, half * DH), BF16)] * 2,
            held_values, spiked, spikes, *first_parts, later_a,
            flops=small, moved=2**21,
        )
        token = (first[0], gain_there)
        return token, (*paired, gain_here, gain_there, *first)

    _, later_b, (grad_query, key_part, value_part, gain_here, gain_there, *first) = scan_pair(
        local_a, local_b, "ctx", True, False, pair, finish
    )
    total_tokens = tok * lax.axis_size("ctx") * lax.axis_size("dp")
    grad_key, grad_value, grad_gain = call(
        functools.partial(final_last_kernel, 1.0 / math.sqrt(total_tokens)),
        [whole, whole, shape((1, width_dev), F32)],
        held_values, spiked, spikes, key_part, value_part, later_b, gain_here, gain_there, *first,
        flops=small, moved=2**21,
    )
    return grad_query, grad_key, grad_value, grad_gain.reshape(width_dev)


def solution(mesh):
    spec = P("dp", "ctx", "head")
    return jax.shard_map(
        per_device,
        mesh=mesh,
        in_specs=(spec, spec, spec, spec, P("head"), spec),
        out_specs=(spec, spec, spec, P("head")),
        check_vma=False,
    )
```

time: 46.8 us -> 45.2 us (0.966)
  waiting for transfers between devices: 22.7 us -> 20.8 us
  starting transfers between devices: 15.4 us -> 16.9 us
  Pallas kernels: 7.65 us -> 6.34 us
    ppermute x11 -> x4, waiting for transfers between devices: 22.7 us -> 3.21 us  [swap(): return lax.ppermute(array, axis, [(i, i ^ stride) for i in range(size)])]
    ppermute x0 -> x8, waiting for transfers between devices: none -> 17.6 us  [swap_by_core(): return lax.ppermute(array, ('dp', axis), pairs)]
    ppermute x0 -> x8, starting transfers between devices: none -> 13.4 us  [swap_by_core(): return lax.ppermute(array, ('dp', axis), pairs)]
    ppermute x11 -> x4, starting transfers between devices: 15.4 us -> 3.55 us  [swap(): return lax.ppermute(array, axis, [(i, i ^ stride) for i in range(size)])]
    pallas_call x7 -> x9, Pallas kernels: 7.65 us -> 6.34 us  [call(): pl.pallas_call(body, out_shape=outs, in_specs=[HBM if k in hbm else VMEM...]
  transfers between devices with their start and end apart: 11 -> 12, of which waited for: 10 -> 9; matrix products, arithmetic and copies ran while one was open for 0% -> 0% of each run, Pallas kernels for 8% -> 7%
where the time goes in v3:
time: 45.2 us; the launch traced here: 45.1 us
  waiting for transfers between devices  20.8 us (46%)
  starting transfers between devices  16.9 us (37%)
  Pallas kernels  6.34 us (14%)
  between operations  0.78 us (2%)
    ppermute x8, waiting for transfers between devices, swap_by_core(): return lax.ppermute(array, ('dp', axis), pairs)  17.6 us
    ppermute x8, starting transfers between devices, swap_by_core(): return lax.ppermute(array, ('dp', axis), pairs)  13.4 us
    pallas_call x9, Pallas kernels, call(): pl.pallas_call(body, out_shape=outs, in_specs=[HBM if k in hbm else VMEM...  6.34 us
    ppermute x4, starting transfers between devices, swap(): return lax.ppermute(array, axis, [(i, i ^ stride) for i in range(size)])  3.55 us
    ppermute x4, waiting for transfers between devices, swap(): return lax.ppermute(array, axis, [(i, i ^ stride) for i in range(size)])  3.21 us
  transfers between devices with their start and end apart: 12, of which 9 were waited for; matrix products, arithmetic and copies ran while one was open for 0% of the time, Pallas kernels for 7%

profile of v3, /device:TPU:0, one launch (start us, length us, event | category | flops | bytes accessed | tf_op | source)
XLA Modules:
  0.0 45.1 jit_solution(12561441804022540567)
XLA Ops:
  0.6 1.5 %shard_map.93 = (bf16[1,256,512]{2,1,0:T(8,128)(2,1)S(1)}, bf16[1,256,512]{2,1,0:T(8,128)(2,1)S(1)}, bf16[1,256,512]{2,1,0:T(8,128)(2,1)S(1)}, bf16[256,512]{1,0...) custom-call(bf16[1,256,512]{2,1,0:T(8,128)(2,1)} %queries.1, bf16[1,256,512]{2,1,0:T(8,128)(2,1)} %keys.1, ...), custom_call_target="tpu_custom_call" | custom-call | flops 33554432 | bytes 1048576 | tf_op jit(solution)/shard_map/pallas_call | solution.py:40
  2.2 3.1 %collective-permute-start = (f32[256,128]{1,0:T(8,128)S(1)}, f32[256,128]{1,0:T(8,128)S(1)}, u32[]{:S(2)}, u32[]{:S(2)}) collective-permute-start(f32[256,128]{1,0:T(8,128)S(1)} %get-tuple-element.42), channel_id=1, source_target_pairs={{0,4},{4,0},{8,12},{12,8},{16,24},{20,28},{24,16},{28,20},{1,5},{5... | collective-permute-start | bytes 393224 | tf_op jit(solution)/shard_map/ppermute | solution.py:223
  5.2 2.6 %collective-permute-start.2 = (f32[256,128]{1,0:T(8,128)S(1)}, f32[256,128]{1,0:T(8,128)S(1)}, u32[]{:S(2)}, u32[]{:S(2)}) collective-permute-start(f32[256,128]{1,0:T(8,128)S(1)} %get-tuple-element.43), channel_id=1, source_target_pairs={{0,8},{4,12},{8,0},{12,4},{16,20},{20,16},{24,28},{28,24},{1,9},{5... | collective-permute-start | bytes 393224 | tf_op jit(solution)/shard_map/ppermute | solution.py:223
  7.8 0.7 %shard_map.94 = (bf16[4,256,256]{2,1,0:T(8,128)(2,1)S(1)}, f32[256,512]{1,0:T(8,128)S(1)}) custom-call(bf16[1,256,512]{2,1,0:T(8,128)(2,1)S(1)} %get-tuple-element.37.queries.refs_0_, bf16[256,512]{1,0:T(8,128)(2,1)S(1)} %get-tuple-element.38.spiked.refs_1_, bf16[1,256,512]{2,1,0:T(8,128)(2,1)S(1)} %get-tuple-element.39.values.refs_2_), custom_call_target="tpu_custom_call" | custom-call | flops 134217728 | bytes 2097152 | tf_op jit(solution)/shard_map/pallas_call | solution.py:40
  8.5 3.3 %collective-permute-done = f32[256,128]{1,0:T(8,128)S(1)} collective-permute-done((f32[256,128]{1,0:T(8,128)S(1)}, f32[256,128]{1,0:T(8,128)S(1)}, u32[]{:S(2)}, u32[]{:S(2)}) %collective-permute-start) | collective-permute-done | bytes 131104 | tf_op jit(solution)/shard_map/ppermute | solution.py:223
  11.8 0.1 add_select_fusion.1.after
  11.9 0.0 copy-start.1
  12.0 1.0 %collective-permute-start.1 = (f32[256,128]{1,0:T(8,128)S(1)}, f32[256,128]{1,0:T(8,128)S(1)}, u32[]{:S(2)}, u32[]{:S(2)}) collective-permute-start(f32[256,128]{1,0:T(8,128)S(1)} %add_select_fusion.1.after), channel_id=1, source_target_pairs={{0,8},{4,12},{8,0},{12,4},{16,20},{20,16},{24,28},{28,24},{1,9},{5... | collective-permute-start | bytes 393224 | tf_op jit(solution)/shard_map/ppermute | solution.py:223
  13.0 0.0 collective-permute-done.2
  13.0 2.7 %collective-permute-start.3 = (f32[256,128]{1,0:T(8,128)S(1)}, f32[256,128]{1,0:T(8,128)S(1)}, u32[]{:S(2)}, u32[]{:S(2)}) collective-permute-start(f32[256,128]{1,0:T(8,128)S(1)} %add_select_fusion), channel_id=1, source_target_pairs={{0,4},{4,0},{8,12},{12,8},{16,24},{20,28},{24,16},{28,20},{1,5},{5... | collective-permute-start | bytes 393224 | tf_op jit(solution)/shard_map/ppermute | solution.py:223
  15.7 5.8 %collective-permute-done.1 = f32[256,128]{1,0:T(8,128)S(1)} collective-permute-done((f32[256,128]{1,0:T(8,128)S(1)}, f32[256,128]{1,0:T(8,128)S(1)}, u32[]{:S(2)}, u32[]{:S(2)}) %collective-permute-start.1) | collective-permute-done | bytes 131104 | tf_op jit(solution)/shard_map/ppermute | solution.py:223
  21.5 0.0 collective-permute-done.3
  21.5 0.4 shard_map.96
  21.9 2.7 %collective-permute-start.6 = (f32[2,256]{1,0:T(2,128)S(1)}, f32[2,256]{1,0:T(2,128)S(1)}, u32[]{:S(2)}, u32[]{:S(2)}) collective-permute-start(f32[2,256]{1,0:T(2,128)S(1)} %get-tuple-element.47), channel_id=1, source_target_pairs={{0,3},{1,2},{2,1},{3,0},{4,7},{5,6},{6,5},{7,4},{8,11},{9,10},{10,... | collective-permute-start | bytes 6152 | tf_op jit(solution)/shard_map/ppermute | solution.py:198
  24.6 0.5 %collective-permute-start.5 = (f32[2,256]{1,0:T(2,128)S(1)}, f32[2,256]{1,0:T(2,128)S(1)}, u32[]{:S(2)}, u32[]{:S(2)}) collective-permute-start(f32[2,256]{1,0:T(2,128)S(1)} %get-tuple-element.47), channel_id=1, source_target_pairs={{0,2},{1,3},{2,0},{3,1},{4,6},{5,7},{6,4},{7,5},{8,10},{9,11},{10,... | collective-permute-start | bytes 6152 | tf_op jit(solution)/shard_map/ppermute | solution.py:198
  25.1 0.4 collective-permute-start.4
  25.4 1.0 %collective-permute-done.6 = f32[2,256]{1,0:T(2,128)S(1)} collective-permute-done((f32[2,256]{1,0:T(2,128)S(1)}, f32[2,256]{1,0:T(2,128)S(1)}, u32[]{:S(2)}, u32[]{:S(2)}) %collective-permute-start.6) | collective-permute-done | bytes 2080 | tf_op jit(solution)/shard_map/ppermute | solution.py:198
  26.4 1.7 %collective-permute-done.5 = f32[2,256]{1,0:T(2,128)S(1)} collective-permute-done((f32[2,256]{1,0:T(2,128)S(1)}, f32[2,256]{1,0:T(2,128)S(1)}, u32[]{:S(2)}, u32[]{:S(2)}) %collective-permute-start.5) | collective-permute-done | bytes 2080 | tf_op jit(solution)/shard_map/ppermute | solution.py:198
  28.2 0.5 %collective-permute-done.4 = f32[2,256]{1,0:T(2,128)S(1)} collective-permute-done((f32[2,256]{1,0:T(2,128)S(1)}, f32[2,256]{1,0:T(2,128)S(1)}, u32[]{:S(2)}, u32[]{:S(2)}) %collective-permute-start.4) | collective-permute-done | bytes 2080 | tf_op jit(solution)/shard_map/ppermute | solution.py:198
  28.7 0.4 shard_map.97
  29.1 0.1 collective-permute-start.7
  29.2 2.8 %collective-permute-start.8 = (f32[256,128]{1,0:T(8,128)S(1)}, f32[256,128]{1,0:T(8,128)S(1)}, u32[]{:S(2)}, u32[]{:S(2)}) collective-permute-start(f32[256,128]{1,0:T(8,128)S(1)} %get-tuple-element.60), channel_id=1, source_target_pairs={{0,8},{4,12},{8,0},{12,4},{16,24},{20,28},{24,16},{28,20},{1,9},{5... | collective-permute-start | bytes 393224 | tf_op jit(solution)/shard_map/ppermute | solution.py:223
  32.0 0.8 %shard_map.98 = (bf16[1,256,256]{2,1,0:T(8,128)(2,1)S(1)}, f32[256,256]{1,0:T(8,128)S(1)}, f32[256,256]{1,0:T(8,128)S(1)}) custom-call(bf16[1,256,512]{2,1,0:T(8,128)(2,1)S(1)} %get-tuple-element.37.queries.refs_0_, bf16[256,512]{1,0:T(8,128)(2,1)S(1)} %get-tuple-element.38.spiked.refs_1_, bf16[1,256,512]{2,1,0:T(8,128)(2,1)S(1)} %get-tuple-element.39.values.refs_2_, ...), custom_call_target="tpu_custom_call" | custom-call | flops 134217728 | bytes 2097152 | tf_op jit(solution)/shard_map/pallas_call | solution.py:40
  32.8 2.9 %collective-permute-done.7 = f32[264,128]{1,0:T(8,128)S(1)} collective-permute-done((f32[264,128]{1,0:T(8,128)S(1)}, f32[264,128]{1,0:T(8,128)S(1)}, u32[]{:S(2)}, u32[]{:S(2)}) %collective-permute-start.7) | collective-permute-done | bytes 135200 | tf_op jit(solution)/shard_map/ppermute | solution.py:223
  35.7 0.1 collective-permute-start.10
  35.8 1.4 %shard_map.99 = (bf16[1,256,512]{2,1,0:T(8,128)(2,1)}, f32[256,256]{1,0:T(8,128)S(1)}, f32[256,256]{1,0:T(8,128)S(1)}) custom-call(bf16[1,256,512]{2,1,0:T(8,128)(2,1)S(1)} %get-tuple-element.37.queries.refs_0_, bf16[256,512]{1,0:T(8,128)(2,1)S(1)} %get-tuple-element.38.spiked.refs_1_, bf16[1,256,512]{2,1,0:T(8,128)(2,1)S(1)} %get-tuple-element.39.values.refs_2_, ...), custom_call_target="tpu_custom_call" | custom-call | flops 134217728 | bytes 2097152 | tf_op jit(solution)/shard_map/pallas_call | solution.py:40
  37.2 1.0 %collective-permute-done.8 = f32[256,128]{1,0:T(8,128)S(1)} collective-permute-done((f32[256,128]{1,0:T(8,128)S(1)}, f32[256,128]{1,0:T(8,128)S(1)}, u32[]{:S(2)}, u32[]{:S(2)}) %collective-permute-start.8) | collective-permute-done | bytes 131104 | tf_op jit(solution)/shard_map/ppermute | solution.py:223
  38.2 1.1 %collective-permute-start.9 = (f32[256,128]{1,0:T(8,128)S(1)}, f32[256,128]{1,0:T(8,128)S(1)}, u32[]{:S(2)}, u32[]{:S(2)}) collective-permute-start(f32[256,128]{1,0:T(8,128)S(1)} %select_add_fusion.1), channel_id=1, source_target_pairs={{0,4},{4,0},{8,12},{12,8},{16,20},{20,16},{24,28},{28,24},{1,5},{5... | collective-permute-start | bytes 393224 | tf_op jit(solution)/shard_map/ppermute | solution.py:223
  39.3 3.4 %collective-permute-done.10 = f32[264,128]{1,0:T(8,128)S(1)} collective-permute-done((f32[264,128]{1,0:T(8,128)S(1)}, f32[264,128]{1,0:T(8,128)S(1)}, u32[]{:S(2)}, u32[]{:S(2)}) %collective-permute-start.10) | collective-permute-done | bytes 135200 | tf_op jit(solution)/shard_map/ppermute | solution.py:223
  42.8 0.2 shard_map.100
  43.0 1.1 %collective-permute-done.9 = f32[256,128]{1,0:T(8,128)S(1)} collective-permute-done((f32[256,128]{1,0:T(8,128)S(1)}, f32[256,128]{1,0:T(8,128)S(1)}, u32[]{:S(2)}, u32[]{:S(2)}) %collective-permute-start.9) | collective-permute-done | bytes 131104 | tf_op jit(solution)/shard_map/ppermute | solution.py:223
  44.1 1.0 %shard_map.101 = (bf16[1,256,512]{2,1,0:T(8,128)(2,1)}, bf16[1,256,512]{2,1,0:T(8,128)(2,1)}, f32[1,512]{1,0:T(1,128)}) custom-call(bf16[1,256,512]{2,1,0:T(8,128)(2,1)S(1)} %get-tuple-element.39.values.refs_2_, bf16[256,512]{1,0:T(8,128)(2,1)S(1)} %get-tuple-element.38.spiked.refs_1_, s32[1,256,512]{2,1,0:T(8,128)S(1)} %copy-done, ...), custom_call_target="tpu_custom_call" | custom-call | flops 33554432 | bytes 2097152 | tf_op jit(solution)/shard_map/pallas_call | solution.py:40
  (18 shorter events, 0.2 us)
Async XLA Ops:
  2.2 9.7 %collective-permute-start = (f32[256,128]{1,0:T(8,128)S(1)}, f32[256,128]{1,0:T(8,128)S(1)}, u32[]{:S(2)}, u32[]{:S(2)}) collective-permute-start(f32[256,128]{1,0:T(8,128)S(1)} %get-tuple-element.42), channel_id=1, source_target_pairs={{0,4},{4,0},{8,12},{12,8},{16,24},{20,28},{24,16},{28,20},{1,5},{5... | collective-permute-start | bytes 393224 | tf_op jit(solution)/shard_map/ppermute | solution.py:223
  5.2 7.7 %collective-permute-start.2 = (f32[256,128]{1,0:T(8,128)S(1)}, f32[256,128]{1,0:T(8,128)S(1)}, u32[]{:S(2)}, u32[]{:S(2)}) collective-permute-start(f32[256,128]{1,0:T(8,128)S(1)} %get-tuple-element.43), channel_id=1, source_target_pairs={{0,8},{4,12},{8,0},{12,4},{16,20},{20,16},{24,28},{28,24},{1,9},{5... | collective-permute-start | bytes 393224 | tf_op jit(solution)/shard_map/ppermute | solution.py:223
  11.9 1.0 %copy-start.1 = (f32[512]{0:T(512)S(1)}, f32[512]{0:T(512)}, u32[]{:S(2)}) copy-start(f32[512]{0:T(512)} %param.10) | copy-start | bytes 6148
  12.0 9.5 %collective-permute-start.1 = (f32[256,128]{1,0:T(8,128)S(1)}, f32[256,128]{1,0:T(8,128)S(1)}, u32[]{:S(2)}, u32[]{:S(2)}) collective-permute-start(f32[256,128]{1,0:T(8,128)S(1)} %add_select_fusion.1.after), channel_id=1, source_target_pairs={{0,8},{4,12},{8,0},{12,4},{16,20},{20,16},{24,28},{28,24},{1,9},{5... | collective-permute-start | bytes 393224 | tf_op jit(solution)/shard_map/ppermute | solution.py:223
  13.0 8.5 %collective-permute-start.3 = (f32[256,128]{1,0:T(8,128)S(1)}, f32[256,128]{1,0:T(8,128)S(1)}, u32[]{:S(2)}, u32[]{:S(2)}) collective-permute-start(f32[256,128]{1,0:T(8,128)S(1)} %add_select_fusion), channel_id=1, source_target_pairs={{0,4},{4,0},{8,12},{12,8},{16,24},{20,28},{24,16},{28,20},{1,5},{5... | collective-permute-start | bytes 393224 | tf_op jit(solution)/shard_map/ppermute | solution.py:223
  21.9 4.5 %collective-permute-start.6 = (f32[2,256]{1,0:T(2,128)S(1)}, f32[2,256]{1,0:T(2,128)S(1)}, u32[]{:S(2)}, u32[]{:S(2)}) collective-permute-start(f32[2,256]{1,0:T(2,128)S(1)} %get-tuple-element.47), channel_id=1, source_target_pairs={{0,3},{1,2},{2,1},{3,0},{4,7},{5,6},{6,5},{7,4},{8,11},{9,10},{10,... | collective-permute-start | bytes 6152 | tf_op jit(solution)/shard_map/ppermute | solution.py:198
  24.6 3.6 %collective-permute-start.5 = (f32[2,256]{1,0:T(2,128)S(1)}, f32[2,256]{1,0:T(2,128)S(1)}, u32[]{:S(2)}, u32[]{:S(2)}) collective-permute-start(f32[2,256]{1,0:T(2,128)S(1)} %get-tuple-element.47), channel_id=1, source_target_pairs={{0,2},{1,3},{2,0},{3,1},{4,6},{5,7},{6,4},{7,5},{8,10},{9,11},{10,... | collective-permute-start | bytes 6152 | tf_op jit(solution)/shard_map/ppermute | solution.py:198
  25.1 3.6 %collective-permute-start.4 = (f32[2,256]{1,0:T(2,128)S(1)}, f32[2,256]{1,0:T(2,128)S(1)}, u32[]{:S(2)}, u32[]{:S(2)}) collective-permute-start(f32[2,256]{1,0:T(2,128)S(1)} %get-tuple-element.47), channel_id=1, source_target_pairs={{0,1},{1,0},{2,3},{3,2},{4,5},{5,4},{6,7},{7,6},{8,9},{9,8},{10,11... | collective-permute-start | bytes 6152 | tf_op jit(solution)/shard_map/ppermute | solution.py:198
  29.1 6.6 %collective-permute-start.7 = (f32[264,128]{1,0:T(8,128)S(1)}, f32[264,128]{1,0:T(8,128)S(1)}, u32[]{:S(2)}, u32[]{:S(2)}) collective-permute-start(f32[264,128]{1,0:T(8,128)S(1)} %get-tuple-element.56), channel_id=1, source_target_pairs={{0,4},{4,0},{8,12},{12,8},{16,20},{20,16},{24,28},{28,24},{1,5},{5... | collective-permute-start | bytes 405512 | tf_op jit(solution)/shard_map/ppermute | solution.py:223
  29.2 9.0 %collective-permute-start.8 = (f32[256,128]{1,0:T(8,128)S(1)}, f32[256,128]{1,0:T(8,128)S(1)}, u32[]{:S(2)}, u32[]{:S(2)}) collective-permute-start(f32[256,128]{1,0:T(8,128)S(1)} %get-tuple-element.60), channel_id=1, source_target_pairs={{0,8},{4,12},{8,0},{12,4},{16,24},{20,28},{24,16},{28,20},{1,9},{5... | collective-permute-start | bytes 393224 | tf_op jit(solution)/shard_map/ppermute | solution.py:223
  35.7 7.0 %collective-permute-start.10 = (f32[264,128]{1,0:T(8,128)S(1)}, f32[264,128]{1,0:T(8,128)S(1)}, u32[]{:S(2)}, u32[]{:S(2)}) collective-permute-start(f32[264,128]{1,0:T(8,128)S(1)} %add.58.after), channel_id=1, source_target_pairs={{0,8},{4,12},{8,0},{12,4},{16,24},{20,28},{24,16},{28,20},{1,9},{5... | collective-permute-start | bytes 405512 | tf_op jit(solution)/shard_map/ppermute | solution.py:223
  37.2 5.6 %copy-start = (s32[1,256,512]{2,1,0:T(8,128)S(1)}, s32[1,256,512]{2,1,0:T(8,128)}, u32[]{:S(2)}) copy-start(s32[1,256,512]{2,1,0:T(8,128)} %spikes.5) | copy-start | bytes 1572868
  38.2 5.8 %collective-permute-start.9 = (f32[256,128]{1,0:T(8,128)S(1)}, f32[256,128]{1,0:T(8,128)S(1)}, u32[]{:S(2)}, u32[]{:S(2)}) collective-permute-start(f32[256,128]{1,0:T(8,128)S(1)} %select_add_fusion.1), channel_id=1, source_target_pairs={{0,4},{4,0},{8,12},{12,8},{16,20},{20,16},{24,28},{28,24},{1,5},{5... | collective-permute-start | bytes 393224 | tf_op jit(solution)/shard_map/ppermute | solution.py:223
  42.7 1.3 %collective-permute-start.11 = (f32[8,128]{1,0:T(8,128)S(1)}, f32[8,128]{1,0:T(8,128)S(1)}, u32[]{:S(2)}, u32[]{:S(2)}) collective-permute-start(f32[8,128]{1,0:T(8,128)S(1)} %slice_add_fusion.gain_here), channel_id=1, source_target_pairs={{0,16},{16,0},{1,17},{17,1},{2,18},{18,2},{3,19},{19,3},{4,20},{20... | collective-permute-start | bytes 12296 | tf_op jit(solution)/shard_map/ppermute | solution.py:198

commit v4 on v3

--- a/solution.py
+++ b/solution.py
@@ -54,13 +54,14 @@
 
 
 def state_kernel(
-    queries, keys, spikes, values, upstream, held_queries, held_values, upper, spiked, *rest
+    queries, keys, spikes, values, upstream, gain,
+    held_queries, held_values, upper, held_gain, spiked, *rest,
 ):
     *states, key_buf, spike_buf, sems = rest
     heads = spiked.shape[1] // DH
     pairs = (
         (keys, key_buf), (spikes, spike_buf), (values, held_values),
-        (queries, held_queries), (upstream, upper),
+        (queries, held_queries), (upstream, upper), (gain, held_gain),
     )
     copies = [pltpu.make_async_copy(src, dst, sems.at[k]) for k, (src, dst) in enumerate(pairs)]
     for copy in copies:
@@ -127,37 +128,27 @@
         locals_[0][gain_at + h : gain_at + h + 1, :] = jnp.sum(terms, axis=0, keepdims=True)
 
 
-def pair_heads(
-    first, to, queries, spiked, values, grad, prior, scores, grad_query, key_part, value_part
+def pairs_kernel(
+    queries, spiked, values, grad, prior, scores,
+    grad_query, key_first, value_first, key_last, value_last,
 ):
-    tok = spiked.shape[0]
+    heads, tok, _ = scores.shape
+    half = heads // 2
     causal = causal_mask(tok)
-    for h in range(key_part.shape[1] // DH):
-        at = cols(first + h)
+    for h in range(heads):
+        at = cols(h)
+        key_part, value_part = ((key_first, value_first), (key_last, value_last))[h // half]
         result = grad[:, at]
         raw = dot(result, values[0, :, at], 1, 1)
         pairs = jnp.where(causal, raw, 0.0).astype(BF16)
-        query_part = dot(result, prior[first + h], 1, 1) + dot(pairs, spiked[:, at], 1, 0)
-        grad_query[0, :, cols(to + h)] = query_part.astype(BF16)
-        key_part[:, cols(h)] = dot(pairs, queries[0, :, at], 0, 0)
-        value_part[:, cols(h)] = dot(scores[first + h], result, 0, 0)
-
-
-def pairs_first_kernel(*refs):
-    pair_heads(0, 0, *refs)
-
-
-def pairs_last_kernel(
-    queries, spiked, values, grad, prior, scores, query_half, after,
-    grad_query, key_part, value_part,
-):
-    del after
-    done = query_half.shape[2]
-    grad_query[:, :, :done] = query_half[...]
-    pair_heads(
-        done // DH, done // DH, queries, spiked, values, grad, prior, scores,
-        grad_query, key_part, value_part,
-    )
+        query_part = dot(result, prior[h], 1, 1) + dot(pairs, spiked[:, at], 1, 0)
+        grad_query[0, :, at] = query_part.astype(BF16)
+        key_part[:, cols(h % half)] = dot(pairs, queries[0, :, at], 0, 0)
+        value_part[:, cols(h % half)] = dot(scores[h], result, 0, 0)
+
+
+def tail_kernel(total, rows):
+    rows[...] = total[total.shape[0] - rows.shape[0] :, :]
 
 
 def final_half(first, values, spiked, spikes, key_part, value_part, sums, outs, to):
@@ -229,7 +220,6 @@
     up_order = strides(axis)
     down_order = up_order[::-1]
     rounds = len(up_order)
-    extra = lax.broadcasted_iota(jnp.int32, lead.shape, 0) >= last.shape[0]
     own = [lead, last]
     goes_up = [lead_up, jnp.logical_not(lead_up)]
     sent = [lead, last]
@@ -255,14 +245,19 @@
                 next_down = down_order[k + 1]
                 serves = ((at & next_down) != 0) if reverse else ((at & next_down) == 0)
                 partial = sums[p] + jnp.where(serves, own[p], 0.0)
-                whole = jnp.logical_or(goes_up[p], extra) if p == 0 else goes_up[p]
+                whole = goes_up[p]
+                if own[p].shape[0] > last.shape[0]:
+                    extra = lax.broadcasted_iota(jnp.int32, own[p].shape, 0) >= last.shape[0]
+                    whole = jnp.logical_or(whole, extra)
                 sent[p] = jnp.where(whole, total[p], partial)
             if p == 0:
                 token = sums[0]
                 if k == 0:
                     token, result = between(sent[0])
-                if k == rounds - 1 and finish is not None:
-                    token, result = finish(sums[0], total[0], result)
+                elif finish is not None and k < rounds - 1:
+                    result = result + got[0][last.shape[0] :]
+                elif finish is not None:
+                    token, result = finish(sums[0], got[0], result)
                 got[1], _ = lax.optimization_barrier((got[1], token))
     return sums[0], sums[1], result
 
@@ -282,15 +277,15 @@
     small = 2 * heads * tok * DH * DH
     big = 2 * heads * tok * tok * DH
 
-    held_queries, held_values, upper, spiked, state_a, state_b = call(
+    held_queries, held_values, upper, held_gain, spiked, state_a, state_b = call(
         state_kernel,
-        [whole, whole, whole, shape(flat, BF16), piece, piece],
-        queries, keys, spikes, values, upstream,
-        hbm=(0, 1, 2, 3, 4),
+        [whole, whole, whole, shape((1, width_dev), F32), shape(flat, BF16), piece, piece],
+        queries, keys, spikes, values, upstream, gain_row,
+        hbm=(0, 1, 2, 3, 4, 5),
         scratch=[
             pltpu.VMEM((1, *flat), BF16),
             pltpu.VMEM((1, *flat), jnp.int32),
-            pltpu.SemaphoreType.DMA((5,)),
+            pltpu.SemaphoreType.DMA((6,)),
         ],
         flops=small, moved=2**20,
     )
@@ -302,7 +297,7 @@
     )
 
     def scale(total):
-        scaled = call(scale_kernel, [shape(flat, F32)], upper, gain_row, total, moved=2**20)[0]
+        scaled = call(scale_kernel, [shape(flat, F32)], upper, held_gain, total, moved=2**20)[0]
         return scaled, scaled
 
     prior_a, prior_b, scaled = scan_pair(state_a, state_b, "ctx", False, True, scale)
@@ -320,41 +315,37 @@
         flops=small, moved=2**21,
     )
 
-    half_outs = [shape((1, tok, half * DH), BF16)] + [shape((tok, half * DH), F32)] * 2
-    pair_args = (held_queries, spiked, held_values, grad, prior, scores)
-    query_half, *first_parts = call(
-        pairs_first_kernel, half_outs, *pair_args, flops=2 * big, moved=2**21
-    )
-
-    def pair(total):
-        outs = call(
-            pairs_last_kernel,
-            [whole, *half_outs[1:]],
-            *pair_args, query_half, total,
-            flops=2 * big, moved=2**21,
-        )
-        return outs[1], outs
-
-    def finish(later_a, total, paired):
-        gain_here = total[half * DH :]
+    half_part = shape((tok, half * DH), F32)
+    grad_query, *parts = call(
+        pairs_kernel,
+        [whole] + [half_part] * 4,
+        held_queries, spiked, held_values, grad, prior, scores,
+        flops=4 * big, moved=2**22,
+    )
+
+    def gain_rows(total):
+        rows = call(tail_kernel, [shape((GAIN_ROWS, DH), F32)], total)[0]
+        return rows, rows
+
+    def finish(later_a, got, gain_before):
+        gain_here = gain_before + got[half * DH :]
         gain_there = swap(gain_here, "dp", 1)
         first = call(
             final_first_kernel,
             [shape((1, tok, half * DH), BF16)] * 2,
-            held_values, spiked, spikes, *first_parts, later_a,
+            held_values, spiked, spikes, *parts[:2], later_a,
             flops=small, moved=2**21,
         )
-        token = (first[0], gain_there)
-        return token, (*paired, gain_here, gain_there, *first)
-
-    _, later_b, (grad_query, key_part, value_part, gain_here, gain_there, *first) = scan_pair(
-        local_a, local_b, "ctx", True, False, pair, finish
+        return (first[0], gain_there), (gain_here, gain_there, *first)
+
+    _, later_b, (gain_here, gain_there, *first) = scan_pair(
+        local_a, local_b, "ctx", True, False, gain_rows, finish
     )
     total_tokens = tok * lax.axis_size("ctx") * lax.axis_size("dp")
     grad_key, grad_value, grad_gain = call(
         functools.partial(final_last_kernel, 1.0 / math.sqrt(total_tokens)),
         [whole, whole, shape((1, width_dev), F32)],
-        held_values, spiked, spikes, key_part, value_part, later_b, gain_here, gain_there, *first,
+        held_values, spiked, spikes, *parts[2:], later_b, gain_here, gain_there, *first,
         flops=small, moved=2**21,
     )
     return grad_query, grad_key, grad_value, grad_gain.reshape(width_dev)

time: 45.2 us -> 44.8 us (level)
  waiting for transfers between devices: 20.8 us -> 19.4 us
  starting transfers between devices: 16.9 us -> 18.1 us
    ppermute x8, waiting for transfers between devices: 17.6 us -> 15.3 us  [swap_by_core(): return lax.ppermute(array, ('dp', axis), pairs)]
    ppermute x8, starting transfers between devices: 13.4 us -> 14.5 us  [swap_by_core(): return lax.ppermute(array, ('dp', axis), pairs)]
    ppermute x4, waiting for transfers between devices: 3.21 us -> 4.14 us  [swap(): return lax.ppermute(array, axis, [(i, i ^ stride) for i in range(size)])]
  transfers between devices with their start and end apart: 12 -> 12, of which waited for: 9 -> 8; matrix products, arithmetic and copies ran while one was open for 0% -> 0% of each run, Pallas kernels for 7% -> 6%
where the time goes in v4:
time: 44.8 us; the launch traced here: 44.7 us
  waiting for transfers between devices  19.4 us (43%)
  starting transfers between devices  18.1 us (40%)
  Pallas kernels  6.18 us (14%)
  between operations  0.78 us (2%)
    ppermute x8, waiting for transfers between devices, swap_by_core(): return lax.ppermute(array, ('dp', axis), pairs)  15.3 us
    ppermute x8, starting transfers between devices, swap_by_core(): return lax.ppermute(array, ('dp', axis), pairs)  14.5 us
    pallas_call x9, Pallas kernels, call(): pl.pallas_call(body, out_shape=outs, in_specs=[HBM if k in hbm else VMEM...  6.18 us
    ppermute x4, waiting for transfers between devices, swap(): return lax.ppermute(array, axis, [(i, i ^ stride) for i in range(size)])  4.14 us
    ppermute x4, starting transfers between devices, swap(): return lax.ppermute(array, axis, [(i, i ^ stride) for i in range(size)])  3.55 us
  transfers between devices with their start and end apart: 12, of which 8 were waited for; matrix products, arithmetic and copies ran while one was open for 0% of the time, Pallas kernels for 6%

profile of v4, /device:TPU:0, one launch (start us, length us, event | category | flops | bytes accessed | tf_op | source)
XLA Modules:
  0.0 44.7 jit_solution(3776952898992698931)
XLA Ops:
  0.6 1.5 %shard_map.93 = (bf16[1,256,512]{2,1,0:T(8,128)(2,1)S(1)}, bf16[1,256,512]{2,1,0:T(8,128)(2,1)S(1)}, bf16[1,256,512]{2,1,0:T(8,128)(2,1)S(1)}, f32[1,512]{1,0:T(...) custom-call(bf16[1,256,512]{2,1,0:T(8,128)(2,1)} %queries.1, ...), custom_call_target="tpu_custom_call" | custom-call | flops 33554432 | bytes 1048576 | tf_op jit(solution)/shard_map/pallas_call | solution.py:40
  2.2 3.1 %collective-permute-start = (f32[256,128]{1,0:T(8,128)S(1)}, f32[256,128]{1,0:T(8,128)S(1)}, u32[]{:S(2)}, u32[]{:S(2)}) collective-permute-start(f32[256,128]{1,0:T(8,128)S(1)} %get-tuple-element.43), channel_id=1, source_target_pairs={{0,4},{4,0},{8,12},{12,8},{16,24},{20,28},{24,16},{28,20},{1,5},{5... | collective-permute-start | bytes 393224 | tf_op jit(solution)/shard_map/ppermute | solution.py:214
  5.3 2.6 %collective-permute-start.2 = (f32[256,128]{1,0:T(8,128)S(1)}, f32[256,128]{1,0:T(8,128)S(1)}, u32[]{:S(2)}, u32[]{:S(2)}) collective-permute-start(f32[256,128]{1,0:T(8,128)S(1)} %get-tuple-element.44), channel_id=1, source_target_pairs={{0,8},{4,12},{8,0},{12,4},{16,20},{20,16},{24,28},{28,24},{1,9},{5... | collective-permute-start | bytes 393224 | tf_op jit(solution)/shard_map/ppermute | solution.py:214
  7.8 0.7 %shard_map.94 = (bf16[4,256,256]{2,1,0:T(8,128)(2,1)S(1)}, f32[256,512]{1,0:T(8,128)S(1)}) custom-call(bf16[1,256,512]{2,1,0:T(8,128)(2,1)S(1)} %get-tuple-element.37.queries, bf16[256,512]{1,0:T(8,128)(2,1)S(1)} %get-tuple-element.38.spiked, bf16[1,256,512]{2,1,0:T(8,128)(2,1)S(1)} %get-tuple-element.39.values), custom_call_target="tpu_custom_call" | custom-call | flops 134217728 | bytes 2097152 | tf_op jit(solution)/shard_map/pallas_call | solution.py:40
  8.5 3.3 %collective-permute-done = f32[256,128]{1,0:T(8,128)S(1)} collective-permute-done((f32[256,128]{1,0:T(8,128)S(1)}, f32[256,128]{1,0:T(8,128)S(1)}, u32[]{:S(2)}, u32[]{:S(2)}) %collective-permute-start) | collective-permute-done | bytes 131104 | tf_op jit(solution)/shard_map/ppermute | solution.py:214
  11.9 1.0 %collective-permute-start.1 = (f32[256,128]{1,0:T(8,128)S(1)}, f32[256,128]{1,0:T(8,128)S(1)}, u32[]{:S(2)}, u32[]{:S(2)}) collective-permute-start(f32[256,128]{1,0:T(8,128)S(1)} %add_select_fusion.1.after), channel_id=1, source_target_pairs={{0,8},{4,12},{8,0},{12,4},{16,20},{20,16},{24,28},{28,24},{1,9},{5... | collective-permute-start | bytes 393224 | tf_op jit(solution)/shard_map/ppermute | solution.py:214
  12.9 0.0 collective-permute-done.2
  12.9 2.7 %collective-permute-start.3 = (f32[256,128]{1,0:T(8,128)S(1)}, f32[256,128]{1,0:T(8,128)S(1)}, u32[]{:S(2)}, u32[]{:S(2)}) collective-permute-start(f32[256,128]{1,0:T(8,128)S(1)} %add_select_fusion), channel_id=1, source_target_pairs={{0,4},{4,0},{8,12},{12,8},{16,24},{20,28},{24,16},{28,20},{1,5},{5... | collective-permute-start | bytes 393224 | tf_op jit(solution)/shard_map/ppermute | solution.py:214
  15.6 5.8 %collective-permute-done.1 = f32[256,128]{1,0:T(8,128)S(1)} collective-permute-done((f32[256,128]{1,0:T(8,128)S(1)}, f32[256,128]{1,0:T(8,128)S(1)}, u32[]{:S(2)}, u32[]{:S(2)}) %collective-permute-start.1) | collective-permute-done | bytes 131104 | tf_op jit(solution)/shard_map/ppermute | solution.py:214
  21.5 0.0 collective-permute-done.3
  21.5 0.4 shard_map.96
  21.9 2.7 %collective-permute-start.6 = (f32[2,256]{1,0:T(2,128)S(1)}, f32[2,256]{1,0:T(2,128)S(1)}, u32[]{:S(2)}, u32[]{:S(2)}) collective-permute-start(f32[2,256]{1,0:T(2,128)S(1)} %get-tuple-element.48), channel_id=1, source_target_pairs={{0,3},{1,2},{2,1},{3,0},{4,7},{5,6},{6,5},{7,4},{8,11},{9,10},{10,... | collective-permute-start | bytes 6152 | tf_op jit(solution)/shard_map/ppermute | solution.py:189
  24.6 0.5 %collective-permute-start.5 = (f32[2,256]{1,0:T(2,128)S(1)}, f32[2,256]{1,0:T(2,128)S(1)}, u32[]{:S(2)}, u32[]{:S(2)}) collective-permute-start(f32[2,256]{1,0:T(2,128)S(1)} %get-tuple-element.48), channel_id=1, source_target_pairs={{0,2},{1,3},{2,0},{3,1},{4,6},{5,7},{6,4},{7,5},{8,10},{9,11},{10,... | collective-permute-start | bytes 6152 | tf_op jit(solution)/shard_map/ppermute | solution.py:189
  25.1 0.3 collective-permute-start.4
  25.4 1.0 %collective-permute-done.6 = f32[2,256]{1,0:T(2,128)S(1)} collective-permute-done((f32[2,256]{1,0:T(2,128)S(1)}, f32[2,256]{1,0:T(2,128)S(1)}, u32[]{:S(2)}, u32[]{:S(2)}) %collective-permute-start.6) | collective-permute-done | bytes 2080 | tf_op jit(solution)/shard_map/ppermute | solution.py:189
  26.4 1.8 %collective-permute-done.5 = f32[2,256]{1,0:T(2,128)S(1)} collective-permute-done((f32[2,256]{1,0:T(2,128)S(1)}, f32[2,256]{1,0:T(2,128)S(1)}, u32[]{:S(2)}, u32[]{:S(2)}) %collective-permute-start.5) | collective-permute-done | bytes 2080 | tf_op jit(solution)/shard_map/ppermute | solution.py:189
  28.2 0.5 %collective-permute-done.4 = f32[2,256]{1,0:T(2,128)S(1)} collective-permute-done((f32[2,256]{1,0:T(2,128)S(1)}, f32[2,256]{1,0:T(2,128)S(1)}, u32[]{:S(2)}, u32[]{:S(2)}) %collective-permute-start.4) | collective-permute-done | bytes 2080 | tf_op jit(solution)/shard_map/ppermute | solution.py:189
  28.7 0.4 shard_map.97
  29.1 0.1 collective-permute-start.8
  29.2 2.7 %collective-permute-start.7 = (f32[256,128]{1,0:T(8,128)S(1)}, f32[256,128]{1,0:T(8,128)S(1)}, u32[]{:S(2)}, u32[]{:S(2)}) collective-permute-start(f32[256,128]{1,0:T(8,128)S(1)} %get-tuple-element.59), channel_id=1, source_target_pairs={{0,8},{4,12},{8,0},{12,4},{16,24},{20,28},{24,16},{28,20},{1,9},{5... | collective-permute-start | bytes 393224 | tf_op jit(solution)/shard_map/ppermute | solution.py:214
  31.8 1.9 %shard_map.98 = (bf16[1,256,512]{2,1,0:T(8,128)(2,1)}, f32[256,256]{1,0:T(8,128)S(1)}, f32[256,256]{1,0:T(8,128)S(1)}, f32[256,256]{1,0:T(8,128)S(1)}, f32[256,256]{1,0:T(8,128)S(1)}) custom-call(bf16[1,256,512]{2,1,0:T(8,128)(2,1)S(1)} %get-tuple-element.37.queries, bf16[256,512]{1,0:T(8,128)(2,1)S(1)} %get-tuple-element.38.spiked, ...), custom_call_target="tpu_custom_call" | custom-call | flops 268435456 | bytes 4194304 | tf_op jit(solution)/shard_map/pallas_call | solution.py:40
  33.8 2.0 %collective-permute-done.8 = f32[264,128]{1,0:T(8,128)S(1)} collective-permute-done((f32[264,128]{1,0:T(8,128)S(1)}, f32[264,128]{1,0:T(8,128)S(1)}, u32[]{:S(2)}, u32[]{:S(2)}) %collective-permute-start.8) | collective-permute-done | bytes 135200 | tf_op jit(solution)/shard_map/ppermute | solution.py:214
  35.8 0.0 copy-start
  35.8 0.1 collective-permute-start.10
  35.9 0.0 collective-permute-done.7
  35.9 2.4 %collective-permute-start.9 = (f32[256,128]{1,0:T(8,128)S(1)}, f32[256,128]{1,0:T(8,128)S(1)}, u32[]{:S(2)}, u32[]{:S(2)}) collective-permute-start(f32[256,128]{1,0:T(8,128)S(1)} %select_add_fusion.1), channel_id=1, source_target_pairs={{0,4},{4,0},{8,12},{12,8},{16,20},{20,16},{24,28},{28,24},{1,5},{5... | collective-permute-start | bytes 393224 | tf_op jit(solution)/shard_map/ppermute | solution.py:214
  38.3 4.1 %collective-permute-done.10 = f32[264,128]{1,0:T(8,128)S(1)} collective-permute-done((f32[264,128]{1,0:T(8,128)S(1)}, f32[264,128]{1,0:T(8,128)S(1)}, u32[]{:S(2)}, u32[]{:S(2)}) %collective-permute-start.10) | collective-permute-done | bytes 135200 | tf_op jit(solution)/shard_map/ppermute | solution.py:214
  42.5 0.0 collective-permute-start.11
  42.5 0.2 shard_map.100
  42.7 0.0 collective-permute-done.9
  42.7 0.9 %collective-permute-done.11.gain_there = f32[8,128]{1,0:T(8,128)S(1)} collective-permute-done((f32[8,128]{1,0:T(8,128)S(1)}, f32[8,128]{1,0:T(8,128)S(1)}, u32[]{:S(2)}, u32[]{:S(2)}) %collective-permute-start.11) | collective-permute-done | bytes 4128 | tf_op jit(solution)/shard_map/ppermute | solution.py:189
  43.7 1.0 %shard_map.101 = (bf16[1,256,512]{2,1,0:T(8,128)(2,1)}, bf16[1,256,512]{2,1,0:T(8,128)(2,1)}, f32[1,512]{1,0:T(1,128)}) custom-call(bf16[1,256,512]{2,1,0:T(8,128)(2,1)S(1)} %get-tuple-element.39.values, bf16[256,512]{1,0:T(8,128)(2,1)S(1)} %get-tuple-element.38.spiked, s32[1,256,512]{2,1,0:T(8,128)S(1)} %copy-done, ...), custom_call_target="tpu_custom_call" | custom-call | flops 33554432 | bytes 2097152 | tf_op jit(solution)/shard_map/pallas_call | solution.py:40
  (15 shorter events, 0.2 us)
Async XLA Ops:
  2.2 9.7 %collective-permute-start = (f32[256,128]{1,0:T(8,128)S(1)}, f32[256,128]{1,0:T(8,128)S(1)}, u32[]{:S(2)}, u32[]{:S(2)}) collective-permute-start(f32[256,128]{1,0:T(8,128)S(1)} %get-tuple-element.43), channel_id=1, source_target_pairs={{0,4},{4,0},{8,12},{12,8},{16,24},{20,28},{24,16},{28,20},{1,5},{5... | collective-permute-start | bytes 393224 | tf_op jit(solution)/shard_map/ppermute | solution.py:214
  5.3 7.6 %collective-permute-start.2 = (f32[256,128]{1,0:T(8,128)S(1)}, f32[256,128]{1,0:T(8,128)S(1)}, u32[]{:S(2)}, u32[]{:S(2)}) collective-permute-start(f32[256,128]{1,0:T(8,128)S(1)} %get-tuple-element.44), channel_id=1, source_target_pairs={{0,8},{4,12},{8,0},{12,4},{16,20},{20,16},{24,28},{28,24},{1,9},{5... | collective-permute-start | bytes 393224 | tf_op jit(solution)/shard_map/ppermute | solution.py:214
  11.9 9.6 %collective-permute-start.1 = (f32[256,128]{1,0:T(8,128)S(1)}, f32[256,128]{1,0:T(8,128)S(1)}, u32[]{:S(2)}, u32[]{:S(2)}) collective-permute-start(f32[256,128]{1,0:T(8,128)S(1)} %add_select_fusion.1.after), channel_id=1, source_target_pairs={{0,8},{4,12},{8,0},{12,4},{16,20},{20,16},{24,28},{28,24},{1,9},{5... | collective-permute-start | bytes 393224 | tf_op jit(solution)/shard_map/ppermute | solution.py:214
  12.9 8.5 %collective-permute-start.3 = (f32[256,128]{1,0:T(8,128)S(1)}, f32[256,128]{1,0:T(8,128)S(1)}, u32[]{:S(2)}, u32[]{:S(2)}) collective-permute-start(f32[256,128]{1,0:T(8,128)S(1)} %add_select_fusion), channel_id=1, source_target_pairs={{0,4},{4,0},{8,12},{12,8},{16,24},{20,28},{24,16},{28,20},{1,5},{5... | collective-permute-start | bytes 393224 | tf_op jit(solution)/shard_map/ppermute | solution.py:214
  21.9 4.5 %collective-permute-start.6 = (f32[2,256]{1,0:T(2,128)S(1)}, f32[2,256]{1,0:T(2,128)S(1)}, u32[]{:S(2)}, u32[]{:S(2)}) collective-permute-start(f32[2,256]{1,0:T(2,128)S(1)} %get-tuple-element.48), channel_id=1, source_target_pairs={{0,3},{1,2},{2,1},{3,0},{4,7},{5,6},{6,5},{7,4},{8,11},{9,10},{10,... | collective-permute-start | bytes 6152 | tf_op jit(solution)/shard_map/ppermute | solution.py:189
  24.6 3.6 %collective-permute-start.5 = (f32[2,256]{1,0:T(2,128)S(1)}, f32[2,256]{1,0:T(2,128)S(1)}, u32[]{:S(2)}, u32[]{:S(2)}) collective-permute-start(f32[2,256]{1,0:T(2,128)S(1)} %get-tuple-element.48), channel_id=1, source_target_pairs={{0,2},{1,3},{2,0},{3,1},{4,6},{5,7},{6,4},{7,5},{8,10},{9,11},{10,... | collective-permute-start | bytes 6152 | tf_op jit(solution)/shard_map/ppermute | solution.py:189
  25.1 3.6 %collective-permute-start.4 = (f32[2,256]{1,0:T(2,128)S(1)}, f32[2,256]{1,0:T(2,128)S(1)}, u32[]{:S(2)}, u32[]{:S(2)}) collective-permute-start(f32[2,256]{1,0:T(2,128)S(1)} %get-tuple-element.48), channel_id=1, source_target_pairs={{0,1},{1,0},{2,3},{3,2},{4,5},{5,4},{6,7},{7,6},{8,9},{9,8},{10,11... | collective-permute-start | bytes 6152 | tf_op jit(solution)/shard_map/ppermute | solution.py:189
  29.1 6.7 %collective-permute-start.8 = (f32[264,128]{1,0:T(8,128)S(1)}, f32[264,128]{1,0:T(8,128)S(1)}, u32[]{:S(2)}, u32[]{:S(2)}) collective-permute-start(f32[264,128]{1,0:T(8,128)S(1)} %get-tuple-element.60), channel_id=1, source_target_pairs={{0,4},{4,0},{8,12},{12,8},{16,20},{20,16},{24,28},{28,24},{1,5},{5... | collective-permute-start | bytes 405512 | tf_op jit(solution)/shard_map/ppermute | solution.py:214
  29.2 6.7 %collective-permute-start.7 = (f32[256,128]{1,0:T(8,128)S(1)}, f32[256,128]{1,0:T(8,128)S(1)}, u32[]{:S(2)}, u32[]{:S(2)}) collective-permute-start(f32[256,128]{1,0:T(8,128)S(1)} %get-tuple-element.59), channel_id=1, source_target_pairs={{0,8},{4,12},{8,0},{12,4},{16,24},{20,28},{24,16},{28,20},{1,9},{5... | collective-permute-start | bytes 393224 | tf_op jit(solution)/shard_map/ppermute | solution.py:214
  35.8 6.7 %copy-start = (s32[1,256,512]{2,1,0:T(8,128)S(1)}, s32[1,256,512]{2,1,0:T(8,128)}, u32[]{:S(2)}) copy-start(s32[1,256,512]{2,1,0:T(8,128)} %spikes.5) | copy-start | bytes 1572868
  35.8 6.6 %collective-permute-start.10 = (f32[264,128]{1,0:T(8,128)S(1)}, f32[264,128]{1,0:T(8,128)S(1)}, u32[]{:S(2)}, u32[]{:S(2)}) collective-permute-start(f32[264,128]{1,0:T(8,128)S(1)} %add.58.total), channel_id=1, source_target_pairs={{0,8},{4,12},{8,0},{12,4},{16,24},{20,28},{24,16},{28,20},{1,9},{5... | collective-permute-start | bytes 405512 | tf_op jit(solution)/shard_map/ppermute | solution.py:214
  35.9 6.8 %collective-permute-start.9 = (f32[256,128]{1,0:T(8,128)S(1)}, f32[256,128]{1,0:T(8,128)S(1)}, u32[]{:S(2)}, u32[]{:S(2)}) collective-permute-start(f32[256,128]{1,0:T(8,128)S(1)} %select_add_fusion.1), channel_id=1, source_target_pairs={{0,4},{4,0},{8,12},{12,8},{16,20},{20,16},{24,28},{28,24},{1,5},{5... | collective-permute-start | bytes 393224 | tf_op jit(solution)/shard_map/ppermute | solution.py:214
  42.5 1.2 %collective-permute-start.11 = (f32[8,128]{1,0:T(8,128)S(1)}, f32[8,128]{1,0:T(8,128)S(1)}, u32[]{:S(2)}, u32[]{:S(2)}) collective-permute-start(f32[8,128]{1,0:T(8,128)S(1)} %slice_add_fusion.gain_here), channel_id=1, source_target_pairs={{0,16},{16,0},{1,17},{17,1},{2,18},{18,2},{3,19},{19,3},{4,20},{20... | collective-permute-start | bytes 12296 | tf_op jit(solution)/shard_map/ppermute | solution.py:189

commit v5 on v4

--- a/solution.py
+++ b/solution.py
@@ -92,13 +92,14 @@
     scaled[...] = upper[0].astype(F32) * gain[...]
 
 
-def attend_kernel(queries, intra, scaled, sum_a, sum_b, attended, prior, sums):
+def attend_kernel(queries, intra, scaled, *rest):
+    *states, attended, prior, sums = rest
     heads = prior.shape[0]
     tok = intra.shape[0]
     square = jnp.zeros((tok, DH), F32)
     cross = jnp.zeros((tok, DH), F32)
     for h in range(heads):
-        ref, rows = block_of((sum_a, sum_b), h)
+        ref, rows = block_of(states, h)
         state = ref[rows, :].astype(BF16)
         prior[h] = state
         block = dot(queries[0, :, cols(h)], state, 1, 0) + intra[:, cols(h)]
@@ -151,35 +152,35 @@
     rows[...] = total[total.shape[0] - rows.shape[0] :, :]
 
 
-def final_half(first, values, spiked, spikes, key_part, value_part, sums, outs, to):
-    for h in range(sums.shape[0] // DH):
+def final_heads(first, values, spiked, spikes, key_part, value_part, states, outs, to):
+    for h in range(key_part.shape[1] // DH):
         at = cols(first + h)
-        later = sums[cols(h), :].astype(BF16)
+        ref, rows = block_of(states, h)
+        later = ref[rows, :].astype(BF16)
         inner = key_part[:, cols(h)] + dot(values[0, :, at], later, 1, 1)
         outs[0][0, :, cols(to + h)] = (inner * spikes[0, :, at].astype(F32)).astype(BF16)
         block = value_part[:, cols(h)] + dot(spiked[:, at], later, 1, 0)
         outs[1][0, :, cols(to + h)] = block.astype(BF16)
 
 
-def final_first_kernel(
-    values, spiked, spikes, key_part, value_part, sums, key_half, value_half
+def final_first_kernel(values, spiked, spikes, key_part, value_part, *rest):
+    *states, key_half, value_half = rest
+    outs = (key_half, value_half)
+    final_heads(0, values, spiked, spikes, key_part, value_part, states, outs, 0)
+
+
+def final_last_kernel(
+    scale, values, spiked, spikes, key_part, value_part, gain_here, gain_there,
+    key_half, value_half, *rest,
 ):
-    outs = (key_half, value_half)
-    final_half(0, values, spiked, spikes, key_part, value_part, sums, outs, 0)
-
-
-def final_last_kernel(
-    scale, values, spiked, spikes, key_part, value_part, sums, gain_here, gain_there,
-    key_half, value_half, grad_key, grad_value, grad_gain,
-):
+    *states, grad_key, grad_value, grad_gain = rest
     outs = (grad_key, grad_value)
     width = spiked.shape[1]
     done = key_half.shape[2]
     for out, half in zip(outs, (key_half, value_half)):
         out[:, :, :done] = half[...]
-    final_half(
-        done // DH, values, spiked, spikes, key_part, value_part, sums, outs, done // DH
-    )
+    first = done // DH
+    final_heads(first, values, spiked, spikes, key_part, value_part, states, outs, first)
     for h in range(width // DH):
         grad_gain[:, cols(h)] = (gain_here[h : h + 1, :] + gain_there[h : h + 1, :]) * scale
 
@@ -214,26 +215,31 @@
     return lax.ppermute(array, ("dp", axis), pairs)
 
 
-def scan_pair(lead, last, axis, reverse, by_core, between, finish=None):
+def scan(pieces, axis, reverse, by_core, between, finish=None):
     at = lax.axis_index(axis)
-    lead_up = lax.axis_index("dp") % 2 == 0 if by_core else jnp.bool_(True)
     up_order = strides(axis)
     down_order = up_order[::-1]
     rounds = len(up_order)
-    own = [lead, last]
-    goes_up = [lead_up, jnp.logical_not(lead_up)]
-    sent = [lead, last]
-    total = [lead, last]
-    sums = [None, None]
+    count = len(pieces)
+    rows = pieces[-1].shape[0]
+    here_up = lax.axis_index("dp") % 2 == 0 if by_core else jnp.bool_(True)
+    first_half = [p < count // 2 for p in range(count)]
+    goes_up = [here_up if first else jnp.logical_not(here_up) for first in first_half]
+    sent = list(pieces)
+    total = list(pieces)
+    sums = [None] * count
     result = None
     for k in range(rounds):
-        up, down = up_order[k], down_order[k]
-        got = [
-            swap_by_core(sent[0], axis, up, down if by_core else up),
-            swap_by_core(sent[1], axis, down, up if by_core else down),
-        ]
-        for p in range(2):
-            stride = jnp.where(goes_up[p], up, down)
+        orders = (up_order[k], down_order[k])
+        got = []
+        for p in range(count):
+            even, odd = orders if first_half[p] else orders[::-1]
+            got.append(swap_by_core(sent[p], axis, even, odd if by_core else even))
+        token = None
+        for p in range(count):
+            if p:
+                got[p], _ = lax.optimization_barrier((got[p], token))
+            stride = jnp.where(goes_up[p], *orders)
             after_partner = ((at & stride) == 0) if reverse else ((at & stride) != 0)
             total[p] = total[p] + got[p]
             if k == 0:
@@ -241,25 +247,23 @@
             else:
                 keep = jnp.logical_or(after_partner, jnp.logical_not(goes_up[p]))
                 sums[p] = sums[p] + jnp.where(keep, got[p], 0.0)
+            token = sums[p]
             if k < rounds - 1:
                 next_down = down_order[k + 1]
                 serves = ((at & next_down) != 0) if reverse else ((at & next_down) == 0)
-                partial = sums[p] + jnp.where(serves, own[p], 0.0)
+                partial = sums[p] + jnp.where(serves, pieces[p], 0.0)
                 whole = goes_up[p]
-                if own[p].shape[0] > last.shape[0]:
-                    extra = lax.broadcasted_iota(jnp.int32, own[p].shape, 0) >= last.shape[0]
+                if pieces[p].shape[0] > rows:
+                    extra = lax.broadcasted_iota(jnp.int32, pieces[p].shape, 0) >= rows
                     whole = jnp.logical_or(whole, extra)
-                sent[p] = jnp.where(whole, total[p], partial)
-            if p == 0:
-                token = sums[0]
-                if k == 0:
-                    token, result = between(sent[0])
-                elif finish is not None and k < rounds - 1:
-                    result = result + got[0][last.shape[0] :]
-                elif finish is not None:
-                    token, result = finish(sums[0], got[0], result)
-                got[1], _ = lax.optimization_barrier((got[1], token))
-    return sums[0], sums[1], result
+                token = sent[p] = jnp.where(whole, total[p], partial)
+            if p == 0 and k == 0:
+                token, result = between(sent[0])
+            elif finish is not None and k == rounds - 1:
+                token, result = finish(p, sums, got, result)
+            elif finish is not None and p == 0:
+                result = result + got[0][rows:]
+    return sums, result
 
 
 def per_device(queries, keys, values, spikes, gain, upstream):
@@ -271,15 +275,16 @@
     gain_row = gain.reshape(1, width_dev)
     shape = jax.ShapeDtypeStruct
     flat = (tok, width_dev)
-    piece = shape((half * DH, DH), F32)
+    piece = shape((DH, DH), F32)
+    half_piece = shape((half * DH, DH), F32)
     longer = shape((half * DH + GAIN_ROWS, DH), F32)
     whole = shape((1, tok, width_dev), BF16)
     small = 2 * heads * tok * DH * DH
     big = 2 * heads * tok * tok * DH
 
-    held_queries, held_values, upper, held_gain, spiked, state_a, state_b = call(
+    held_queries, held_values, upper, held_gain, spiked, *states = call(
         state_kernel,
-        [whole, whole, whole, shape((1, width_dev), F32), shape(flat, BF16), piece, piece],
+        [whole, whole, whole, shape((1, width_dev), F32), shape(flat, BF16)] + [piece] * heads,
         queries, keys, spikes, values, upstream, gain_row,
         hbm=(0, 1, 2, 3, 4, 5),
         scratch=[
@@ -289,28 +294,28 @@
         ],
         flops=small, moved=2**20,
     )
-    scores, intra = call(
-        scores_kernel,
-        [shape((heads, tok, tok), BF16), shape(flat, F32)],
-        held_queries, spiked, held_values,
-        flops=2 * big, moved=2**21,
-    )
-
     def scale(total):
+        late, _ = lax.optimization_barrier((spiked, total))
         scaled = call(scale_kernel, [shape(flat, F32)], upper, held_gain, total, moved=2**20)[0]
-        return scaled, scaled
-
-    prior_a, prior_b, scaled = scan_pair(state_a, state_b, "ctx", False, True, scale)
+        scores, intra = call(
+            scores_kernel,
+            [shape((heads, tok, tok), BF16), shape(flat, F32)],
+            held_queries, late, held_values,
+            flops=2 * big, moved=2**21,
+        )
+        return scaled, (scaled, scores, intra)
+
+    priors, (scaled, scores, intra) = scan(states, "ctx", False, True, scale)
     attended, prior, sums = call(
         attend_kernel,
         [shape(flat, F32), shape((heads, DH, DH), BF16), shape((2, tok), F32)],
-        held_queries, intra, scaled, prior_a, prior_b,
+        held_queries, intra, scaled, *priors,
         flops=small, moved=2**21,
     )
     sums = gathered_sum(sums, "head")
-    grad, local_a, local_b = call(
+    grad, *locals_ = call(
         functools.partial(grad_kernel, width),
-        [shape(flat, BF16), longer, piece],
+        [shape(flat, BF16), longer, half_piece],
         held_queries, attended, scaled, upper, sums,
         flops=small, moved=2**21,
     )
@@ -327,25 +332,25 @@
         rows = call(tail_kernel, [shape((GAIN_ROWS, DH), F32)], total)[0]
         return rows, rows
 
-    def finish(later_a, got, gain_before):
-        gain_here = gain_before + got[half * DH :]
+    def finish(p, sums, got, result):
+        if p:
+            return sums[p], result
+        gain_here = result + got[0][half * DH :]
         gain_there = swap(gain_here, "dp", 1)
         first = call(
             final_first_kernel,
             [shape((1, tok, half * DH), BF16)] * 2,
-            held_values, spiked, spikes, *parts[:2], later_a,
+            held_values, spiked, spikes, *parts[:2], sums[0],
             flops=small, moved=2**21,
         )
         return (first[0], gain_there), (gain_here, gain_there, *first)
 
-    _, later_b, (gain_here, gain_there, *first) = scan_pair(
-        local_a, local_b, "ctx", True, False, gain_rows, finish
-    )
+    later, ends = scan(locals_, "ctx", True, False, gain_rows, finish)
     total_tokens = tok * lax.axis_size("ctx") * lax.axis_size("dp")
     grad_key, grad_value, grad_gain = call(
         functools.partial(final_last_kernel, 1.0 / math.sqrt(total_tokens)),
         [whole, whole, shape((1, width_dev), F32)],
-        held_values, spiked, spikes, *parts[2:], later_b, gain_here, gain_there, *first,
+        held_values, spiked, spikes, *parts[2:], *ends, later[1],
         flops=small, moved=2**21,
     )
     return grad_query, grad_key, grad_value, grad_gain.reshape(width_dev)

time: 44.8 us -> 43.9 us (0.980)
  waiting for transfers between devices: 19.4 us -> 14.4 us
  starting transfers between devices: 18.1 us -> 22.2 us
    ppermute x8 -> x12, waiting for transfers between devices: 15.3 us -> 10.5 us  [swap_by_core(): return lax.ppermute(array, ('dp', axis), pairs)]
    ppermute x8 -> x12, starting transfers between devices: 14.5 us -> 18.6 us  [swap_by_core(): return lax.ppermute(array, ('dp', axis), pairs)]
  transfers between devices with their start and end apart: 12 -> 16, of which waited for: 8 -> 10; matrix products, arithmetic and copies ran while one was open for 0% -> 0% of each run, Pallas kernels for 6% -> 7%
where the time goes in v5:
time: 43.9 us; the launch traced here: 43.7 us
  starting transfers between devices  22.2 us (51%)
  waiting for transfers between devices  14.4 us (33%)
  Pallas kernels  6.19 us (14%)
  between operations  0.8 us (2%)
    ppermute x12, starting transfers between devices, swap_by_core(): return lax.ppermute(array, ('dp', axis), pairs)  18.6 us
    ppermute x12, waiting for transfers between devices, swap_by_core(): return lax.ppermute(array, ('dp', axis), pairs)  10.5 us
    pallas_call x9, Pallas kernels, call(): pl.pallas_call(body, out_shape=outs, in_specs=[HBM if k in hbm else VMEM...  6.19 us
    ppermute x4, waiting for transfers between devices, swap(): return lax.ppermute(array, axis, [(i, i ^ stride) for i in range(size)])  3.83 us
    ppermute x4, starting transfers between devices, swap(): return lax.ppermute(array, axis, [(i, i ^ stride) for i in range(size)])  3.55 us
  transfers between devices with their start and end apart: 16, of which 10 were waited for; matrix products, arithmetic and copies ran while one was open for 0% of the time, Pallas kernels for 7%

profile of v5, /device:TPU:0, one launch (start us, length us, event | category | flops | bytes accessed | tf_op | source)
XLA Modules:
  0.0 43.7 jit_solution(13825388733563374050)
XLA Ops:
  0.6 1.5 %shard_map.93 = (bf16[1,256,512]{2,1,0:T(8,128)(2,1)S(1)}, bf16[1,256,512]{2,1,0:T(8,128)(2,1)S(1)}, bf16[1,256,512]{2,1,0:T(8,128)(2,1)S(1)}, f32[1,512]{1,0:T(...) custom-call(bf16[1,256,512]{2,1,0:T(8,128)(2,1)} %queries.1, ...), custom_call_target="tpu_custom_call" | custom-call | flops 33554432 | bytes 1048576 | tf_op jit(solution)/shard_map/pallas_call | solution.py:40
  2.2 3.1 %collective-permute-start = (f32[128,128]{1,0:T(8,128)S(1)}, f32[128,128]{1,0:T(8,128)S(1)}, u32[]{:S(2)}, u32[]{:S(2)}) collective-permute-start(f32[128,128]{1,0:T(8,128)S(1)} %get-tuple-element.47), channel_id=1, source_target_pairs={{0,4},{4,0},{8,12},{12,8},{16,24},{20,28},{24,16},{28,20},{1,5},{5... | collective-permute-start | bytes 196616 | tf_op jit(solution)/shard_map/ppermute | solution.py:215
  5.3 0.1 collective-permute-start.2
  5.3 3.0 %collective-permute-start.4 = (f32[128,128]{1,0:T(8,128)S(1)}, f32[128,128]{1,0:T(8,128)S(1)}, u32[]{:S(2)}, u32[]{:S(2)}) collective-permute-start(f32[128,128]{1,0:T(8,128)S(1)} %get-tuple-element.55), channel_id=1, source_target_pairs={{0,8},{4,12},{8,0},{12,4},{16,20},{20,16},{24,28},{28,24},{1,9},{5... | collective-permute-start | bytes 196616 | tf_op jit(solution)/shard_map/ppermute | solution.py:215
  8.3 0.0 collective-permute-start.6
  8.3 3.0 %collective-permute-start.1 = (f32[128,128]{1,0:T(8,128)S(1)}, f32[128,128]{1,0:T(8,128)S(1)}, u32[]{:S(2)}, u32[]{:S(2)}) collective-permute-start(f32[128,128]{1,0:T(8,128)S(1)} %add_select_fusion.3.after), channel_id=1, source_target_pairs={{0,8},{4,12},{8,0},{12,4},{16,20},{20,16},{24,28},{28,24},{1,9},{5... | collective-permute-start | bytes 196616 | tf_op jit(solution)/shard_map/ppermute | solution.py:215
  11.3 0.3 collective-permute-done.2
  11.6 1.2 %collective-permute-start.3 = (f32[128,128]{1,0:T(8,128)S(1)}, f32[128,128]{1,0:T(8,128)S(1)}, u32[]{:S(2)}, u32[]{:S(2)}) collective-permute-start(f32[128,128]{1,0:T(8,128)S(1)} %add_select_fusion.2), channel_id=1, source_target_pairs={{0,8},{4,12},{8,0},{12,4},{16,20},{20,16},{24,28},{28,24},{1,9},{5... | collective-permute-start | bytes 196616 | tf_op jit(solution)/shard_map/ppermute | solution.py:215
  12.8 2.7 %collective-permute-start.5 = (f32[128,128]{1,0:T(8,128)S(1)}, f32[128,128]{1,0:T(8,128)S(1)}, u32[]{:S(2)}, u32[]{:S(2)}) collective-permute-start(f32[128,128]{1,0:T(8,128)S(1)} %add_select_fusion.1), channel_id=1, source_target_pairs={{0,4},{4,0},{8,12},{12,8},{16,24},{20,28},{24,16},{28,20},{1,5},{5... | collective-permute-start | bytes 196616 | tf_op jit(solution)/shard_map/ppermute | solution.py:215
  15.6 0.3 collective-permute-start.7
  15.9 0.7 %shard_map.94 = (bf16[4,256,256]{2,1,0:T(8,128)(2,1)S(1)}, f32[256,512]{1,0:T(8,128)S(1)}) custom-call(bf16[1,256,512]{2,1,0:T(8,128)(2,1)S(1)} %get-tuple-element.44.queries, bf16[256,512]{1,0:T(8,128)(2,1)S(1)} %get-tuple-element.48.spiked, bf16[1,256,512]{2,1,0:T(8,128)(2,1)S(1)} %get-tuple-element.46.values), custom_call_target="tpu_custom_call" | custom-call | flops 134217728 | bytes 2097152 | tf_op jit(solution)/shard_map/pallas_call | solution.py:40
  16.6 3.5 %collective-permute-done.3 = f32[128,128]{1,0:T(8,128)S(1)} collective-permute-done((f32[128,128]{1,0:T(8,128)S(1)}, f32[128,128]{1,0:T(8,128)S(1)}, u32[]{:S(2)}, u32[]{:S(2)}) %collective-permute-start.3) | collective-permute-done | bytes 65568 | tf_op jit(solution)/shard_map/ppermute | solution.py:215
  20.1 0.7 %collective-permute-done.7 = f32[128,128]{1,0:T(8,128)S(1)} collective-permute-done((f32[128,128]{1,0:T(8,128)S(1)}, f32[128,128]{1,0:T(8,128)S(1)}, u32[]{:S(2)}, u32[]{:S(2)}) %collective-permute-start.7) | collective-permute-done | bytes 65568 | tf_op jit(solution)/shard_map/ppermute | solution.py:215
  20.8 0.4 shard_map.96
  21.1 2.5 %collective-permute-start.10 = (f32[2,256]{1,0:T(2,128)S(1)}, f32[2,256]{1,0:T(2,128)S(1)}, u32[]{:S(2)}, u32[]{:S(2)}) collective-permute-start(f32[2,256]{1,0:T(2,128)S(1)} %get-tuple-element.62), channel_id=1, source_target_pairs={{0,3},{1,2},{2,1},{3,0},{4,7},{5,6},{6,5},{7,4},{8,11},{9,10},{10,... | collective-permute-start | bytes 6152 | tf_op jit(solution)/shard_map/ppermute | solution.py:190
  23.6 0.5 %collective-permute-start.9 = (f32[2,256]{1,0:T(2,128)S(1)}, f32[2,256]{1,0:T(2,128)S(1)}, u32[]{:S(2)}, u32[]{:S(2)}) collective-permute-start(f32[2,256]{1,0:T(2,128)S(1)} %get-tuple-element.62), channel_id=1, source_target_pairs={{0,2},{1,3},{2,0},{3,1},{4,6},{5,7},{6,4},{7,5},{8,10},{9,11},{10,... | collective-permute-start | bytes 6152 | tf_op jit(solution)/shard_map/ppermute | solution.py:190
  24.1 0.5 %collective-permute-start.8 = (f32[2,256]{1,0:T(2,128)S(1)}, f32[2,256]{1,0:T(2,128)S(1)}, u32[]{:S(2)}, u32[]{:S(2)}) collective-permute-start(f32[2,256]{1,0:T(2,128)S(1)} %get-tuple-element.62), channel_id=1, source_target_pairs={{0,1},{1,0},{2,3},{3,2},{4,5},{5,4},{6,7},{7,6},{8,9},{9,8},{10,11... | collective-permute-start | bytes 6152 | tf_op jit(solution)/shard_map/ppermute | solution.py:190
  24.7 1.0 %collective-permute-done.10 = f32[2,256]{1,0:T(2,128)S(1)} collective-permute-done((f32[2,256]{1,0:T(2,128)S(1)}, f32[2,256]{1,0:T(2,128)S(1)}, u32[]{:S(2)}, u32[]{:S(2)}) %collective-permute-start.10) | collective-permute-done | bytes 2080 | tf_op jit(solution)/shard_map/ppermute | solution.py:190
  25.7 1.5 %collective-permute-done.9 = f32[2,256]{1,0:T(2,128)S(1)} collective-permute-done((f32[2,256]{1,0:T(2,128)S(1)}, f32[2,256]{1,0:T(2,128)S(1)}, u32[]{:S(2)}, u32[]{:S(2)}) %collective-permute-start.9) | collective-permute-done | bytes 2080 | tf_op jit(solution)/shard_map/ppermute | solution.py:190
  27.2 0.5 %collective-permute-done.8 = f32[2,256]{1,0:T(2,128)S(1)} collective-permute-done((f32[2,256]{1,0:T(2,128)S(1)}, f32[2,256]{1,0:T(2,128)S(1)}, u32[]{:S(2)}, u32[]{:S(2)}) %collective-permute-start.8) | collective-permute-done | bytes 2080 | tf_op jit(solution)/shard_map/ppermute | solution.py:190
  27.7 0.4 shard_map.97
  28.2 0.1 collective-permute-start.11
  28.2 2.7 %collective-permute-start.14 = (f32[256,128]{1,0:T(8,128)S(1)}, f32[256,128]{1,0:T(8,128)S(1)}, u32[]{:S(2)}, u32[]{:S(2)}) collective-permute-start(f32[256,128]{1,0:T(8,128)S(1)} %get-tuple-element.78), channel_id=1, source_target_pairs={{0,8},{4,12},{8,0},{12,4},{16,24},{20,28},{24,16},{28,20},{1,9},{5... | collective-permute-start | bytes 393224 | tf_op jit(solution)/shard_map/ppermute | solution.py:215
  30.9 1.9 %shard_map.98 = (bf16[1,256,512]{2,1,0:T(8,128)(2,1)}, f32[256,256]{1,0:T(8,128)S(1)}, f32[256,256]{1,0:T(8,128)S(1)}, f32[256,256]{1,0:T(8,128)S(1)}, f32[256,256]{1,0:T(8,128)S(1)}) custom-call(bf16[1,256,512]{2,1,0:T(8,128)(2,1)S(1)} %get-tuple-element.44.queries, bf16[256,512]{1,0:T(8,128)(2,1)S(1)} %get-tuple-element.48.spiked, ...), custom_call_target="tpu_custom_call" | custom-call | flops 268435456 | bytes 4194304 | tf_op jit(solution)/shard_map/pallas_call | solution.py:40
  32.9 2.0 %collective-permute-done.11 = f32[264,128]{1,0:T(8,128)S(1)} collective-permute-done((f32[264,128]{1,0:T(8,128)S(1)}, f32[264,128]{1,0:T(8,128)S(1)}, u32[]{:S(2)}, u32[]{:S(2)}) %collective-permute-start.11) | collective-permute-done | bytes 135200 | tf_op jit(solution)/shard_map/ppermute | solution.py:215
  34.9 0.1 collective-permute-start.12
  35.0 2.4 %collective-permute-start.15 = (f32[256,128]{1,0:T(8,128)S(1)}, f32[256,128]{1,0:T(8,128)S(1)}, u32[]{:S(2)}, u32[]{:S(2)}) collective-permute-start(f32[256,128]{1,0:T(8,128)S(1)} %select_add_fusion.1), channel_id=1, source_target_pairs={{0,4},{4,0},{8,12},{12,8},{16,20},{20,16},{24,28},{28,24},{1,5},{5... | collective-permute-start | bytes 393224 | tf_op jit(solution)/shard_map/ppermute | solution.py:215
  37.5 4.0 %collective-permute-done.12 = f32[264,128]{1,0:T(8,128)S(1)} collective-permute-done((f32[264,128]{1,0:T(8,128)S(1)}, f32[264,128]{1,0:T(8,128)S(1)}, u32[]{:S(2)}, u32[]{:S(2)}) %collective-permute-start.12) | collective-permute-done | bytes 135200 | tf_op jit(solution)/shard_map/ppermute | solution.py:215
  41.6 0.2 shard_map.100
  41.8 0.1 collective-permute-done.15
  41.9 0.8 %collective-permute-done.13.gain_there = f32[8,128]{1,0:T(8,128)S(1)} collective-permute-done((f32[8,128]{1,0:T(8,128)S(1)}, f32[8,128]{1,0:T(8,128)S(1)}, u32[]{:S(2)}, u32[]{:S(2)}) %collective-permute-start.13) | collective-permute-done | bytes 4128 | tf_op jit(solution)/shard_map/ppermute | solution.py:190
  42.7 1.0 %shard_map.101 = (bf16[1,256,512]{2,1,0:T(8,128)(2,1)}, bf16[1,256,512]{2,1,0:T(8,128)(2,1)}, f32[1,512]{1,0:T(1,128)}) custom-call(bf16[1,256,512]{2,1,0:T(8,128)(2,1)S(1)} %get-tuple-element.46.values, bf16[256,512]{1,0:T(8,128)(2,1)S(1)} %get-tuple-element.48.spiked, s32[1,256,512]{2,1,0:T(8,128)S(1)} %copy-done, ...), custom_call_target="tpu_custom_call" | custom-call | flops 33554432 | bytes 2097152 | tf_op jit(solution)/shard_map/pallas_call | solution.py:40
  (27 shorter events, 0.3 us)
Async XLA Ops:
  2.2 6.2 %collective-permute-start = (f32[128,128]{1,0:T(8,128)S(1)}, f32[128,128]{1,0:T(8,128)S(1)}, u32[]{:S(2)}, u32[]{:S(2)}) collective-permute-start(f32[128,128]{1,0:T(8,128)S(1)} %get-tuple-element.47), channel_id=1, source_target_pairs={{0,4},{4,0},{8,12},{12,8},{16,24},{20,28},{24,16},{28,20},{1,5},{5... | collective-permute-start | bytes 196616 | tf_op jit(solution)/shard_map/ppermute | solution.py:215
  5.3 6.4 %collective-permute-start.2 = (f32[128,128]{1,0:T(8,128)S(1)}, f32[128,128]{1,0:T(8,128)S(1)}, u32[]{:S(2)}, u32[]{:S(2)}) collective-permute-start(f32[128,128]{1,0:T(8,128)S(1)} %get-tuple-element.52), channel_id=1, source_target_pairs={{0,4},{4,0},{8,12},{12,8},{16,24},{20,28},{24,16},{28,20},{1,5},{5... | collective-permute-start | bytes 196616 | tf_op jit(solution)/shard_map/ppermute | solution.py:215
  5.3 7.5 %collective-permute-start.4 = (f32[128,128]{1,0:T(8,128)S(1)}, f32[128,128]{1,0:T(8,128)S(1)}, u32[]{:S(2)}, u32[]{:S(2)}) collective-permute-start(f32[128,128]{1,0:T(8,128)S(1)} %get-tuple-element.55), channel_id=1, source_target_pairs={{0,8},{4,12},{8,0},{12,4},{16,20},{20,16},{24,28},{28,24},{1,9},{5... | collective-permute-start | bytes 196616 | tf_op jit(solution)/shard_map/ppermute | solution.py:215
  8.3 7.3 %collective-permute-start.6 = (f32[128,128]{1,0:T(8,128)S(1)}, f32[128,128]{1,0:T(8,128)S(1)}, u32[]{:S(2)}, u32[]{:S(2)}) collective-permute-start(f32[128,128]{1,0:T(8,128)S(1)} %get-tuple-element.58), channel_id=1, source_target_pairs={{0,8},{4,12},{8,0},{12,4},{16,20},{20,16},{24,28},{28,24},{1,9},{5... | collective-permute-start | bytes 196616 | tf_op jit(solution)/shard_map/ppermute | solution.py:215
  8.3 8.2 %collective-permute-start.1 = (f32[128,128]{1,0:T(8,128)S(1)}, f32[128,128]{1,0:T(8,128)S(1)}, u32[]{:S(2)}, u32[]{:S(2)}) collective-permute-start(f32[128,128]{1,0:T(8,128)S(1)} %add_select_fusion.3.after), channel_id=1, source_target_pairs={{0,8},{4,12},{8,0},{12,4},{16,20},{20,16},{24,28},{28,24},{1,9},{5... | collective-permute-start | bytes 196616 | tf_op jit(solution)/shard_map/ppermute | solution.py:215
  11.6 8.4 %collective-permute-start.3 = (f32[128,128]{1,0:T(8,128)S(1)}, f32[128,128]{1,0:T(8,128)S(1)}, u32[]{:S(2)}, u32[]{:S(2)}) collective-permute-start(f32[128,128]{1,0:T(8,128)S(1)} %add_select_fusion.2), channel_id=1, source_target_pairs={{0,8},{4,12},{8,0},{12,4},{16,20},{20,16},{24,28},{28,24},{1,9},{5... | collective-permute-start | bytes 196616 | tf_op jit(solution)/shard_map/ppermute | solution.py:215
  12.8 7.2 %collective-permute-start.5 = (f32[128,128]{1,0:T(8,128)S(1)}, f32[128,128]{1,0:T(8,128)S(1)}, u32[]{:S(2)}, u32[]{:S(2)}) collective-permute-start(f32[128,128]{1,0:T(8,128)S(1)} %add_select_fusion.1), channel_id=1, source_target_pairs={{0,4},{4,0},{8,12},{12,8},{16,24},{20,28},{24,16},{28,20},{1,5},{5... | collective-permute-start | bytes 196616 | tf_op jit(solution)/shard_map/ppermute | solution.py:215
  15.6 5.2 %collective-permute-start.7 = (f32[128,128]{1,0:T(8,128)S(1)}, f32[128,128]{1,0:T(8,128)S(1)}, u32[]{:S(2)}, u32[]{:S(2)}) collective-permute-start(f32[128,128]{1,0:T(8,128)S(1)} %add_select_fusion), channel_id=1, source_target_pairs={{0,4},{4,0},{8,12},{12,8},{16,24},{20,28},{24,16},{28,20},{1,5},{5... | collective-permute-start | bytes 196616 | tf_op jit(solution)/shard_map/ppermute | solution.py:215
  21.1 4.5 %collective-permute-start.10 = (f32[2,256]{1,0:T(2,128)S(1)}, f32[2,256]{1,0:T(2,128)S(1)}, u32[]{:S(2)}, u32[]{:S(2)}) collective-permute-start(f32[2,256]{1,0:T(2,128)S(1)} %get-tuple-element.62), channel_id=1, source_target_pairs={{0,3},{1,2},{2,1},{3,0},{4,7},{5,6},{6,5},{7,4},{8,11},{9,10},{10,... | collective-permute-start | bytes 6152 | tf_op jit(solution)/shard_map/ppermute | solution.py:190
  23.6 3.6 %collective-permute-start.9 = (f32[2,256]{1,0:T(2,128)S(1)}, f32[2,256]{1,0:T(2,128)S(1)}, u32[]{:S(2)}, u32[]{:S(2)}) collective-permute-start(f32[2,256]{1,0:T(2,128)S(1)} %get-tuple-element.62), channel_id=1, source_target_pairs={{0,2},{1,3},{2,0},{3,1},{4,6},{5,7},{6,4},{7,5},{8,10},{9,11},{10,... | collective-permute-start | bytes 6152 | tf_op jit(solution)/shard_map/ppermute | solution.py:190
  24.1 3.6 %collective-permute-start.8 = (f32[2,256]{1,0:T(2,128)S(1)}, f32[2,256]{1,0:T(2,128)S(1)}, u32[]{:S(2)}, u32[]{:S(2)}) collective-permute-start(f32[2,256]{1,0:T(2,128)S(1)} %get-tuple-element.62), channel_id=1, source_target_pairs={{0,1},{1,0},{2,3},{3,2},{4,5},{5,4},{6,7},{7,6},{8,9},{9,8},{10,11... | collective-permute-start | bytes 6152 | tf_op jit(solution)/shard_map/ppermute | solution.py:190
  28.2 6.7 %collective-permute-start.11 = (f32[264,128]{1,0:T(8,128)S(1)}, f32[264,128]{1,0:T(8,128)S(1)}, u32[]{:S(2)}, u32[]{:S(2)}) collective-permute-start(f32[264,128]{1,0:T(8,128)S(1)} %get-tuple-element.73), channel_id=1, source_target_pairs={{0,4},{4,0},{8,12},{12,8},{16,20},{20,16},{24,28},{28,24},{1,5},{5... | collective-permute-start | bytes 405512 | tf_op jit(solution)/shard_map/ppermute | solution.py:215
  28.2 6.8 %collective-permute-start.14 = (f32[256,128]{1,0:T(8,128)S(1)}, f32[256,128]{1,0:T(8,128)S(1)}, u32[]{:S(2)}, u32[]{:S(2)}) collective-permute-start(f32[256,128]{1,0:T(8,128)S(1)} %get-tuple-element.78), channel_id=1, source_target_pairs={{0,8},{4,12},{8,0},{12,4},{16,24},{20,28},{24,16},{28,20},{1,9},{5... | collective-permute-start | bytes 393224 | tf_op jit(solution)/shard_map/ppermute | solution.py:215
  34.9 6.6 %copy-start = (s32[1,256,512]{2,1,0:T(8,128)S(1)}, s32[1,256,512]{2,1,0:T(8,128)}, u32[]{:S(2)}) copy-start(s32[1,256,512]{2,1,0:T(8,128)} %spikes.5) | copy-start | bytes 1572868
  34.9 6.6 %collective-permute-start.12 = (f32[264,128]{1,0:T(8,128)S(1)}, f32[264,128]{1,0:T(8,128)S(1)}, u32[]{:S(2)}, u32[]{:S(2)}) collective-permute-start(f32[264,128]{1,0:T(8,128)S(1)} %add.82.total), channel_id=1, source_target_pairs={{0,8},{4,12},{8,0},{12,4},{16,24},{20,28},{24,16},{28,20},{1,9},{5... | collective-permute-start | bytes 405512 | tf_op jit(solution)/shard_map/ppermute | solution.py:215
  35.0 6.8 %collective-permute-start.15 = (f32[256,128]{1,0:T(8,128)S(1)}, f32[256,128]{1,0:T(8,128)S(1)}, u32[]{:S(2)}, u32[]{:S(2)}) collective-permute-start(f32[256,128]{1,0:T(8,128)S(1)} %select_add_fusion.1), channel_id=1, source_target_pairs={{0,4},{4,0},{8,12},{12,8},{16,20},{20,16},{24,28},{28,24},{1,5},{5... | collective-permute-start | bytes 393224 | tf_op jit(solution)/shard_map/ppermute | solution.py:215
  41.5 1.2 %collective-permute-start.13 = (f32[8,128]{1,0:T(8,128)S(1)}, f32[8,128]{1,0:T(8,128)S(1)}, u32[]{:S(2)}, u32[]{:S(2)}) collective-permute-start(f32[8,128]{1,0:T(8,128)S(1)} %slice_add_fusion.gain_here), channel_id=1, source_target_pairs={{0,16},{16,0},{1,17},{17,1},{2,18},{18,2},{3,19},{19,3},{4,20},{20... | collective-permute-start | bytes 12296 | tf_op jit(solution)/shard_map/ppermute | solution.py:190

commit v6 on v5

--- a/solution.py
+++ b/solution.py
@@ -53,43 +53,72 @@
     return rows >= lax.broadcasted_iota(jnp.int32, (tok, tok), 1)
 
 
-def state_kernel(
-    queries, keys, spikes, values, upstream, gain,
-    held_queries, held_values, upper, held_gain, spiked, *rest,
-):
-    *states, key_buf, spike_buf, sems = rest
-    heads = spiked.shape[1] // DH
-    pairs = (
-        (keys, key_buf), (spikes, spike_buf), (values, held_values),
-        (queries, held_queries), (upstream, upper), (gain, held_gain),
-    )
-    copies = [pltpu.make_async_copy(src, dst, sems.at[k]) for k, (src, dst) in enumerate(pairs)]
+def fetch(pairs, sems, first=0):
+    copies = [
+        pltpu.make_async_copy(src, dst, sems.at[first + k]) for k, (src, dst) in enumerate(pairs)
+    ]
     for copy in copies:
         copy.start()
-    for copy in copies[:3]:
+    return copies
+
+
+def mask_keys(keys, spikes, spiked):
+    for h in range(spiked.shape[1] // DH):
+        spiked[:, cols(h)] = keys[0, :, cols(h)] * spikes[0, :, cols(h)].astype(F32).astype(BF16)
+
+
+def is_last_block():
+    return lax.axis_index("ctx") == lax.axis_size("ctx") - 1
+
+
+def state_kernel(keys, spikes, values, held_values, spiked, *rest):
+    *states, key_buf, spike_buf, sems = rest
+
+    @pl.when(is_last_block())
+    def _():
+        for state in states:
+            state[...] = jnp.zeros(state.shape, F32)
+
+    @pl.when(jnp.logical_not(is_last_block()))
+    def _():
+        pairs = ((keys, key_buf), (spikes, spike_buf), (values, held_values))
+        for copy in fetch(pairs, sems):
+            copy.wait()
+        mask_keys(key_buf, spike_buf, spiked)
+        for h in range(spiked.shape[1] // DH):
+            ref, rows = block_of(states, h)
+            ref[rows, :] = dot(spiked[:, cols(h)], held_values[0, :, cols(h)], 0, 0)
+
+
+def scores_kernel(
+    queries, upstream, gain, keys, spikes, values, values_in, spiked_in,
+    held_queries, upper, held_values, spiked, scores, intra, scaled,
+    key_buf, spike_buf, gain_buf, sems,
+):
+    copies = fetch(((queries, held_queries), (upstream, upper), (gain, gain_buf)), sems)
+
+    @pl.when(is_last_block())
+    def _():
+        pairs = ((keys, key_buf), (spikes, spike_buf), (values, held_values))
+        for copy in fetch(pairs, sems, 3):
+            copy.wait()
+        mask_keys(key_buf, spike_buf, spiked)
+
+    @pl.when(jnp.logical_not(is_last_block()))
+    def _():
+        held_values[...] = values_in[...]
+        spiked[...] = spiked_in[...]
+
+    for copy in copies:
         copy.wait()
-    for h in range(heads):
-        block = key_buf[0, :, cols(h)] * spike_buf[0, :, cols(h)].astype(F32).astype(BF16)
-        spiked[:, cols(h)] = block
-        ref, rows = block_of(states, h)
-        ref[rows, :] = dot(block, held_values[0, :, cols(h)], 0, 0)
-    for copy in copies[3:]:
-        copy.wait()
-
-
-def scores_kernel(queries, spiked, values, scores, intra):
     heads, tok, _ = scores.shape
     causal = causal_mask(tok)
     for h in range(heads):
-        raw = dot(queries[0, :, cols(h)], spiked[:, cols(h)], 1, 1)
+        raw = dot(held_queries[0, :, cols(h)], spiked[:, cols(h)], 1, 1)
         block = jnp.where(causal, raw, 0.0).astype(BF16)
         scores[h] = block
-        intra[:, cols(h)] = dot(block, values[0, :, cols(h)], 1, 0)
-
-
-def scale_kernel(upper, gain, after, scaled):
-    del after
-    scaled[...] = upper[0].astype(F32) * gain[...]
+        intra[:, cols(h)] = dot(block, held_values[0, :, cols(h)], 1, 0)
+    scaled[...] = upper[0].astype(F32) * gain_buf[...]
 
 
 def attend_kernel(queries, intra, scaled, *rest):
@@ -282,30 +311,42 @@
     small = 2 * heads * tok * DH * DH
     big = 2 * heads * tok * tok * DH
 
-    held_queries, held_values, upper, held_gain, spiked, *states = call(
+    early_values, early_spiked, *states = call(
         state_kernel,
-        [whole, whole, whole, shape((1, width_dev), F32), shape(flat, BF16)] + [piece] * heads,
-        queries, keys, spikes, values, upstream, gain_row,
-        hbm=(0, 1, 2, 3, 4, 5),
+        [whole, shape(flat, BF16)] + [piece] * heads,
+        keys, spikes, values,
+        hbm=(0, 1, 2),
         scratch=[
             pltpu.VMEM((1, *flat), BF16),
             pltpu.VMEM((1, *flat), jnp.int32),
-            pltpu.SemaphoreType.DMA((6,)),
+            pltpu.SemaphoreType.DMA((3,)),
         ],
         flops=small, moved=2**20,
     )
-    def scale(total):
-        late, _ = lax.optimization_barrier((spiked, total))
-        scaled = call(scale_kernel, [shape(flat, F32)], upper, held_gain, total, moved=2**20)[0]
-        scores, intra = call(
+
+    def score(total):
+        late, _ = lax.optimization_barrier((early_spiked, total))
+        outs = call(
             scores_kernel,
-            [shape((heads, tok, tok), BF16), shape(flat, F32)],
-            held_queries, late, held_values,
+            [
+                whole, whole, whole, shape(flat, BF16),
+                shape((heads, tok, tok), BF16), shape(flat, F32), shape(flat, F32),
+            ],
+            queries, upstream, gain_row, keys, spikes, values, early_values, late,
+            hbm=(0, 1, 2, 3, 4, 5),
+            scratch=[
+                pltpu.VMEM((1, *flat), BF16),
+                pltpu.VMEM((1, *flat), jnp.int32),
+                pltpu.VMEM((1, width_dev), F32),
+                pltpu.SemaphoreType.DMA((6,)),
+            ],
             flops=2 * big, moved=2**21,
         )
-        return scaled, (scaled, scores, intra)
-
-    priors, (scaled, scores, intra) = scan(states, "ctx", False, True, scale)
+        return total, outs
+
+    priors, (held_queries, upper, held_values, spiked, scores, intra, scaled) = scan(
+        states, "ctx", False, True, score
+    )
     attended, prior, sums = call(
         attend_kernel,
         [shape(flat, F32), shape((heads, DH, DH), BF16), shape((2, tok), F32)],

time: 43.9 us -> 44 us (level)
  starting transfers between devices: 22.2 us -> 18.1 us
  waiting for transfers between devices: 14.4 us -> 17.5 us
  Pallas kernels: 6.19 us -> 7.25 us
    ppermute x12, starting transfers between devices: 18.6 us -> 14.5 us  [swap_by_core(): return lax.ppermute(array, ('dp', axis), pairs)]
    ppermute x12, waiting for transfers between devices: 10.5 us -> 14.4 us  [swap_by_core(): return lax.ppermute(array, ('dp', axis), pairs)]
    pallas_call x9 -> x8, Pallas kernels: 6.19 us -> 7.25 us  [call(): pl.pallas_call(body, out_shape=outs, in_specs=[HBM if k in hbm else VMEM...]
    ppermute x4, waiting for transfers between devices: 3.83 us -> 3.05 us  [swap(): return lax.ppermute(array, axis, [(i, i ^ stride) for i in range(size)])]
  transfers between devices with their start and end apart: 16 -> 16, of which waited for: 10 -> 11; matrix products, arithmetic and copies ran while one was open for 0% -> 0% of each run, Pallas kernels for 7% -> 9%
where the time goes in v6:
time: 44 us; the launch traced here: 43.8 us
  starting transfers between devices  18.1 us (41%)
  waiting for transfers between devices  17.5 us (40%)
  Pallas kernels  7.25 us (16%)
  between operations  0.78 us (2%)
    ppermute x12, starting transfers between devices, swap_by_core(): return lax.ppermute(array, ('dp', axis), pairs)  14.5 us
    ppermute x12, waiting for transfers between devices, swap_by_core(): return lax.ppermute(array, ('dp', axis), pairs)  14.4 us
    pallas_call x8, Pallas kernels, call(): pl.pallas_call(body, out_shape=outs, in_specs=[HBM if k in hbm else VMEM...  7.25 us
    ppermute x4, starting transfers between devices, swap(): return lax.ppermute(array, axis, [(i, i ^ stride) for i in range(size)])  3.55 us
    ppermute x4, waiting for transfers between devices, swap(): return lax.ppermute(array, axis, [(i, i ^ stride) for i in range(size)])  3.05 us
  transfers between devices with their start and end apart: 16, of which 11 were waited for; matrix products, arithmetic and copies ran while one was open for 0% of the time, Pallas kernels for 9%

profile of v6, /device:TPU:0, one launch (start us, length us, event | category | flops | bytes accessed | tf_op | source)
XLA Modules:
  0.0 43.8 jit_solution(6928869534182899879)
XLA Ops:
  0.6 1.5 %shard_map.93 = (bf16[1,256,512]{2,1,0:T(8,128)(2,1)S(1)}, bf16[256,512]{1,0:T(8,128)(2,1)S(1)}, f32[128,128]{1,0:T(8,128)S(1)}, f32[128,128]{1,0:T(8,128)S(1)},...) custom-call(bf16[1,256,512]{2,1,0:T(8,128)(2,1)} %keys.3, s32[1,256,512]{2,1,0:T(8,128)} %spikes.7, ...), custom_call_target="tpu_custom_call" | custom-call | flops 33554432 | bytes 1048576 | tf_op jit(solution)/shard_map/pallas_call | solution.py:40
  2.2 3.1 %collective-permute-start = (f32[128,128]{1,0:T(8,128)S(1)}, f32[128,128]{1,0:T(8,128)S(1)}, u32[]{:S(2)}, u32[]{:S(2)}) collective-permute-start(f32[128,128]{1,0:T(8,128)S(1)} %get-tuple-element.48), channel_id=1, source_target_pairs={{0,4},{4,0},{8,12},{12,8},{16,24},{20,28},{24,16},{28,20},{1,5},{5... | collective-permute-start | bytes 196616 | tf_op jit(solution)/shard_map/ppermute | solution.py:244
  5.3 0.1 collective-permute-start.2
  5.3 3.0 %collective-permute-start.4 = (f32[128,128]{1,0:T(8,128)S(1)}, f32[128,128]{1,0:T(8,128)S(1)}, u32[]{:S(2)}, u32[]{:S(2)}) collective-permute-start(f32[128,128]{1,0:T(8,128)S(1)} %get-tuple-element.58), channel_id=1, source_target_pairs={{0,8},{4,12},{8,0},{12,4},{16,20},{20,16},{24,28},{28,24},{1,9},{5... | collective-permute-start | bytes 196616 | tf_op jit(solution)/shard_map/ppermute | solution.py:244
  8.4 3.0 %collective-permute-start.1 = (f32[128,128]{1,0:T(8,128)S(1)}, f32[128,128]{1,0:T(8,128)S(1)}, u32[]{:S(2)}, u32[]{:S(2)}) collective-permute-start(f32[128,128]{1,0:T(8,128)S(1)} %add_select_fusion.3), channel_id=1, source_target_pairs={{0,8},{4,12},{8,0},{12,4},{16,20},{20,16},{24,28},{28,24},{1,9},{5... | collective-permute-start | bytes 196616 | tf_op jit(solution)/shard_map/ppermute | solution.py:244
  11.3 0.3 collective-permute-done.2
  11.7 0.4 collective-permute-start.3
  12.1 2.4 %collective-permute-start.5 = (f32[128,128]{1,0:T(8,128)S(1)}, f32[128,128]{1,0:T(8,128)S(1)}, u32[]{:S(2)}, u32[]{:S(2)}) collective-permute-start(f32[128,128]{1,0:T(8,128)S(1)} %add_select_fusion.1), channel_id=1, source_target_pairs={{0,4},{4,0},{8,12},{12,8},{16,24},{20,28},{24,16},{28,20},{1,5},{5... | collective-permute-start | bytes 196616 | tf_op jit(solution)/shard_map/ppermute | solution.py:244
  14.6 0.3 collective-permute-start.7
  14.9 1.8 %shard_map.94 = (bf16[1,256,512]{2,1,0:T(8,128)(2,1)S(1)}, bf16[1,256,512]{2,1,0:T(8,128)(2,1)S(1)}, bf16[1,256,512]{2,1,0:T(8,128)(2,1)S(1)}, bf16[256,512]{1,0...) custom-call(bf16[1,256,512]{2,1,0:T(8,128)(2,1)} %queries.1, ...), custom_call_target="tpu_custom_call" | custom-call | flops 134217728 | bytes 2097152 | tf_op jit(solution)/shard_map/pallas_call | solution.py:40
  16.6 1.3 %collective-permute-done.1 = f32[128,128]{1,0:T(8,128)S(1)} collective-permute-done((f32[128,128]{1,0:T(8,128)S(1)}, f32[128,128]{1,0:T(8,128)S(1)}, u32[]{:S(2)}, u32[]{:S(2)}) %collective-permute-start.1) | collective-permute-done | bytes 65568 | tf_op jit(solution)/shard_map/ppermute | solution.py:244
  18.0 1.7 %collective-permute-done.3 = f32[128,128]{1,0:T(8,128)S(1)} collective-permute-done((f32[128,128]{1,0:T(8,128)S(1)}, f32[128,128]{1,0:T(8,128)S(1)}, u32[]{:S(2)}, u32[]{:S(2)}) %collective-permute-start.3) | collective-permute-done | bytes 65568 | tf_op jit(solution)/shard_map/ppermute | solution.py:244
  19.7 0.8 %collective-permute-done.7 = f32[128,128]{1,0:T(8,128)S(1)} collective-permute-done((f32[128,128]{1,0:T(8,128)S(1)}, f32[128,128]{1,0:T(8,128)S(1)}, u32[]{:S(2)}, u32[]{:S(2)}) %collective-permute-start.7) | collective-permute-done | bytes 65568 | tf_op jit(solution)/shard_map/ppermute | solution.py:244
  20.5 0.4 shard_map.95
  20.8 2.5 %collective-permute-start.10 = (f32[2,256]{1,0:T(2,128)S(1)}, f32[2,256]{1,0:T(2,128)S(1)}, u32[]{:S(2)}, u32[]{:S(2)}) collective-permute-start(f32[2,256]{1,0:T(2,128)S(1)} %get-tuple-element.66), channel_id=1, source_target_pairs={{0,3},{1,2},{2,1},{3,0},{4,7},{5,6},{6,5},{7,4},{8,11},{9,10},{10,... | collective-permute-start | bytes 6152 | tf_op jit(solution)/shard_map/ppermute | solution.py:219
  23.4 0.5 %collective-permute-start.9 = (f32[2,256]{1,0:T(2,128)S(1)}, f32[2,256]{1,0:T(2,128)S(1)}, u32[]{:S(2)}, u32[]{:S(2)}) collective-permute-start(f32[2,256]{1,0:T(2,128)S(1)} %get-tuple-element.66), channel_id=1, source_target_pairs={{0,2},{1,3},{2,0},{3,1},{4,6},{5,7},{6,4},{7,5},{8,10},{9,11},{10,... | collective-permute-start | bytes 6152 | tf_op jit(solution)/shard_map/ppermute | solution.py:219
  23.9 0.5 %collective-permute-start.8 = (f32[2,256]{1,0:T(2,128)S(1)}, f32[2,256]{1,0:T(2,128)S(1)}, u32[]{:S(2)}, u32[]{:S(2)}) collective-permute-start(f32[2,256]{1,0:T(2,128)S(1)} %get-tuple-element.66), channel_id=1, source_target_pairs={{0,1},{1,0},{2,3},{3,2},{4,5},{5,4},{6,7},{7,6},{8,9},{9,8},{10,11... | collective-permute-start | bytes 6152 | tf_op jit(solution)/shard_map/ppermute | solution.py:219
  24.4 1.0 %collective-permute-done.10 = f32[2,256]{1,0:T(2,128)S(1)} collective-permute-done((f32[2,256]{1,0:T(2,128)S(1)}, f32[2,256]{1,0:T(2,128)S(1)}, u32[]{:S(2)}, u32[]{:S(2)}) %collective-permute-start.10) | collective-permute-done | bytes 2080 | tf_op jit(solution)/shard_map/ppermute | solution.py:219
  25.4 1.5 %collective-permute-done.9 = f32[2,256]{1,0:T(2,128)S(1)} collective-permute-done((f32[2,256]{1,0:T(2,128)S(1)}, f32[2,256]{1,0:T(2,128)S(1)}, u32[]{:S(2)}, u32[]{:S(2)}) %collective-permute-start.9) | collective-permute-done | bytes 2080 | tf_op jit(solution)/shard_map/ppermute | solution.py:219
  26.9 0.5 %collective-permute-done.8 = f32[2,256]{1,0:T(2,128)S(1)} collective-permute-done((f32[2,256]{1,0:T(2,128)S(1)}, f32[2,256]{1,0:T(2,128)S(1)}, u32[]{:S(2)}, u32[]{:S(2)}) %collective-permute-start.8) | collective-permute-done | bytes 2080 | tf_op jit(solution)/shard_map/ppermute | solution.py:219
  27.4 0.4 shard_map.96
  27.9 0.1 collective-permute-start.11
  27.9 2.0 %collective-permute-start.14 = (f32[256,128]{1,0:T(8,128)S(1)}, f32[256,128]{1,0:T(8,128)S(1)}, u32[]{:S(2)}, u32[]{:S(2)}) collective-permute-start(f32[256,128]{1,0:T(8,128)S(1)} %get-tuple-element.82), channel_id=1, source_target_pairs={{0,8},{4,12},{8,0},{12,4},{16,24},{20,28},{24,16},{28,20},{1,9},{5... | collective-permute-start | bytes 393224 | tf_op jit(solution)/shard_map/ppermute | solution.py:244
  30.0 1.9 %shard_map.97 = (bf16[1,256,512]{2,1,0:T(8,128)(2,1)}, f32[256,256]{1,0:T(8,128)S(1)}, f32[256,256]{1,0:T(8,128)S(1)}, f32[256,256]{1,0:T(8,128)S(1)}, f32[256,256]{1,0:T(8,128)S(1)}) custom-call(bf16[1,256,512]{2,1,0:T(8,128)(2,1)S(1)} %get-tuple-element.50.queries, bf16[256,512]{1,0:T(8,128)(2,1)S(1)} %get-tuple-element.51.spiked, ...), custom_call_target="tpu_custom_call" | custom-call | flops 268435456 | bytes 4194304 | tf_op jit(solution)/shard_map/pallas_call | solution.py:40
  31.9 2.2 %collective-permute-done.11 = f32[264,128]{1,0:T(8,128)S(1)} collective-permute-done((f32[264,128]{1,0:T(8,128)S(1)}, f32[264,128]{1,0:T(8,128)S(1)}, u32[]{:S(2)}, u32[]{:S(2)}) %collective-permute-start.11) | collective-permute-done | bytes 135200 | tf_op jit(solution)/shard_map/ppermute | solution.py:244
  34.1 0.1 collective-permute-start.12
  34.2 3.0 %collective-permute-done.14 = f32[256,128]{1,0:T(8,128)S(1)} collective-permute-done((f32[256,128]{1,0:T(8,128)S(1)}, f32[256,128]{1,0:T(8,128)S(1)}, u32[]{:S(2)}, u32[]{:S(2)}) %collective-permute-start.14) | collective-permute-done | bytes 131104 | tf_op jit(solution)/shard_map/ppermute | solution.py:244
  37.3 0.1 collective-permute-start.15
  37.4 4.0 %collective-permute-done.12 = f32[264,128]{1,0:T(8,128)S(1)} collective-permute-done((f32[264,128]{1,0:T(8,128)S(1)}, f32[264,128]{1,0:T(8,128)S(1)}, u32[]{:S(2)}, u32[]{:S(2)}) %collective-permute-start.12) | collective-permute-done | bytes 135200 | tf_op jit(solution)/shard_map/ppermute | solution.py:244
  41.4 0.2 shard_map.99
  41.7 1.1 %collective-permute-done.15 = f32[256,128]{1,0:T(8,128)S(1)} collective-permute-done((f32[256,128]{1,0:T(8,128)S(1)}, f32[256,128]{1,0:T(8,128)S(1)}, u32[]{:S(2)}, u32[]{:S(2)}) %collective-permute-start.15) | collective-permute-done | bytes 131104 | tf_op jit(solution)/shard_map/ppermute | solution.py:244
  42.8 1.0 %shard_map.100 = (bf16[1,256,512]{2,1,0:T(8,128)(2,1)}, bf16[1,256,512]{2,1,0:T(8,128)(2,1)}, f32[1,512]{1,0:T(1,128)}) custom-call(bf16[1,256,512]{2,1,0:T(8,128)(2,1)S(1)} %get-tuple-element.52.values, bf16[256,512]{1,0:T(8,128)(2,1)S(1)} %get-tuple-element.51.spiked, s32[1,256,512]{2,1,0:T(8,128)S(1)} %copy-done, ...), custom_call_target="tpu_custom_call" | custom-call | flops 33554432 | bytes 2097152 | tf_op jit(solution)/shard_map/pallas_call | solution.py:40
  (26 shorter events, 0.2 us)
Async XLA Ops:
  2.2 6.2 %collective-permute-start = (f32[128,128]{1,0:T(8,128)S(1)}, f32[128,128]{1,0:T(8,128)S(1)}, u32[]{:S(2)}, u32[]{:S(2)}) collective-permute-start(f32[128,128]{1,0:T(8,128)S(1)} %get-tuple-element.48), channel_id=1, source_target_pairs={{0,4},{4,0},{8,12},{12,8},{16,24},{20,28},{24,16},{28,20},{1,5},{5... | collective-permute-start | bytes 196616 | tf_op jit(solution)/shard_map/ppermute | solution.py:244
  5.3 6.4 %collective-permute-start.2 = (f32[128,128]{1,0:T(8,128)S(1)}, f32[128,128]{1,0:T(8,128)S(1)}, u32[]{:S(2)}, u32[]{:S(2)}) collective-permute-start(f32[128,128]{1,0:T(8,128)S(1)} %get-tuple-element.55), channel_id=1, source_target_pairs={{0,4},{4,0},{8,12},{12,8},{16,24},{20,28},{24,16},{28,20},{1,5},{5... | collective-permute-start | bytes 196616 | tf_op jit(solution)/shard_map/ppermute | solution.py:244
  5.3 6.7 %collective-permute-start.4 = (f32[128,128]{1,0:T(8,128)S(1)}, f32[128,128]{1,0:T(8,128)S(1)}, u32[]{:S(2)}, u32[]{:S(2)}) collective-permute-start(f32[128,128]{1,0:T(8,128)S(1)} %get-tuple-element.58), channel_id=1, source_target_pairs={{0,8},{4,12},{8,0},{12,4},{16,20},{20,16},{24,28},{28,24},{1,9},{5... | collective-permute-start | bytes 196616 | tf_op jit(solution)/shard_map/ppermute | solution.py:244
  8.3 6.2 %collective-permute-start.6 = (f32[128,128]{1,0:T(8,128)S(1)}, f32[128,128]{1,0:T(8,128)S(1)}, u32[]{:S(2)}, u32[]{:S(2)}) collective-permute-start(f32[128,128]{1,0:T(8,128)S(1)} %get-tuple-element.61), channel_id=1, source_target_pairs={{0,8},{4,12},{8,0},{12,4},{16,20},{20,16},{24,28},{28,24},{1,9},{5... | collective-permute-start | bytes 196616 | tf_op jit(solution)/shard_map/ppermute | solution.py:244
  8.4 9.6 %collective-permute-start.1 = (f32[128,128]{1,0:T(8,128)S(1)}, f32[128,128]{1,0:T(8,128)S(1)}, u32[]{:S(2)}, u32[]{:S(2)}) collective-permute-start(f32[128,128]{1,0:T(8,128)S(1)} %add_select_fusion.3), channel_id=1, source_target_pairs={{0,8},{4,12},{8,0},{12,4},{16,20},{20,16},{24,28},{28,24},{1,9},{5... | collective-permute-start | bytes 196616 | tf_op jit(solution)/shard_map/ppermute | solution.py:244
  11.7 8.0 %collective-permute-start.3 = (f32[128,128]{1,0:T(8,128)S(1)}, f32[128,128]{1,0:T(8,128)S(1)}, u32[]{:S(2)}, u32[]{:S(2)}) collective-permute-start(f32[128,128]{1,0:T(8,128)S(1)} %add_select_fusion.2), channel_id=1, source_target_pairs={{0,8},{4,12},{8,0},{12,4},{16,20},{20,16},{24,28},{28,24},{1,9},{5... | collective-permute-start | bytes 196616 | tf_op jit(solution)/shard_map/ppermute | solution.py:244
  12.1 7.5 %collective-permute-start.5 = (f32[128,128]{1,0:T(8,128)S(1)}, f32[128,128]{1,0:T(8,128)S(1)}, u32[]{:S(2)}, u32[]{:S(2)}) collective-permute-start(f32[128,128]{1,0:T(8,128)S(1)} %add_select_fusion.1), channel_id=1, source_target_pairs={{0,4},{4,0},{8,12},{12,8},{16,24},{20,28},{24,16},{28,20},{1,5},{5... | collective-permute-start | bytes 196616 | tf_op jit(solution)/shard_map/ppermute | solution.py:244
  14.6 5.9 %collective-permute-start.7 = (f32[128,128]{1,0:T(8,128)S(1)}, f32[128,128]{1,0:T(8,128)S(1)}, u32[]{:S(2)}, u32[]{:S(2)}) collective-permute-start(f32[128,128]{1,0:T(8,128)S(1)} %add_select_fusion), channel_id=1, source_target_pairs={{0,4},{4,0},{8,12},{12,8},{16,24},{20,28},{24,16},{28,20},{1,5},{5... | collective-permute-start | bytes 196616 | tf_op jit(solution)/shard_map/ppermute | solution.py:244
  20.8 4.5 %collective-permute-start.10 = (f32[2,256]{1,0:T(2,128)S(1)}, f32[2,256]{1,0:T(2,128)S(1)}, u32[]{:S(2)}, u32[]{:S(2)}) collective-permute-start(f32[2,256]{1,0:T(2,128)S(1)} %get-tuple-element.66), channel_id=1, source_target_pairs={{0,3},{1,2},{2,1},{3,0},{4,7},{5,6},{6,5},{7,4},{8,11},{9,10},{10,... | collective-permute-start | bytes 6152 | tf_op jit(solution)/shard_map/ppermute | solution.py:219
  23.4 3.6 %collective-permute-start.9 = (f32[2,256]{1,0:T(2,128)S(1)}, f32[2,256]{1,0:T(2,128)S(1)}, u32[]{:S(2)}, u32[]{:S(2)}) collective-permute-start(f32[2,256]{1,0:T(2,128)S(1)} %get-tuple-element.66), channel_id=1, source_target_pairs={{0,2},{1,3},{2,0},{3,1},{4,6},{5,7},{6,4},{7,5},{8,10},{9,11},{10,... | collective-permute-start | bytes 6152 | tf_op jit(solution)/shard_map/ppermute | solution.py:219
  23.9 3.6 %collective-permute-start.8 = (f32[2,256]{1,0:T(2,128)S(1)}, f32[2,256]{1,0:T(2,128)S(1)}, u32[]{:S(2)}, u32[]{:S(2)}) collective-permute-start(f32[2,256]{1,0:T(2,128)S(1)} %get-tuple-element.66), channel_id=1, source_target_pairs={{0,1},{1,0},{2,3},{3,2},{4,5},{5,4},{6,7},{7,6},{8,9},{9,8},{10,11... | collective-permute-start | bytes 6152 | tf_op jit(solution)/shard_map/ppermute | solution.py:219
  27.9 6.2 %collective-permute-start.11 = (f32[264,128]{1,0:T(8,128)S(1)}, f32[264,128]{1,0:T(8,128)S(1)}, u32[]{:S(2)}, u32[]{:S(2)}) collective-permute-start(f32[264,128]{1,0:T(8,128)S(1)} %get-tuple-element.77), channel_id=1, source_target_pairs={{0,4},{4,0},{8,12},{12,8},{16,20},{20,16},{24,28},{28,24},{1,5},{5... | collective-permute-start | bytes 405512 | tf_op jit(solution)/shard_map/ppermute | solution.py:244
  27.9 9.3 %collective-permute-start.14 = (f32[256,128]{1,0:T(8,128)S(1)}, f32[256,128]{1,0:T(8,128)S(1)}, u32[]{:S(2)}, u32[]{:S(2)}) collective-permute-start(f32[256,128]{1,0:T(8,128)S(1)} %get-tuple-element.82), channel_id=1, source_target_pairs={{0,8},{4,12},{8,0},{12,4},{16,24},{20,28},{24,16},{28,20},{1,9},{5... | collective-permute-start | bytes 393224 | tf_op jit(solution)/shard_map/ppermute | solution.py:244
  34.1 7.3 %copy-start = (s32[1,256,512]{2,1,0:T(8,128)S(1)}, s32[1,256,512]{2,1,0:T(8,128)}, u32[]{:S(2)}) copy-start(s32[1,256,512]{2,1,0:T(8,128)} %spikes.7) | copy-start | bytes 1572868
  34.1 7.3 %collective-permute-start.12 = (f32[264,128]{1,0:T(8,128)S(1)}, f32[264,128]{1,0:T(8,128)S(1)}, u32[]{:S(2)}, u32[]{:S(2)}) collective-permute-start(f32[264,128]{1,0:T(8,128)S(1)} %add.82.total), channel_id=1, source_target_pairs={{0,8},{4,12},{8,0},{12,4},{16,24},{20,28},{24,16},{28,20},{1,9},{5... | collective-permute-start | bytes 405512 | tf_op jit(solution)/shard_map/ppermute | solution.py:244
  37.3 5.5 %collective-permute-start.15 = (f32[256,128]{1,0:T(8,128)S(1)}, f32[256,128]{1,0:T(8,128)S(1)}, u32[]{:S(2)}, u32[]{:S(2)}) collective-permute-start(f32[256,128]{1,0:T(8,128)S(1)} %select_add_fusion.1), channel_id=1, source_target_pairs={{0,4},{4,0},{8,12},{12,8},{16,20},{20,16},{24,28},{28,24},{1,5},{5... | collective-permute-start | bytes 393224 | tf_op jit(solution)/shard_map/ppermute | solution.py:244
  41.4 1.4 %collective-permute-start.13 = (f32[8,128]{1,0:T(8,128)S(1)}, f32[8,128]{1,0:T(8,128)S(1)}, u32[]{:S(2)}, u32[]{:S(2)}) collective-permute-start(f32[8,128]{1,0:T(8,128)S(1)} %slice_add_fusion.gain_here), channel_id=1, source_target_pairs={{0,16},{16,0},{1,17},{17,1},{2,18},{18,2},{3,19},{19,3},{4,20},{20... | collective-permute-start | bytes 12296 | tf_op jit(solution)/shard_map/ppermute | solution.py:219

commit v7 on v6

--- a/solution.py
+++ b/solution.py
@@ -152,10 +152,20 @@
         block = attended[:, cols(h)]
         result = (inv * scaled[:, cols(h)] - block * factor).astype(BF16)
         grad[:, cols(h)] = result
-        ref, rows = block_of(locals_, h)
-        ref[rows, :] = dot(queries[0, :, cols(h)], result, 0, 0)
         terms = upper[0, :, cols(h)].astype(F32) * block * inv
         locals_[0][gain_at + h : gain_at + h + 1, :] = jnp.sum(terms, axis=0, keepdims=True)
+
+    @pl.when(lax.axis_index("ctx") == 0)
+    def _():
+        for h in range(heads):
+            ref, rows = block_of(locals_, h)
+            ref[rows, :] = jnp.zeros((DH, DH), F32)
+
+    @pl.when(lax.axis_index("ctx") != 0)
+    def _():
+        for h in range(heads):
+            ref, rows = block_of(locals_, h)
+            ref[rows, :] = dot(queries[0, :, cols(h)], grad[:, cols(h)], 0, 0)
 
 
 def pairs_kernel(

time: 44 us -> 43.7 us (level)
  waiting for transfers between devices: 17.5 us -> 16.9 us
  starting transfers between devices: 18.1 us -> 18.6 us
    ppermute x12, waiting for transfers between devices: 14.4 us -> 13.8 us  [swap_by_core(): return lax.ppermute(array, ('dp', axis), pairs)]
    ppermute x12, starting transfers between devices: 14.5 us -> 15 us  [swap_by_core(): return lax.ppermute(array, ('dp', axis), pairs)]
where the time goes in v7:
time: 43.7 us; the launch traced here: 43.5 us
  starting transfers between devices  18.6 us (43%)
  waiting for transfers between devices  16.9 us (39%)
  Pallas kernels  7.07 us (16%)
  between operations  0.78 us (2%)
    ppermute x12, starting transfers between devices, swap_by_core(): return lax.ppermute(array, ('dp', axis), pairs)  15 us
    ppermute x12, waiting for transfers between devices, swap_by_core(): return lax.ppermute(array, ('dp', axis), pairs)  13.8 us
    pallas_call x8, Pallas kernels, call(): pl.pallas_call(body, out_shape=outs, in_specs=[HBM if k in hbm else VMEM...  7.07 us
    ppermute x4, starting transfers between devices, swap(): return lax.ppermute(array, axis, [(i, i ^ stride) for i in range(size)])  3.55 us
    ppermute x4, waiting for transfers between devices, swap(): return lax.ppermute(array, axis, [(i, i ^ stride) for i in range(size)])  3.05 us
  transfers between devices with their start and end apart: 16, of which 11 were waited for; matrix products, arithmetic and copies ran while one was open for 0% of the time, Pallas kernels for 9%

profile of v7, /device:TPU:0, one launch (start us, length us, event | category | flops | bytes accessed | tf_op | source)
XLA Modules:
  0.0 43.5 jit_solution(16996375962178228034)
XLA Ops:
  0.6 1.5 %shard_map.93 = (bf16[1,256,512]{2,1,0:T(8,128)(2,1)S(1)}, bf16[256,512]{1,0:T(8,128)(2,1)S(1)}, f32[128,128]{1,0:T(8,128)S(1)}, f32[128,128]{1,0:T(8,128)S(1)},...) custom-call(bf16[1,256,512]{2,1,0:T(8,128)(2,1)} %keys.3, s32[1,256,512]{2,1,0:T(8,128)} %spikes.7, ...), custom_call_target="tpu_custom_call" | custom-call | flops 33554432 | bytes 1048576 | tf_op jit(solution)/shard_map/pallas_call | solution.py:40
  2.2 3.1 %collective-permute-start = (f32[128,128]{1,0:T(8,128)S(1)}, f32[128,128]{1,0:T(8,128)S(1)}, u32[]{:S(2)}, u32[]{:S(2)}) collective-permute-start(f32[128,128]{1,0:T(8,128)S(1)} %get-tuple-element.48), channel_id=1, source_target_pairs={{0,4},{4,0},{8,12},{12,8},{16,24},{20,28},{24,16},{28,20},{1,5},{5... | collective-permute-start | bytes 196616 | tf_op jit(solution)/shard_map/ppermute | solution.py:254
  5.3 0.1 collective-permute-start.2
  5.3 3.0 %collective-permute-start.4 = (f32[128,128]{1,0:T(8,128)S(1)}, f32[128,128]{1,0:T(8,128)S(1)}, u32[]{:S(2)}, u32[]{:S(2)}) collective-permute-start(f32[128,128]{1,0:T(8,128)S(1)} %get-tuple-element.58), channel_id=1, source_target_pairs={{0,8},{4,12},{8,0},{12,4},{16,20},{20,16},{24,28},{28,24},{1,9},{5... | collective-permute-start | bytes 196616 | tf_op jit(solution)/shard_map/ppermute | solution.py:254
  8.4 3.0 %collective-permute-start.1 = (f32[128,128]{1,0:T(8,128)S(1)}, f32[128,128]{1,0:T(8,128)S(1)}, u32[]{:S(2)}, u32[]{:S(2)}) collective-permute-start(f32[128,128]{1,0:T(8,128)S(1)} %add_select_fusion.3), channel_id=1, source_target_pairs={{0,8},{4,12},{8,0},{12,4},{16,20},{20,16},{24,28},{28,24},{1,9},{5... | collective-permute-start | bytes 196616 | tf_op jit(solution)/shard_map/ppermute | solution.py:254
  11.3 0.3 collective-permute-done.2
  11.7 0.4 collective-permute-start.3
  12.1 2.4 %collective-permute-start.5 = (f32[128,128]{1,0:T(8,128)S(1)}, f32[128,128]{1,0:T(8,128)S(1)}, u32[]{:S(2)}, u32[]{:S(2)}) collective-permute-start(f32[128,128]{1,0:T(8,128)S(1)} %add_select_fusion.1), channel_id=1, source_target_pairs={{0,4},{4,0},{8,12},{12,8},{16,24},{20,28},{24,16},{28,20},{1,5},{5... | collective-permute-start | bytes 196616 | tf_op jit(solution)/shard_map/ppermute | solution.py:254
  14.6 0.3 collective-permute-start.7
  14.9 1.8 %shard_map.94 = (bf16[1,256,512]{2,1,0:T(8,128)(2,1)S(1)}, bf16[1,256,512]{2,1,0:T(8,128)(2,1)S(1)}, bf16[1,256,512]{2,1,0:T(8,128)(2,1)S(1)}, bf16[256,512]{1,0...) custom-call(bf16[1,256,512]{2,1,0:T(8,128)(2,1)} %queries.1, ...), custom_call_target="tpu_custom_call" | custom-call | flops 134217728 | bytes 2097152 | tf_op jit(solution)/shard_map/pallas_call | solution.py:40
  16.6 1.3 %collective-permute-done.1 = f32[128,128]{1,0:T(8,128)S(1)} collective-permute-done((f32[128,128]{1,0:T(8,128)S(1)}, f32[128,128]{1,0:T(8,128)S(1)}, u32[]{:S(2)}, u32[]{:S(2)}) %collective-permute-start.1) | collective-permute-done | bytes 65568 | tf_op jit(solution)/shard_map/ppermute | solution.py:254
  18.0 1.7 %collective-permute-done.3 = f32[128,128]{1,0:T(8,128)S(1)} collective-permute-done((f32[128,128]{1,0:T(8,128)S(1)}, f32[128,128]{1,0:T(8,128)S(1)}, u32[]{:S(2)}, u32[]{:S(2)}) %collective-permute-start.3) | collective-permute-done | bytes 65568 | tf_op jit(solution)/shard_map/ppermute | solution.py:254
  19.7 0.8 %collective-permute-done.7 = f32[128,128]{1,0:T(8,128)S(1)} collective-permute-done((f32[128,128]{1,0:T(8,128)S(1)}, f32[128,128]{1,0:T(8,128)S(1)}, u32[]{:S(2)}, u32[]{:S(2)}) %collective-permute-start.7) | collective-permute-done | bytes 65568 | tf_op jit(solution)/shard_map/ppermute | solution.py:254
  20.5 0.4 shard_map.95
  20.8 2.5 %collective-permute-start.10 = (f32[2,256]{1,0:T(2,128)S(1)}, f32[2,256]{1,0:T(2,128)S(1)}, u32[]{:S(2)}, u32[]{:S(2)}) collective-permute-start(f32[2,256]{1,0:T(2,128)S(1)} %get-tuple-element.66), channel_id=1, source_target_pairs={{0,3},{1,2},{2,1},{3,0},{4,7},{5,6},{6,5},{7,4},{8,11},{9,10},{10,... | collective-permute-start | bytes 6152 | tf_op jit(solution)/shard_map/ppermute | solution.py:229
  23.4 0.5 %collective-permute-start.9 = (f32[2,256]{1,0:T(2,128)S(1)}, f32[2,256]{1,0:T(2,128)S(1)}, u32[]{:S(2)}, u32[]{:S(2)}) collective-permute-start(f32[2,256]{1,0:T(2,128)S(1)} %get-tuple-element.66), channel_id=1, source_target_pairs={{0,2},{1,3},{2,0},{3,1},{4,6},{5,7},{6,4},{7,5},{8,10},{9,11},{10,... | collective-permute-start | bytes 6152 | tf_op jit(solution)/shard_map/ppermute | solution.py:229
  23.9 0.5 %collective-permute-start.8 = (f32[2,256]{1,0:T(2,128)S(1)}, f32[2,256]{1,0:T(2,128)S(1)}, u32[]{:S(2)}, u32[]{:S(2)}) collective-permute-start(f32[2,256]{1,0:T(2,128)S(1)} %get-tuple-element.66), channel_id=1, source_target_pairs={{0,1},{1,0},{2,3},{3,2},{4,5},{5,4},{6,7},{7,6},{8,9},{9,8},{10,11... | collective-permute-start | bytes 6152 | tf_op jit(solution)/shard_map/ppermute | solution.py:229
  24.4 1.0 %collective-permute-done.10 = f32[2,256]{1,0:T(2,128)S(1)} collective-permute-done((f32[2,256]{1,0:T(2,128)S(1)}, f32[2,256]{1,0:T(2,128)S(1)}, u32[]{:S(2)}, u32[]{:S(2)}) %collective-permute-start.10) | collective-permute-done | bytes 2080 | tf_op jit(solution)/shard_map/ppermute | solution.py:229
  25.4 1.5 %collective-permute-done.9 = f32[2,256]{1,0:T(2,128)S(1)} collective-permute-done((f32[2,256]{1,0:T(2,128)S(1)}, f32[2,256]{1,0:T(2,128)S(1)}, u32[]{:S(2)}, u32[]{:S(2)}) %collective-permute-start.9) | collective-permute-done | bytes 2080 | tf_op jit(solution)/shard_map/ppermute | solution.py:229
  26.9 0.5 %collective-permute-done.8 = f32[2,256]{1,0:T(2,128)S(1)} collective-permute-done((f32[2,256]{1,0:T(2,128)S(1)}, f32[2,256]{1,0:T(2,128)S(1)}, u32[]{:S(2)}, u32[]{:S(2)}) %collective-permute-start.8) | collective-permute-done | bytes 2080 | tf_op jit(solution)/shard_map/ppermute | solution.py:229
  27.4 0.2 shard_map.96
  27.7 0.1 collective-permute-start.11
  27.8 2.3 %collective-permute-start.14 = (f32[256,128]{1,0:T(8,128)S(1)}, f32[256,128]{1,0:T(8,128)S(1)}, u32[]{:S(2)}, u32[]{:S(2)}) collective-permute-start(f32[256,128]{1,0:T(8,128)S(1)} %get-tuple-element.82), channel_id=1, source_target_pairs={{0,8},{4,12},{8,0},{12,4},{16,24},{20,28},{24,16},{28,20},{1,9},{5... | collective-permute-start | bytes 393224 | tf_op jit(solution)/shard_map/ppermute | solution.py:254
  30.0 1.9 %shard_map.97 = (bf16[1,256,512]{2,1,0:T(8,128)(2,1)}, f32[256,256]{1,0:T(8,128)S(1)}, f32[256,256]{1,0:T(8,128)S(1)}, f32[256,256]{1,0:T(8,128)S(1)}, f32[256,256]{1,0:T(8,128)S(1)}) custom-call(bf16[1,256,512]{2,1,0:T(8,128)(2,1)S(1)} %get-tuple-element.50.queries, bf16[256,512]{1,0:T(8,128)(2,1)S(1)} %get-tuple-element.51.spiked, ...), custom_call_target="tpu_custom_call" | custom-call | flops 268435456 | bytes 4194304 | tf_op jit(solution)/shard_map/pallas_call | solution.py:40
  32.0 2.2 %collective-permute-done.11 = f32[264,128]{1,0:T(8,128)S(1)} collective-permute-done((f32[264,128]{1,0:T(8,128)S(1)}, f32[264,128]{1,0:T(8,128)S(1)}, u32[]{:S(2)}, u32[]{:S(2)}) %collective-permute-start.11) | collective-permute-done | bytes 135200 | tf_op jit(solution)/shard_map/ppermute | solution.py:254
  34.3 0.1 collective-permute-start.12
  34.3 2.4 %collective-permute-done.14 = f32[256,128]{1,0:T(8,128)S(1)} collective-permute-done((f32[256,128]{1,0:T(8,128)S(1)}, f32[256,128]{1,0:T(8,128)S(1)}, u32[]{:S(2)}, u32[]{:S(2)}) %collective-permute-start.14) | collective-permute-done | bytes 131104 | tf_op jit(solution)/shard_map/ppermute | solution.py:254
  36.8 0.4 collective-permute-start.15
  37.2 4.0 %collective-permute-done.12 = f32[264,128]{1,0:T(8,128)S(1)} collective-permute-done((f32[264,128]{1,0:T(8,128)S(1)}, f32[264,128]{1,0:T(8,128)S(1)}, u32[]{:S(2)}, u32[]{:S(2)}) %collective-permute-start.12) | collective-permute-done | bytes 135200 | tf_op jit(solution)/shard_map/ppermute | solution.py:254
  41.2 0.2 shard_map.99
  41.4 1.1 %collective-permute-done.15 = f32[256,128]{1,0:T(8,128)S(1)} collective-permute-done((f32[256,128]{1,0:T(8,128)S(1)}, f32[256,128]{1,0:T(8,128)S(1)}, u32[]{:S(2)}, u32[]{:S(2)}) %collective-permute-start.15) | collective-permute-done | bytes 131104 | tf_op jit(solution)/shard_map/ppermute | solution.py:254
  42.5 1.0 %shard_map.100 = (bf16[1,256,512]{2,1,0:T(8,128)(2,1)}, bf16[1,256,512]{2,1,0:T(8,128)(2,1)}, f32[1,512]{1,0:T(1,128)}) custom-call(bf16[1,256,512]{2,1,0:T(8,128)(2,1)S(1)} %get-tuple-element.52.values, bf16[256,512]{1,0:T(8,128)(2,1)S(1)} %get-tuple-element.51.spiked, s32[1,256,512]{2,1,0:T(8,128)S(1)} %copy-done, ...), custom_call_target="tpu_custom_call" | custom-call | flops 33554432 | bytes 2097152 | tf_op jit(solution)/shard_map/pallas_call | solution.py:40
  (26 shorter events, 0.2 us)
Async XLA Ops:
  2.2 6.2 %collective-permute-start = (f32[128,128]{1,0:T(8,128)S(1)}, f32[128,128]{1,0:T(8,128)S(1)}, u32[]{:S(2)}, u32[]{:S(2)}) collective-permute-start(f32[128,128]{1,0:T(8,128)S(1)} %get-tuple-element.48), channel_id=1, source_target_pairs={{0,4},{4,0},{8,12},{12,8},{16,24},{20,28},{24,16},{28,20},{1,5},{5... | collective-permute-start | bytes 196616 | tf_op jit(solution)/shard_map/ppermute | solution.py:254
  5.3 6.4 %collective-permute-start.2 = (f32[128,128]{1,0:T(8,128)S(1)}, f32[128,128]{1,0:T(8,128)S(1)}, u32[]{:S(2)}, u32[]{:S(2)}) collective-permute-start(f32[128,128]{1,0:T(8,128)S(1)} %get-tuple-element.55), channel_id=1, source_target_pairs={{0,4},{4,0},{8,12},{12,8},{16,24},{20,28},{24,16},{28,20},{1,5},{5... | collective-permute-start | bytes 196616 | tf_op jit(solution)/shard_map/ppermute | solution.py:254
  5.3 6.7 %collective-permute-start.4 = (f32[128,128]{1,0:T(8,128)S(1)}, f32[128,128]{1,0:T(8,128)S(1)}, u32[]{:S(2)}, u32[]{:S(2)}) collective-permute-start(f32[128,128]{1,0:T(8,128)S(1)} %get-tuple-element.58), channel_id=1, source_target_pairs={{0,8},{4,12},{8,0},{12,4},{16,20},{20,16},{24,28},{28,24},{1,9},{5... | collective-permute-start | bytes 196616 | tf_op jit(solution)/shard_map/ppermute | solution.py:254
  8.3 6.2 %collective-permute-start.6 = (f32[128,128]{1,0:T(8,128)S(1)}, f32[128,128]{1,0:T(8,128)S(1)}, u32[]{:S(2)}, u32[]{:S(2)}) collective-permute-start(f32[128,128]{1,0:T(8,128)S(1)} %get-tuple-element.61), channel_id=1, source_target_pairs={{0,8},{4,12},{8,0},{12,4},{16,20},{20,16},{24,28},{28,24},{1,9},{5... | collective-permute-start | bytes 196616 | tf_op jit(solution)/shard_map/ppermute | solution.py:254
  8.4 9.6 %collective-permute-start.1 = (f32[128,128]{1,0:T(8,128)S(1)}, f32[128,128]{1,0:T(8,128)S(1)}, u32[]{:S(2)}, u32[]{:S(2)}) collective-permute-start(f32[128,128]{1,0:T(8,128)S(1)} %add_select_fusion.3), channel_id=1, source_target_pairs={{0,8},{4,12},{8,0},{12,4},{16,20},{20,16},{24,28},{28,24},{1,9},{5... | collective-permute-start | bytes 196616 | tf_op jit(solution)/shard_map/ppermute | solution.py:254
  11.7 8.0 %collective-permute-start.3 = (f32[128,128]{1,0:T(8,128)S(1)}, f32[128,128]{1,0:T(8,128)S(1)}, u32[]{:S(2)}, u32[]{:S(2)}) collective-permute-start(f32[128,128]{1,0:T(8,128)S(1)} %add_select_fusion.2), channel_id=1, source_target_pairs={{0,8},{4,12},{8,0},{12,4},{16,20},{20,16},{24,28},{28,24},{1,9},{5... | collective-permute-start | bytes 196616 | tf_op jit(solution)/shard_map/ppermute | solution.py:254
  12.1 7.5 %collective-permute-start.5 = (f32[128,128]{1,0:T(8,128)S(1)}, f32[128,128]{1,0:T(8,128)S(1)}, u32[]{:S(2)}, u32[]{:S(2)}) collective-permute-start(f32[128,128]{1,0:T(8,128)S(1)} %add_select_fusion.1), channel_id=1, source_target_pairs={{0,4},{4,0},{8,12},{12,8},{16,24},{20,28},{24,16},{28,20},{1,5},{5... | collective-permute-start | bytes 196616 | tf_op jit(solution)/shard_map/ppermute | solution.py:254
  14.6 5.9 %collective-permute-start.7 = (f32[128,128]{1,0:T(8,128)S(1)}, f32[128,128]{1,0:T(8,128)S(1)}, u32[]{:S(2)}, u32[]{:S(2)}) collective-permute-start(f32[128,128]{1,0:T(8,128)S(1)} %add_select_fusion), channel_id=1, source_target_pairs={{0,4},{4,0},{8,12},{12,8},{16,24},{20,28},{24,16},{28,20},{1,5},{5... | collective-permute-start | bytes 196616 | tf_op jit(solution)/shard_map/ppermute | solution.py:254
  20.8 4.5 %collective-permute-start.10 = (f32[2,256]{1,0:T(2,128)S(1)}, f32[2,256]{1,0:T(2,128)S(1)}, u32[]{:S(2)}, u32[]{:S(2)}) collective-permute-start(f32[2,256]{1,0:T(2,128)S(1)} %get-tuple-element.66), channel_id=1, source_target_pairs={{0,3},{1,2},{2,1},{3,0},{4,7},{5,6},{6,5},{7,4},{8,11},{9,10},{10,... | collective-permute-start | bytes 6152 | tf_op jit(solution)/shard_map/ppermute | solution.py:229
  23.4 3.6 %collective-permute-start.9 = (f32[2,256]{1,0:T(2,128)S(1)}, f32[2,256]{1,0:T(2,128)S(1)}, u32[]{:S(2)}, u32[]{:S(2)}) collective-permute-start(f32[2,256]{1,0:T(2,128)S(1)} %get-tuple-element.66), channel_id=1, source_target_pairs={{0,2},{1,3},{2,0},{3,1},{4,6},{5,7},{6,4},{7,5},{8,10},{9,11},{10,... | collective-permute-start | bytes 6152 | tf_op jit(solution)/shard_map/ppermute | solution.py:229
  23.9 3.6 %collective-permute-start.8 = (f32[2,256]{1,0:T(2,128)S(1)}, f32[2,256]{1,0:T(2,128)S(1)}, u32[]{:S(2)}, u32[]{:S(2)}) collective-permute-start(f32[2,256]{1,0:T(2,128)S(1)} %get-tuple-element.66), channel_id=1, source_target_pairs={{0,1},{1,0},{2,3},{3,2},{4,5},{5,4},{6,7},{7,6},{8,9},{9,8},{10,11... | collective-permute-start | bytes 6152 | tf_op jit(solution)/shard_map/ppermute | solution.py:229
  27.7 6.5 %collective-permute-start.11 = (f32[264,128]{1,0:T(8,128)S(1)}, f32[264,128]{1,0:T(8,128)S(1)}, u32[]{:S(2)}, u32[]{:S(2)}) collective-permute-start(f32[264,128]{1,0:T(8,128)S(1)} %get-tuple-element.77), channel_id=1, source_target_pairs={{0,4},{4,0},{8,12},{12,8},{16,20},{20,16},{24,28},{28,24},{1,5},{5... | collective-permute-start | bytes 405512 | tf_op jit(solution)/shard_map/ppermute | solution.py:254
  27.8 9.0 %collective-permute-start.14 = (f32[256,128]{1,0:T(8,128)S(1)}, f32[256,128]{1,0:T(8,128)S(1)}, u32[]{:S(2)}, u32[]{:S(2)}) collective-permute-start(f32[256,128]{1,0:T(8,128)S(1)} %get-tuple-element.82), channel_id=1, source_target_pairs={{0,8},{4,12},{8,0},{12,4},{16,24},{20,28},{24,16},{28,20},{1,9},{5... | collective-permute-start | bytes 393224 | tf_op jit(solution)/shard_map/ppermute | solution.py:254
  34.2 6.9 %copy-start = (s32[1,256,512]{2,1,0:T(8,128)S(1)}, s32[1,256,512]{2,1,0:T(8,128)}, u32[]{:S(2)}) copy-start(s32[1,256,512]{2,1,0:T(8,128)} %spikes.7) | copy-start | bytes 1572868
  34.3 6.9 %collective-permute-start.12 = (f32[264,128]{1,0:T(8,128)S(1)}, f32[264,128]{1,0:T(8,128)S(1)}, u32[]{:S(2)}, u32[]{:S(2)}) collective-permute-start(f32[264,128]{1,0:T(8,128)S(1)} %add.82.total), channel_id=1, source_target_pairs={{0,8},{4,12},{8,0},{12,4},{16,24},{20,28},{24,16},{28,20},{1,9},{5... | collective-permute-start | bytes 405512 | tf_op jit(solution)/shard_map/ppermute | solution.py:254
  36.8 5.7 %collective-permute-start.15 = (f32[256,128]{1,0:T(8,128)S(1)}, f32[256,128]{1,0:T(8,128)S(1)}, u32[]{:S(2)}, u32[]{:S(2)}) collective-permute-start(f32[256,128]{1,0:T(8,128)S(1)} %select_add_fusion.1), channel_id=1, source_target_pairs={{0,4},{4,0},{8,12},{12,8},{16,20},{20,16},{24,28},{28,24},{1,5},{5... | collective-permute-start | bytes 393224 | tf_op jit(solution)/shard_map/ppermute | solution.py:254
  41.2 1.3 %collective-permute-start.13 = (f32[8,128]{1,0:T(8,128)S(1)}, f32[8,128]{1,0:T(8,128)S(1)}, u32[]{:S(2)}, u32[]{:S(2)}) collective-permute-start(f32[8,128]{1,0:T(8,128)S(1)} %slice_add_fusion.gain_here), channel_id=1, source_target_pairs={{0,16},{16,0},{1,17},{17,1},{2,18},{18,2},{3,19},{19,3},{4,20},{20... | collective-permute-start | bytes 12296 | tf_op jit(solution)/shard_map/ppermute | solution.py:229

commit v8 on v7

--- a/solution.py
+++ b/solution.py
@@ -125,18 +125,28 @@
     *states, attended, prior, sums = rest
     heads = prior.shape[0]
     tok = intra.shape[0]
-    square = jnp.zeros((tok, DH), F32)
-    cross = jnp.zeros((tok, DH), F32)
-    for h in range(heads):
-        ref, rows = block_of(states, h)
-        state = ref[rows, :].astype(BF16)
-        prior[h] = state
-        block = dot(queries[0, :, cols(h)], state, 1, 0) + intra[:, cols(h)]
-        attended[:, cols(h)] = block
-        square += block * block
-        cross += scaled[:, cols(h)] * block
-    sums[0:1, :] = jnp.sum(square.T, axis=0, keepdims=True)
-    sums[1:2, :] = jnp.sum(cross.T, axis=0, keepdims=True)
+
+    def attend(first_block):
+        square = jnp.zeros((tok, DH), F32)
+        cross = jnp.zeros((tok, DH), F32)
+        for h in range(heads):
+            block = intra[:, cols(h)]
+            if first_block:
+                prior[h] = jnp.zeros((DH, DH), BF16)
+            else:
+                ref, rows = block_of(states, h)
+                state = ref[rows, :].astype(BF16)
+                prior[h] = state
+                block = dot(queries[0, :, cols(h)], state, 1, 0) + block
+            attended[:, cols(h)] = block
+            square += block * block
+            cross += scaled[:, cols(h)] * block
+        sums[0:1, :] = jnp.sum(square.T, axis=0, keepdims=True)
+        sums[1:2, :] = jnp.sum(cross.T, axis=0, keepdims=True)
+
+    at = lax.axis_index("ctx")
+    pl.when(at == 0)(functools.partial(attend, True))
+    pl.when(at != 0)(functools.partial(attend, False))
 
 
 def grad_kernel(width, queries, attended, scaled, upper, sums, grad, *locals_):

time: 43.7 us -> 43.4 us (level)
  no operation moved by 1% of the time
where the time goes in v8:
time: 43.4 us; the launch traced here: 43.3 us
  starting transfers between devices  18.8 us (43%)
  waiting for transfers between devices  16.6 us (38%)
  Pallas kernels  6.9 us (16%)
  between operations  0.77 us (2%)
    ppermute x12, starting transfers between devices, swap_by_core(): return lax.ppermute(array, ('dp', axis), pairs)  15.2 us
    ppermute x12, waiting for transfers between devices, swap_by_core(): return lax.ppermute(array, ('dp', axis), pairs)  13.6 us
    pallas_call x8, Pallas kernels, call(): pl.pallas_call(body, out_shape=outs, in_specs=[HBM if k in hbm else VMEM...  6.9 us
    ppermute x4, starting transfers between devices, swap(): return lax.ppermute(array, axis, [(i, i ^ stride) for i in range(size)])  3.56 us
    ppermute x4, waiting for transfers between devices, swap(): return lax.ppermute(array, axis, [(i, i ^ stride) for i in range(size)])  3.05 us
  transfers between devices with their start and end apart: 16, of which 11 were waited for; matrix products, arithmetic and copies ran while one was open for 0% of the time, Pallas kernels for 9%

profile of v8, /device:TPU:0, one launch (start us, length us, event | category | flops | bytes accessed | tf_op | source)
XLA Modules:
  0.0 43.3 jit_solution(13710027230142813420)
XLA Ops:
  0.6 1.5 %shard_map.93 = (bf16[1,256,512]{2,1,0:T(8,128)(2,1)S(1)}, bf16[256,512]{1,0:T(8,128)(2,1)S(1)}, f32[128,128]{1,0:T(8,128)S(1)}, f32[128,128]{1,0:T(8,128)S(1)},...) custom-call(bf16[1,256,512]{2,1,0:T(8,128)(2,1)} %keys.3, s32[1,256,512]{2,1,0:T(8,128)} %spikes.7, ...), custom_call_target="tpu_custom_call" | custom-call | flops 33554432 | bytes 1048576 | tf_op jit(solution)/shard_map/pallas_call | solution.py:40
  2.2 3.1 %collective-permute-start = (f32[128,128]{1,0:T(8,128)S(1)}, f32[128,128]{1,0:T(8,128)S(1)}, u32[]{:S(2)}, u32[]{:S(2)}) collective-permute-start(f32[128,128]{1,0:T(8,128)S(1)} %get-tuple-element.48), channel_id=1, source_target_pairs={{0,4},{4,0},{8,12},{12,8},{16,24},{20,28},{24,16},{28,20},{1,5},{5... | collective-permute-start | bytes 196616 | tf_op jit(solution)/shard_map/ppermute | solution.py:264
  5.3 0.1 collective-permute-start.2
  5.3 3.0 %collective-permute-start.4 = (f32[128,128]{1,0:T(8,128)S(1)}, f32[128,128]{1,0:T(8,128)S(1)}, u32[]{:S(2)}, u32[]{:S(2)}) collective-permute-start(f32[128,128]{1,0:T(8,128)S(1)} %get-tuple-element.58), channel_id=1, source_target_pairs={{0,8},{4,12},{8,0},{12,4},{16,20},{20,16},{24,28},{28,24},{1,9},{5... | collective-permute-start | bytes 196616 | tf_op jit(solution)/shard_map/ppermute | solution.py:264
  8.4 3.0 %collective-permute-start.1 = (f32[128,128]{1,0:T(8,128)S(1)}, f32[128,128]{1,0:T(8,128)S(1)}, u32[]{:S(2)}, u32[]{:S(2)}) collective-permute-start(f32[128,128]{1,0:T(8,128)S(1)} %add_select_fusion.3), channel_id=1, source_target_pairs={{0,8},{4,12},{8,0},{12,4},{16,20},{20,16},{24,28},{28,24},{1,9},{5... | collective-permute-start | bytes 196616 | tf_op jit(solution)/shard_map/ppermute | solution.py:264
  11.3 0.3 collective-permute-done.2
  11.7 0.4 collective-permute-start.3
  12.1 2.4 %collective-permute-start.5 = (f32[128,128]{1,0:T(8,128)S(1)}, f32[128,128]{1,0:T(8,128)S(1)}, u32[]{:S(2)}, u32[]{:S(2)}) collective-permute-start(f32[128,128]{1,0:T(8,128)S(1)} %add_select_fusion.1), channel_id=1, source_target_pairs={{0,4},{4,0},{8,12},{12,8},{16,24},{20,28},{24,16},{28,20},{1,5},{5... | collective-permute-start | bytes 196616 | tf_op jit(solution)/shard_map/ppermute | solution.py:264
  14.6 0.3 collective-permute-start.7
  14.9 1.8 %shard_map.94 = (bf16[1,256,512]{2,1,0:T(8,128)(2,1)S(1)}, bf16[1,256,512]{2,1,0:T(8,128)(2,1)S(1)}, bf16[1,256,512]{2,1,0:T(8,128)(2,1)S(1)}, bf16[256,512]{1,0...) custom-call(bf16[1,256,512]{2,1,0:T(8,128)(2,1)} %queries.1, ...), custom_call_target="tpu_custom_call" | custom-call | flops 134217728 | bytes 2097152 | tf_op jit(solution)/shard_map/pallas_call | solution.py:40
  16.6 1.3 %collective-permute-done.1 = f32[128,128]{1,0:T(8,128)S(1)} collective-permute-done((f32[128,128]{1,0:T(8,128)S(1)}, f32[128,128]{1,0:T(8,128)S(1)}, u32[]{:S(2)}, u32[]{:S(2)}) %collective-permute-start.1) | collective-permute-done | bytes 65568 | tf_op jit(solution)/shard_map/ppermute | solution.py:264
  18.0 1.7 %collective-permute-done.3 = f32[128,128]{1,0:T(8,128)S(1)} collective-permute-done((f32[128,128]{1,0:T(8,128)S(1)}, f32[128,128]{1,0:T(8,128)S(1)}, u32[]{:S(2)}, u32[]{:S(2)}) %collective-permute-start.3) | collective-permute-done | bytes 65568 | tf_op jit(solution)/shard_map/ppermute | solution.py:264
  19.7 0.8 %collective-permute-done.7 = f32[128,128]{1,0:T(8,128)S(1)} collective-permute-done((f32[128,128]{1,0:T(8,128)S(1)}, f32[128,128]{1,0:T(8,128)S(1)}, u32[]{:S(2)}, u32[]{:S(2)}) %collective-permute-start.7) | collective-permute-done | bytes 65568 | tf_op jit(solution)/shard_map/ppermute | solution.py:264
  20.5 0.2 shard_map.95
  20.7 2.5 %collective-permute-start.10 = (f32[2,256]{1,0:T(2,128)S(1)}, f32[2,256]{1,0:T(2,128)S(1)}, u32[]{:S(2)}, u32[]{:S(2)}) collective-permute-start(f32[2,256]{1,0:T(2,128)S(1)} %get-tuple-element.66), channel_id=1, source_target_pairs={{0,3},{1,2},{2,1},{3,0},{4,7},{5,6},{6,5},{7,4},{8,11},{9,10},{10,... | collective-permute-start | bytes 6152 | tf_op jit(solution)/shard_map/ppermute | solution.py:239
  23.2 0.5 %collective-permute-start.9 = (f32[2,256]{1,0:T(2,128)S(1)}, f32[2,256]{1,0:T(2,128)S(1)}, u32[]{:S(2)}, u32[]{:S(2)}) collective-permute-start(f32[2,256]{1,0:T(2,128)S(1)} %get-tuple-element.66), channel_id=1, source_target_pairs={{0,2},{1,3},{2,0},{3,1},{4,6},{5,7},{6,4},{7,5},{8,10},{9,11},{10,... | collective-permute-start | bytes 6152 | tf_op jit(solution)/shard_map/ppermute | solution.py:239
  23.7 0.5 %collective-permute-start.8 = (f32[2,256]{1,0:T(2,128)S(1)}, f32[2,256]{1,0:T(2,128)S(1)}, u32[]{:S(2)}, u32[]{:S(2)}) collective-permute-start(f32[2,256]{1,0:T(2,128)S(1)} %get-tuple-element.66), channel_id=1, source_target_pairs={{0,1},{1,0},{2,3},{3,2},{4,5},{5,4},{6,7},{7,6},{8,9},{9,8},{10,11... | collective-permute-start | bytes 6152 | tf_op jit(solution)/shard_map/ppermute | solution.py:239
  24.2 1.0 %collective-permute-done.10 = f32[2,256]{1,0:T(2,128)S(1)} collective-permute-done((f32[2,256]{1,0:T(2,128)S(1)}, f32[2,256]{1,0:T(2,128)S(1)}, u32[]{:S(2)}, u32[]{:S(2)}) %collective-permute-start.10) | collective-permute-done | bytes 2080 | tf_op jit(solution)/shard_map/ppermute | solution.py:239
  25.2 1.5 %collective-permute-done.9 = f32[2,256]{1,0:T(2,128)S(1)} collective-permute-done((f32[2,256]{1,0:T(2,128)S(1)}, f32[2,256]{1,0:T(2,128)S(1)}, u32[]{:S(2)}, u32[]{:S(2)}) %collective-permute-start.9) | collective-permute-done | bytes 2080 | tf_op jit(solution)/shard_map/ppermute | solution.py:239
  26.8 0.5 %collective-permute-done.8 = f32[2,256]{1,0:T(2,128)S(1)} collective-permute-done((f32[2,256]{1,0:T(2,128)S(1)}, f32[2,256]{1,0:T(2,128)S(1)}, u32[]{:S(2)}, u32[]{:S(2)}) %collective-permute-start.8) | collective-permute-done | bytes 2080 | tf_op jit(solution)/shard_map/ppermute | solution.py:239
  27.3 0.2 shard_map.96
  27.5 0.1 collective-permute-start.11
  27.6 2.4 %collective-permute-start.14 = (f32[256,128]{1,0:T(8,128)S(1)}, f32[256,128]{1,0:T(8,128)S(1)}, u32[]{:S(2)}, u32[]{:S(2)}) collective-permute-start(f32[256,128]{1,0:T(8,128)S(1)} %get-tuple-element.82), channel_id=1, source_target_pairs={{0,8},{4,12},{8,0},{12,4},{16,24},{20,28},{24,16},{28,20},{1,9},{5... | collective-permute-start | bytes 393224 | tf_op jit(solution)/shard_map/ppermute | solution.py:264
  30.1 1.9 %shard_map.97 = (bf16[1,256,512]{2,1,0:T(8,128)(2,1)}, f32[256,256]{1,0:T(8,128)S(1)}, f32[256,256]{1,0:T(8,128)S(1)}, f32[256,256]{1,0:T(8,128)S(1)}, f32[256,256]{1,0:T(8,128)S(1)}) custom-call(bf16[1,256,512]{2,1,0:T(8,128)(2,1)S(1)} %get-tuple-element.50.queries, bf16[256,512]{1,0:T(8,128)(2,1)S(1)} %get-tuple-element.51.spiked, ...), custom_call_target="tpu_custom_call" | custom-call | flops 268435456 | bytes 4194304 | tf_op jit(solution)/shard_map/pallas_call | solution.py:40
  32.0 2.2 %collective-permute-done.11 = f32[264,128]{1,0:T(8,128)S(1)} collective-permute-done((f32[264,128]{1,0:T(8,128)S(1)}, f32[264,128]{1,0:T(8,128)S(1)}, u32[]{:S(2)}, u32[]{:S(2)}) %collective-permute-start.11) | collective-permute-done | bytes 135200 | tf_op jit(solution)/shard_map/ppermute | solution.py:264
  34.3 0.1 collective-permute-start.12
  34.4 2.1 %collective-permute-done.14 = f32[256,128]{1,0:T(8,128)S(1)} collective-permute-done((f32[256,128]{1,0:T(8,128)S(1)}, f32[256,128]{1,0:T(8,128)S(1)}, u32[]{:S(2)}, u32[]{:S(2)}) %collective-permute-start.14) | collective-permute-done | bytes 131104 | tf_op jit(solution)/shard_map/ppermute | solution.py:264
  36.5 0.3 collective-permute-start.15
  36.8 4.1 %collective-permute-done.12 = f32[264,128]{1,0:T(8,128)S(1)} collective-permute-done((f32[264,128]{1,0:T(8,128)S(1)}, f32[264,128]{1,0:T(8,128)S(1)}, u32[]{:S(2)}, u32[]{:S(2)}) %collective-permute-start.12) | collective-permute-done | bytes 135200 | tf_op jit(solution)/shard_map/ppermute | solution.py:264
  40.9 0.2 shard_map.99
  41.2 1.1 %collective-permute-done.15 = f32[256,128]{1,0:T(8,128)S(1)} collective-permute-done((f32[256,128]{1,0:T(8,128)S(1)}, f32[256,128]{1,0:T(8,128)S(1)}, u32[]{:S(2)}, u32[]{:S(2)}) %collective-permute-start.15) | collective-permute-done | bytes 131104 | tf_op jit(solution)/shard_map/ppermute | solution.py:264
  42.3 1.0 %shard_map.100 = (bf16[1,256,512]{2,1,0:T(8,128)(2,1)}, bf16[1,256,512]{2,1,0:T(8,128)(2,1)}, f32[1,512]{1,0:T(1,128)}) custom-call(bf16[1,256,512]{2,1,0:T(8,128)(2,1)S(1)} %get-tuple-element.52.values, bf16[256,512]{1,0:T(8,128)(2,1)S(1)} %get-tuple-element.51.spiked, s32[1,256,512]{2,1,0:T(8,128)S(1)} %copy-done, ...), custom_call_target="tpu_custom_call" | custom-call | flops 33554432 | bytes 2097152 | tf_op jit(solution)/shard_map/pallas_call | solution.py:40
  (26 shorter events, 0.2 us)
Async XLA Ops:
  2.2 6.2 %collective-permute-start = (f32[128,128]{1,0:T(8,128)S(1)}, f32[128,128]{1,0:T(8,128)S(1)}, u32[]{:S(2)}, u32[]{:S(2)}) collective-permute-start(f32[128,128]{1,0:T(8,128)S(1)} %get-tuple-element.48), channel_id=1, source_target_pairs={{0,4},{4,0},{8,12},{12,8},{16,24},{20,28},{24,16},{28,20},{1,5},{5... | collective-permute-start | bytes 196616 | tf_op jit(solution)/shard_map/ppermute | solution.py:264
  5.3 6.4 %collective-permute-start.2 = (f32[128,128]{1,0:T(8,128)S(1)}, f32[128,128]{1,0:T(8,128)S(1)}, u32[]{:S(2)}, u32[]{:S(2)}) collective-permute-start(f32[128,128]{1,0:T(8,128)S(1)} %get-tuple-element.55), channel_id=1, source_target_pairs={{0,4},{4,0},{8,12},{12,8},{16,24},{20,28},{24,16},{28,20},{1,5},{5... | collective-permute-start | bytes 196616 | tf_op jit(solution)/shard_map/ppermute | solution.py:264
  5.3 6.7 %collective-permute-start.4 = (f32[128,128]{1,0:T(8,128)S(1)}, f32[128,128]{1,0:T(8,128)S(1)}, u32[]{:S(2)}, u32[]{:S(2)}) collective-permute-start(f32[128,128]{1,0:T(8,128)S(1)} %get-tuple-element.58), channel_id=1, source_target_pairs={{0,8},{4,12},{8,0},{12,4},{16,20},{20,16},{24,28},{28,24},{1,9},{5... | collective-permute-start | bytes 196616 | tf_op jit(solution)/shard_map/ppermute | solution.py:264
  8.3 6.2 %collective-permute-start.6 = (f32[128,128]{1,0:T(8,128)S(1)}, f32[128,128]{1,0:T(8,128)S(1)}, u32[]{:S(2)}, u32[]{:S(2)}) collective-permute-start(f32[128,128]{1,0:T(8,128)S(1)} %get-tuple-element.61), channel_id=1, source_target_pairs={{0,8},{4,12},{8,0},{12,4},{16,20},{20,16},{24,28},{28,24},{1,9},{5... | collective-permute-start | bytes 196616 | tf_op jit(solution)/shard_map/ppermute | solution.py:264
  8.4 9.6 %collective-permute-start.1 = (f32[128,128]{1,0:T(8,128)S(1)}, f32[128,128]{1,0:T(8,128)S(1)}, u32[]{:S(2)}, u32[]{:S(2)}) collective-permute-start(f32[128,128]{1,0:T(8,128)S(1)} %add_select_fusion.3), channel_id=1, source_target_pairs={{0,8},{4,12},{8,0},{12,4},{16,20},{20,16},{24,28},{28,24},{1,9},{5... | collective-permute-start | bytes 196616 | tf_op jit(solution)/shard_map/ppermute | solution.py:264
  11.7 8.0 %collective-permute-start.3 = (f32[128,128]{1,0:T(8,128)S(1)}, f32[128,128]{1,0:T(8,128)S(1)}, u32[]{:S(2)}, u32[]{:S(2)}) collective-permute-start(f32[128,128]{1,0:T(8,128)S(1)} %add_select_fusion.2), channel_id=1, source_target_pairs={{0,8},{4,12},{8,0},{12,4},{16,20},{20,16},{24,28},{28,24},{1,9},{5... | collective-permute-start | bytes 196616 | tf_op jit(solution)/shard_map/ppermute | solution.py:264
  12.1 7.5 %collective-permute-start.5 = (f32[128,128]{1,0:T(8,128)S(1)}, f32[128,128]{1,0:T(8,128)S(1)}, u32[]{:S(2)}, u32[]{:S(2)}) collective-permute-start(f32[128,128]{1,0:T(8,128)S(1)} %add_select_fusion.1), channel_id=1, source_target_pairs={{0,4},{4,0},{8,12},{12,8},{16,24},{20,28},{24,16},{28,20},{1,5},{5... | collective-permute-start | bytes 196616 | tf_op jit(solution)/shard_map/ppermute | solution.py:264
  14.6 5.9 %collective-permute-start.7 = (f32[128,128]{1,0:T(8,128)S(1)}, f32[128,128]{1,0:T(8,128)S(1)}, u32[]{:S(2)}, u32[]{:S(2)}) collective-permute-start(f32[128,128]{1,0:T(8,128)S(1)} %add_select_fusion), channel_id=1, source_target_pairs={{0,4},{4,0},{8,12},{12,8},{16,24},{20,28},{24,16},{28,20},{1,5},{5... | collective-permute-start | bytes 196616 | tf_op jit(solution)/shard_map/ppermute | solution.py:264
  20.7 4.5 %collective-permute-start.10 = (f32[2,256]{1,0:T(2,128)S(1)}, f32[2,256]{1,0:T(2,128)S(1)}, u32[]{:S(2)}, u32[]{:S(2)}) collective-permute-start(f32[2,256]{1,0:T(2,128)S(1)} %get-tuple-element.66), channel_id=1, source_target_pairs={{0,3},{1,2},{2,1},{3,0},{4,7},{5,6},{6,5},{7,4},{8,11},{9,10},{10,... | collective-permute-start | bytes 6152 | tf_op jit(solution)/shard_map/ppermute | solution.py:239
  23.2 3.6 %collective-permute-start.9 = (f32[2,256]{1,0:T(2,128)S(1)}, f32[2,256]{1,0:T(2,128)S(1)}, u32[]{:S(2)}, u32[]{:S(2)}) collective-permute-start(f32[2,256]{1,0:T(2,128)S(1)} %get-tuple-element.66), channel_id=1, source_target_pairs={{0,2},{1,3},{2,0},{3,1},{4,6},{5,7},{6,4},{7,5},{8,10},{9,11},{10,... | collective-permute-start | bytes 6152 | tf_op jit(solution)/shard_map/ppermute | solution.py:239
  23.7 3.6 %collective-permute-start.8 = (f32[2,256]{1,0:T(2,128)S(1)}, f32[2,256]{1,0:T(2,128)S(1)}, u32[]{:S(2)}, u32[]{:S(2)}) collective-permute-start(f32[2,256]{1,0:T(2,128)S(1)} %get-tuple-element.66), channel_id=1, source_target_pairs={{0,1},{1,0},{2,3},{3,2},{4,5},{5,4},{6,7},{7,6},{8,9},{9,8},{10,11... | collective-permute-start | bytes 6152 | tf_op jit(solution)/shard_map/ppermute | solution.py:239
  27.5 6.7 %collective-permute-start.11 = (f32[264,128]{1,0:T(8,128)S(1)}, f32[264,128]{1,0:T(8,128)S(1)}, u32[]{:S(2)}, u32[]{:S(2)}) collective-permute-start(f32[264,128]{1,0:T(8,128)S(1)} %get-tuple-element.77), channel_id=1, source_target_pairs={{0,4},{4,0},{8,12},{12,8},{16,20},{20,16},{24,28},{28,24},{1,5},{5... | collective-permute-start | bytes 405512 | tf_op jit(solution)/shard_map/ppermute | solution.py:264
  27.6 8.9 %collective-permute-start.14 = (f32[256,128]{1,0:T(8,128)S(1)}, f32[256,128]{1,0:T(8,128)S(1)}, u32[]{:S(2)}, u32[]{:S(2)}) collective-permute-start(f32[256,128]{1,0:T(8,128)S(1)} %get-tuple-element.82), channel_id=1, source_target_pairs={{0,8},{4,12},{8,0},{12,4},{16,24},{20,28},{24,16},{28,20},{1,9},{5... | collective-permute-start | bytes 393224 | tf_op jit(solution)/shard_map/ppermute | solution.py:264
  34.3 6.7 %copy-start = (s32[1,256,512]{2,1,0:T(8,128)S(1)}, s32[1,256,512]{2,1,0:T(8,128)}, u32[]{:S(2)}) copy-start(s32[1,256,512]{2,1,0:T(8,128)} %spikes.7) | copy-start | bytes 1572868
  34.3 6.6 %collective-permute-start.12 = (f32[264,128]{1,0:T(8,128)S(1)}, f32[264,128]{1,0:T(8,128)S(1)}, u32[]{:S(2)}, u32[]{:S(2)}) collective-permute-start(f32[264,128]{1,0:T(8,128)S(1)} %add.82.total), channel_id=1, source_target_pairs={{0,8},{4,12},{8,0},{12,4},{16,24},{20,28},{24,16},{28,20},{1,9},{5... | collective-permute-start | bytes 405512 | tf_op jit(solution)/shard_map/ppermute | solution.py:264
  36.5 5.7 %collective-permute-start.15 = (f32[256,128]{1,0:T(8,128)S(1)}, f32[256,128]{1,0:T(8,128)S(1)}, u32[]{:S(2)}, u32[]{:S(2)}) collective-permute-start(f32[256,128]{1,0:T(8,128)S(1)} %select_add_fusion.1), channel_id=1, source_target_pairs={{0,4},{4,0},{8,12},{12,8},{16,20},{20,16},{24,28},{28,24},{1,5},{5... | collective-permute-start | bytes 393224 | tf_op jit(solution)/shard_map/ppermute | solution.py:264
  40.9 1.3 %collective-permute-start.13 = (f32[8,128]{1,0:T(8,128)S(1)}, f32[8,128]{1,0:T(8,128)S(1)}, u32[]{:S(2)}, u32[]{:S(2)}) collective-permute-start(f32[8,128]{1,0:T(8,128)S(1)} %slice_add_fusion.gain_here), channel_id=1, source_target_pairs={{0,16},{16,0},{1,17},{17,1},{2,18},{18,2},{3,19},{19,3},{4,20},{20... | collective-permute-start | bytes 12296 | tf_op jit(solution)/shard_map/ppermute | solution.py:239
